TPU v7x, 32 devices: a whole 2x2x4 slice. The times are simulated.
32 devices in a mesh: ens: 2 (over x), lon: 16 (over z, y, core).
Axes of the slice: x: 2, y: 2, z: 4, core: 2. Of those that a mesh axis runs over, the one named last changes fastest.
Arguments:
- tracer: float32 [32, 128, 512], P('ens', 'lon'), parts along dimension 0, may hold values from -6 to 6
- zonal_flow: float32 [32, 128, 512], P('ens', 'lon'), parts along dimension 0, may hold values from -10.8 to 10.8
- meridional_flow: float32 [32, 128, 512], P('ens', 'lon'), parts along dimension 0, may hold values from -10.8 to 10.8
- level_count: int32 [128, 512], P('lon'), may hold values from 0 to 16
- diffusivity: float32 [128, 512], P('lon'), may hold values from 0.02 to 0.2
- surface: float32 [128, 512], P('lon'), may hold values from 0.05 to 0.5
Outputs:
- tracer_next: float32 [32, 128, 512], P('ens', 'lon'), parts along dimension 0
- zonal_next: float32 [32, 128, 512], P('ens', 'lon'), parts along dimension 0
- meridional_next: float32 [32, 128, 512], P('ens', 'lon'), parts along dimension 0
- surface_height: float32 [128, 1024], P('lon', 'ens'), parts along dimension 1
There are 2 independent parts, one for each index of `ens`. A program takes and returns all parts, laid end to end along the dimension named above; an argument that names none is the same for every part. Nothing has to cross between parts.
All inputs are finite; a program needn't handle non-finite values.
Results may differ from a plain program's by a relative error of at most 0.0001.
Values sent between devices are 32-bit elements; how exact they have to be, the bound alone decides.
No kernel may reach another device: no remote copies, remote signals or barrier semaphores. Data moves between devices by JAX's collectives and lax.ppermute only.
A program may use at most 64 MiB of HBM per device.

v0:
```python
import jax
import jax.numpy as jnp
from jax import lax
from jax.sharding import PartitionSpec as P

K = 16
NY = 512
ITERS = 6


vertical_mix = 0.1
advection = 0.25
coriolis_scale = 0.3
gravity = 0.5
corner_weight = 0.25
center_base = 5.0


def extended_2(value, sides, width):
    for axis, dim in sides:
        size, length = (lax.axis_size(axis), value.shape[dim])
        up = [(i, (i + 1) % size) for i in range(size)]
        down = [(j, i) for i, j in up]
        last = lax.slice_in_dim(value, length - width, length, axis=dim)
        initial = lax.slice_in_dim(value, 0, width, axis=dim)
        before = lax.ppermute(last, axis, up)
        after = lax.ppermute(initial, axis, down)
        value = jnp.concatenate([before, value, after], axis=dim)
    return value


def extend(fields, sign_flip):
    padded = extended_2(fields, (("lon", 2),), 1)
    block_cols = fields.shape[2]
    all_rows = lax.all_gather(fields[:, :, :, NY - 1], "lon", axis=2, tiled=True)
    reversed_rows = jnp.flip(all_rows, 2)
    extended = jnp.concatenate(
        [reversed_rows[:, :, -1:], reversed_rows, reversed_rows[:, :, :1]], axis=2
    )
    ghost_row = lax.dynamic_slice_in_dim(
        extended, lax.axis_index("lon") * block_cols, block_cols + 2, 2
    )
    ghost_row = ghost_row * sign_flip[:, None, None]
    south_row = jnp.zeros_like(ghost_row)
    return jnp.concatenate([south_row[..., None], padded, ghost_row[..., None]], axis=3)


def nine_point(padded, ocean_mask, surface):
    center_cells = padded[1:-1, 1:-1]
    edge_sum = padded[2:, 1:-1] + padded[:-2, 1:-1] + padded[1:-1, 2:] + padded[1:-1, :-2]
    corner_sum = padded[2:, 2:] + padded[2:, :-2] + padded[:-2, 2:] + padded[:-2, :-2]
    return ocean_mask * (
        (center_base + surface) * center_cells - edge_sum - corner_weight * corner_sum
    )


def baroclinic(padded, tracer, zonal_flow, meridional_flow, level_mask, diffusivity):
    center_cells = padded[:, :, 1:-1, 1:-1]
    east_side = padded[:, :, 2:, 1:-1]
    west_side = padded[:, :, :-2, 1:-1]
    north_side = padded[:, :, 1:-1, 2:]
    south_side = padded[:, :, 1:-1, :-2]
    edge_sum = east_side + west_side + north_side + south_side
    mask_sum = edge_sum[3]
    deeper = jnp.concatenate([center_cells[:, 1:], jnp.zeros_like(center_cells[:, :1])], axis=1)
    shallower = jnp.concatenate([jnp.zeros_like(center_cells[:, :1]), center_cells[:, :-1]], axis=1)
    vertical_term = deeper[0] + shallower[0] - (deeper[3] + shallower[3]) * tracer
    carried = zonal_flow * (east_side[0] - west_side[0]) + meridional_flow * (
        north_side[0] - south_side[0]
    )
    tracer_next = level_mask * (
        tracer
        + diffusivity * (edge_sum[0] - mask_sum * tracer)
        + vertical_mix * vertical_term
        - advection * carried
    )
    latitude = (jnp.arange(NY, dtype=jnp.float32) + 0.5) / NY
    planetary = coriolis_scale * (2.0 * latitude - 1.0)
    zonal_step = level_mask * (
        zonal_flow
        + diffusivity * (edge_sum[1] - mask_sum * zonal_flow)
        + planetary * meridional_flow
    )
    meridional_step = level_mask * (
        meridional_flow
        + diffusivity * (edge_sum[2] - mask_sum * meridional_flow)
        - planetary * zonal_flow
    )
    return (tracer_next, zonal_step, meridional_step)


def column_sum(zonal_step, meridional_step):
    thickness = 0.5 * (0.5 + jnp.arange(K, dtype=jnp.float32) / K)
    return jnp.sum(thickness[:, None, None] * (zonal_step + meridional_step), axis=0)


def operate(direction, ocean_mask, surface):
    padded = extend(direction[None, None], jnp.ones((1,), jnp.float32))[0, 0]
    return (padded, nine_point(padded, ocean_mask, surface))


def global_norm(residual):
    return lax.psum(jnp.sum(residual * residual), "lon")


def body(tracer, zonal_flow, meridional_flow, level_count, diffusivity, surface):
    levels = jnp.arange(K, dtype=jnp.int32)[:, None, None]
    level_mask = (levels < level_count[None]).astype(jnp.float32)
    stacked = jnp.stack(
        [level_mask * tracer, level_mask * zonal_flow, level_mask * meridional_flow, level_mask]
    )
    padded = extend(stacked, jnp.array([1.0, -1.0, -1.0, 1.0], jnp.float32))
    tracer_next, zonal_step, meridional_step = baroclinic(
        padded, tracer, zonal_flow, meridional_flow, level_mask, diffusivity
    )
    forcing = column_sum(zonal_step, meridional_step)
    ocean_mask = level_mask[0]
    solution = jnp.zeros_like(forcing)
    residual = forcing
    direction = forcing
    norm_now = global_norm(residual)
    for iteration in range(ITERS):
        direction_padded, applied = operate(direction, ocean_mask, surface)
        curvature = lax.psum(jnp.sum(direction * applied), "lon")
        step_size = norm_now / curvature
        solution = solution + step_size * direction
        residual = residual - step_size * applied
        if iteration + 1 < ITERS:
            norm_next = global_norm(residual)
            direction = residual + norm_next / norm_now * direction
            norm_now = norm_next
    height_padded = extend(solution[None, None], jnp.ones((1,), jnp.float32))[0, 0]
    east_height = height_padded[2:, 1:-1]
    north_height = height_padded[1:-1, 2:]
    zonal_next = level_mask * (zonal_step - gravity * (east_height - solution)[None])
    meridional_next = level_mask * (meridional_step - gravity * (north_height - solution)[None])
    return (tracer_next, zonal_next, meridional_next, solution)


def solution(mesh):
    return jax.shard_map(
        body,
        mesh=mesh,
        in_specs=(
            P("ens", "lon", None),
            P("ens", "lon", None),
            P("ens", "lon", None),
            P("lon", None),
            P("lon", None),
            P("lon", None),
        ),
        out_specs=(
            P("ens", "lon", None),
            P("ens", "lon", None),
            P("ens", "lon", None),
            P("lon", "ens"),
        ),
        check_vma=False,
    )
```

profile of v0, /device:TPU:0, one launch (start us, length us, event | category | flops | bytes accessed | tf_op | source)
XLA Modules:
  0.0 667.0 jit_solution(1174608502218354405)
XLA Ops:
  1.4 1.2 select_bitcast_fusion.2
  2.8 5.5 collective-permute-start
  8.8 18.8 %all-gather = f32[4,16,128,1]{1,0,3,2:T(4,128)S(1)} all-gather(f32[4,16,8,1]{1,0,3,2:T(4,128)S(1)} %copy.329), channel_id=2, replica_groups=mesh['ens'=2,'lon'=16] {'lon'}, dimensions={2}, use_global_device_ids=true | all-gather | bytes 34816 | tf_op jit(solution)/shard_map/all_gather | solution.py:35
  28.7 1.3 copy.310
  32.1 1.7 select_maximum_fusion
  37.6 30.6 %all-reduce.3 = f32[128]{0:T(128)S(1)} all-reduce(f32[128]{0:T(128)S(1)} %dynamic-update-slice), channel_id=3, replica_groups=mesh['ens'=2,'lon'=16] {'lon'}, use_global_device_ids=true, to_apply=%add.3 | all-reduce | flops 128 | bytes 1024
  68.9 4.4 collective-permute-start.3
  73.3 1.7 multiply_reduce_fusion
  75.0 1.3 fusion.72
  76.6 1.4 multiply_reduce_fusion.11
  78.0 32.7 %all-reduce.10 = (f32[]{:T(128)}, f32[]{:T(128)}) all-reduce(f32[]{:T(128)} %multiply_reduce_fusion, f32[]{:T(128)} %get-tuple-element.44), channel_id=1, replica_groups=mesh['ens'=2,'lon'=16] {'lon'}, use_global_device_ids=true, to_apply=%region_2.3 | all-reduce | flops 2 | bytes 16 | tf_op jit(solution)/shard_map/psum | solution.py:103
  112.6 30.1 %psum.86 = f32[]{:T(128)} all-reduce(f32[]{:T(128)} %multiply_reduce_fusion.10), channel_id=1, replica_groups=mesh['ens'=2,'lon'=16] {'lon'}, use_global_device_ids=true, to_apply=%region_6.7 | all-reduce | flops 1 | bytes 8 | tf_op jit(solution)/shard_map/psum | solution.py:103
  144.3 4.4 collective-permute-start.5
  148.9 29.5 %all-reduce.4 = f32[128]{0:T(128)S(1)} all-reduce(f32[128]{0:T(128)S(1)} %dynamic-update-slice.1), channel_id=4, replica_groups=mesh['ens'=2,'lon'=16] {'lon'}, use_global_device_ids=true, to_apply=%add.4 | all-reduce | flops 128 | bytes 1024
  179.1 1.3 fusion.74
  180.6 1.4 multiply_reduce_fusion.9
  182.0 30.1 %psum.87 = f32[]{:T(128)} all-reduce(f32[]{:T(128)} %get-tuple-element.42), channel_id=1, replica_groups=mesh['ens'=2,'lon'=16] {'lon'}, use_global_device_ids=true, to_apply=%region_8.9 | all-reduce | flops 1 | bytes 8 | tf_op jit(solution)/shard_map/psum | solution.py:124
  214.0 30.1 %psum.88 = f32[]{:T(128)} all-reduce(f32[]{:T(128)} %get-tuple-element.40), channel_id=1, replica_groups=mesh['ens'=2,'lon'=16] {'lon'}, use_global_device_ids=true, to_apply=%region_10.11 | all-reduce | flops 1 | bytes 8 | tf_op jit(solution)/shard_map/psum | solution.py:103
  245.7 4.4 collective-permute-start.7
  250.4 29.5 %all-reduce.5 = f32[128]{0:T(128)S(1)} all-reduce(f32[128]{0:T(128)S(1)} %dynamic-update-slice.2), channel_id=5, replica_groups=mesh['ens'=2,'lon'=16] {'lon'}, use_global_device_ids=true, to_apply=%add.5 | all-reduce | flops 128 | bytes 1024
  280.5 1.3 fusion.76
  282.1 1.4 multiply_reduce_fusion.7
  283.4 30.1 %psum.89 = f32[]{:T(128)} all-reduce(f32[]{:T(128)} %get-tuple-element.38), channel_id=1, replica_groups=mesh['ens'=2,'lon'=16] {'lon'}, use_global_device_ids=true, to_apply=%region_12.13 | all-reduce | flops 1 | bytes 8 | tf_op jit(solution)/shard_map/psum | solution.py:124
  315.5 30.1 %psum.90 = f32[]{:T(128)} all-reduce(f32[]{:T(128)} %get-tuple-element.36), channel_id=1, replica_groups=mesh['ens'=2,'lon'=16] {'lon'}, use_global_device_ids=true, to_apply=%region_14.15 | all-reduce | flops 1 | bytes 8 | tf_op jit(solution)/shard_map/psum | solution.py:103
  347.2 4.4 collective-permute-start.9
  351.8 29.5 %all-reduce.6 = f32[128]{0:T(128)S(1)} all-reduce(f32[128]{0:T(128)S(1)} %dynamic-update-slice.3), channel_id=6, replica_groups=mesh['ens'=2,'lon'=16] {'lon'}, use_global_device_ids=true, to_apply=%add.6 | all-reduce | flops 128 | bytes 1024
  382.0 1.4 fusion.78
  383.5 2.0 multiply_reduce_fusion.5
  385.5 30.1 %psum.91 = f32[]{:T(128)} all-reduce(f32[]{:T(128)} %get-tuple-element.34), channel_id=1, replica_groups=mesh['ens'=2,'lon'=16] {'lon'}, use_global_device_ids=true, to_apply=%region_16.17 | all-reduce | flops 1 | bytes 8 | tf_op jit(solution)/shard_map/psum | solution.py:124
  416.9 1.3 multiply_reduce_fusion.4
  418.2 30.2 %psum.92 = f32[]{:T(128)} all-reduce(f32[]{:T(128)} %get-tuple-element.32), channel_id=1, replica_groups=mesh['ens'=2,'lon'=16] {'lon'}, use_global_device_ids=true, to_apply=%region_18.19 | all-reduce | flops 1 | bytes 8 | tf_op jit(solution)/shard_map/psum | solution.py:103
  450.6 4.4 collective-permute-start.11
  455.2 29.5 %all-reduce.7 = f32[128]{0:T(128)S(1)} all-reduce(f32[128]{0:T(128)S(1)} %dynamic-update-slice.4), channel_id=7, replica_groups=mesh['ens'=2,'lon'=16] {'lon'}, use_global_device_ids=true, to_apply=%add.7 | all-reduce | flops 128 | bytes 1024
  485.3 1.8 fusion.80
  488.7 2.0 multiply_reduce_fusion.3
  490.7 30.1 %psum.93 = f32[]{:T(128)} all-reduce(f32[]{:T(128)} %get-tuple-element.30), channel_id=1, replica_groups=mesh['ens'=2,'lon'=16] {'lon'}, use_global_device_ids=true, to_apply=%region_20.21 | all-reduce | flops 1 | bytes 8 | tf_op jit(solution)/shard_map/psum | solution.py:124
  522.1 1.3 multiply_reduce_fusion.2
  523.4 1.5 fusion.97
  524.9 30.2 %psum.94 = f32[]{:T(128)} all-reduce(f32[]{:T(128)} %multiply_reduce_fusion.2), channel_id=1, replica_groups=mesh['ens'=2,'lon'=16] {'lon'}, use_global_device_ids=true, to_apply=%region_22.23 | all-reduce | flops 1 | bytes 8 | tf_op jit(solution)/shard_map/psum | solution.py:103
  557.4 4.4 collective-permute-start.13
  562.0 29.5 %all-reduce.8 = f32[128]{0:T(128)S(1)} all-reduce(f32[128]{0:T(128)S(1)} %dynamic-update-slice.5), channel_id=8, replica_groups=mesh['ens'=2,'lon'=16] {'lon'}, use_global_device_ids=true, to_apply=%add.8 | all-reduce | flops 128 | bytes 1024
  592.2 1.4 fusion.82
  593.7 1.4 fusion.47
  595.1 2.9 fusion.13
  598.0 30.1 %psum.95 = f32[]{:T(128)} all-reduce(f32[]{:T(128)} %fusion.47), channel_id=1, replica_groups=mesh['ens'=2,'lon'=16] {'lon'}, use_global_device_ids=true, to_apply=%region_24.25 | all-reduce | flops 1 | bytes 8 | tf_op jit(solution)/shard_map/psum | solution.py:124
  629.7 4.4 collective-permute-start.15
  634.4 29.5 %all-reduce.9 = f32[128]{0:T(128)S(1)} all-reduce(f32[128]{0:T(128)S(1)} %dynamic-update-slice.6), channel_id=9, replica_groups=mesh['ens'=2,'lon'=16] {'lon'}, use_global_device_ids=true, to_apply=%add.9 | all-reduce | flops 128 | bytes 1024
  664.5 1.3 fusion.89
  (136 shorter events, 21.6 us)
Async XLA Ops:
  1.4 26.5 %copy-start.6 = (s32[8,512]{1,0:T(8,128)S(1)}, s32[8,512]{1,0:T(8,128)}, u32[]{:S(2)}) copy-start(s32[8,512]{1,0:T(8,128)} %param.10) | copy-start | bytes 49156
  1.4 27.2 %copy-start.10 = (f32[4]{0:T(128)S(1)}, f32[4]{0:T(128)}, u32[]{:S(2)}) copy-start(f32[4]{0:T(128)} %constant.55.clone) | copy-start | bytes 52
  2.6 27.4 %copy-start.11 = (u32[32]{0:T(128)S(1)}, u32[32]{0:T(128)}, u32[]{:S(2)}) copy-start(u32[32]{0:T(128)} %constant.70) | copy-start | bytes 388
  2.8 28.5 %collective-permute-start = (f32[4,16,1,512]{3,1,2,0:T(8,128)S(1)}, f32[4,16,1,512]{3,1,2,0:T(8,128)S(1)}, u32[]{:S(2)}, u32[]{:S(2)}) collective-permute-start(f32[4,16,1,512]{3,1,2,0:T(8,128)S(1)} %copy.327), channel_id=1, source_target_pairs={{1,0},{2,1},{3,2},{4,3},{5,4},{6,5},{7,6},{8,7},{9,8},{10,9},{11,1... | collective-permute-start | bytes 393224 | tf_op jit(solution)/shard_map/ppermute | solution.py:27
  8.3 23.1 %collective-permute-start.1 = (f32[4,16,1,512]{3,1,2,0:T(8,128)S(1)}, f32[4,16,1,512]{3,1,2,0:T(8,128)S(1)}, u32[]{:S(2)}, u32[]{:S(2)}) collective-permute-start(f32[4,16,1,512]{3,1,2,0:T(8,128)S(1)} %copy.328), channel_id=1, source_target_pairs={{0,1},{1,2},{2,3},{3,4},{4,5},{5,6},{6,7},{7,8},{8,9},{9,10},{10,1... | collective-permute-start | bytes 393224 | tf_op jit(solution)/shard_map/ppermute | solution.py:26
  32.1 1.7 copy-start.1
  33.9 1.5 copy-start
  33.9 1.5 copy-start.2
  33.9 1.5 copy-start.3
  33.9 1.5 copy-start.9
  33.9 42.6 %copy-start.7 = (f32[8,512]{1,0:T(8,128)S(1)}, f32[8,512]{1,0:T(8,128)}, u32[]{:S(2)}) copy-start(f32[8,512]{1,0:T(8,128)} %param.12) | copy-start | bytes 49156
  68.9 7.6 %collective-permute-start.2 = (f32[1,1,1,512]{3,2,1,0:T(1,128)S(1)}, f32[1,1,1,512]{3,2,1,0:T(1,128)S(1)}, u32[]{:S(2)}, u32[]{:S(2)}) collective-permute-start(f32[1,1,1,512]{3,2,1,0:T(1,128)S(1)} %get-tuple-element.75), channel_id=1, source_target_pairs={{0,1},{1,2},{2,3},{3,4},{4,5},{5,6},{6,7},{7,8},{8,9},{9,10},{10,1... | collective-permute-start | bytes 6152 | tf_op jit(solution)/shard_map/ppermute | solution.py:26
  68.9 7.6 %collective-permute-start.3 = (f32[1,1,1,512]{3,2,1,0:T(1,128)S(1)}, f32[1,1,1,512]{3,2,1,0:T(1,128)S(1)}, u32[]{:S(2)}, u32[]{:S(2)}) collective-permute-start(f32[1,1,1,512]{3,2,1,0:T(1,128)S(1)} %get-tuple-element.76), channel_id=1, source_target_pairs={{1,0},{2,1},{3,2},{4,3},{5,4},{6,5},{7,6},{8,7},{9,8},{10,9},{11,1... | collective-permute-start | bytes 6152 | tf_op jit(solution)/shard_map/ppermute | solution.py:27
  144.2 36.3 %collective-permute-start.4 = (f32[1,1,1,512]{3,2,1,0:T(1,128)S(1)}, f32[1,1,1,512]{3,2,1,0:T(1,128)S(1)}, u32[]{:S(2)}, u32[]{:S(2)}) collective-permute-start(f32[1,1,1,512]{3,2,1,0:T(1,128)S(1)} %get-tuple-element.73), channel_id=1, source_target_pairs={{0,1},{1,2},{2,3},{3,4},{4,5},{5,6},{6,7},{7,8},{8,9},{9,10},{10,1... | collective-permute-start | bytes 6152 | tf_op jit(solution)/shard_map/ppermute | solution.py:26
  144.3 36.2 %collective-permute-start.5 = (f32[1,1,1,512]{3,2,1,0:T(1,128)S(1)}, f32[1,1,1,512]{3,2,1,0:T(1,128)S(1)}, u32[]{:S(2)}, u32[]{:S(2)}) collective-permute-start(f32[1,1,1,512]{3,2,1,0:T(1,128)S(1)} %get-tuple-element.74), channel_id=1, source_target_pairs={{1,0},{2,1},{3,2},{4,3},{5,4},{6,5},{7,6},{8,7},{9,8},{10,9},{11,1... | collective-permute-start | bytes 6152 | tf_op jit(solution)/shard_map/ppermute | solution.py:27
  245.7 36.3 %collective-permute-start.6 = (f32[1,1,1,512]{3,2,1,0:T(1,128)S(1)}, f32[1,1,1,512]{3,2,1,0:T(1,128)S(1)}, u32[]{:S(2)}, u32[]{:S(2)}) collective-permute-start(f32[1,1,1,512]{3,2,1,0:T(1,128)S(1)} %get-tuple-element.71), channel_id=1, source_target_pairs={{0,1},{1,2},{2,3},{3,4},{4,5},{5,6},{6,7},{7,8},{8,9},{9,10},{10,1... | collective-permute-start | bytes 6152 | tf_op jit(solution)/shard_map/ppermute | solution.py:26
  245.7 36.2 %collective-permute-start.7 = (f32[1,1,1,512]{3,2,1,0:T(1,128)S(1)}, f32[1,1,1,512]{3,2,1,0:T(1,128)S(1)}, u32[]{:S(2)}, u32[]{:S(2)}) collective-permute-start(f32[1,1,1,512]{3,2,1,0:T(1,128)S(1)} %get-tuple-element.72), channel_id=1, source_target_pairs={{1,0},{2,1},{3,2},{4,3},{5,4},{6,5},{7,6},{8,7},{9,8},{10,9},{11,1... | collective-permute-start | bytes 6152 | tf_op jit(solution)/shard_map/ppermute | solution.py:27
  347.1 36.3 %collective-permute-start.8 = (f32[1,1,1,512]{3,2,1,0:T(1,128)S(1)}, f32[1,1,1,512]{3,2,1,0:T(1,128)S(1)}, u32[]{:S(2)}, u32[]{:S(2)}) collective-permute-start(f32[1,1,1,512]{3,2,1,0:T(1,128)S(1)} %get-tuple-element.69), channel_id=1, source_target_pairs={{0,1},{1,2},{2,3},{3,4},{4,5},{5,6},{6,7},{7,8},{8,9},{9,10},{10,1... | collective-permute-start | bytes 6152 | tf_op jit(solution)/shard_map/ppermute | solution.py:26
  347.2 36.2 %collective-permute-start.9 = (f32[1,1,1,512]{3,2,1,0:T(1,128)S(1)}, f32[1,1,1,512]{3,2,1,0:T(1,128)S(1)}, u32[]{:S(2)}, u32[]{:S(2)}) collective-permute-start(f32[1,1,1,512]{3,2,1,0:T(1,128)S(1)} %get-tuple-element.70), channel_id=1, source_target_pairs={{1,0},{2,1},{3,2},{4,3},{5,4},{6,5},{7,6},{8,7},{9,8},{10,9},{11,1... | collective-permute-start | bytes 6152 | tf_op jit(solution)/shard_map/ppermute | solution.py:27
  450.5 37.4 %collective-permute-start.10 = (f32[1,1,1,512]{3,2,1,0:T(1,128)}, f32[1,1,1,512]{3,2,1,0:T(1,128)S(1)}, u32[]{:S(2)}, u32[]{:S(2)}) collective-permute-start(f32[1,1,1,512]{3,2,1,0:T(1,128)} %get-tuple-element.67), channel_id=1, source_target_pairs={{0,1},{1,2},{2,3},{3,4},{4,5},{5,6},{6,7},{7,8},{8,9},{9,10},{10,1... | collective-permute-start | bytes 6152 | tf_op jit(solution)/shard_map/ppermute | solution.py:26
  450.6 37.4 %collective-permute-start.11 = (f32[1,1,1,512]{3,2,1,0:T(1,128)}, f32[1,1,1,512]{3,2,1,0:T(1,128)}, u32[]{:S(2)}, u32[]{:S(2)}) collective-permute-start(f32[1,1,1,512]{3,2,1,0:T(1,128)} %get-tuple-element.68), channel_id=1, source_target_pairs={{1,0},{2,1},{3,2},{4,3},{5,4},{6,5},{7,6},{8,7},{9,8},{10,9},{11,1... | collective-permute-start | bytes 6152 | tf_op jit(solution)/shard_map/ppermute | solution.py:27
  557.3 36.3 %collective-permute-start.12 = (f32[1,1,1,512]{3,2,1,0:T(1,128)S(1)}, f32[1,1,1,512]{3,2,1,0:T(1,128)S(1)}, u32[]{:S(2)}, u32[]{:S(2)}) collective-permute-start(f32[1,1,1,512]{3,2,1,0:T(1,128)S(1)} %get-tuple-element.65), channel_id=1, source_target_pairs={{0,1},{1,2},{2,3},{3,4},{4,5},{5,6},{6,7},{7,8},{8,9},{9,10},{10,1... | collective-permute-start | bytes 6152 | tf_op jit(solution)/shard_map/ppermute | solution.py:26
  557.4 36.2 %collective-permute-start.13 = (f32[1,1,1,512]{3,2,1,0:T(1,128)S(1)}, f32[1,1,1,512]{3,2,1,0:T(1,128)S(1)}, u32[]{:S(2)}, u32[]{:S(2)}) collective-permute-start(f32[1,1,1,512]{3,2,1,0:T(1,128)S(1)} %get-tuple-element.66), channel_id=1, source_target_pairs={{1,0},{2,1},{3,2},{4,3},{5,4},{6,5},{7,6},{8,7},{9,8},{10,9},{11,1... | collective-permute-start | bytes 6152 | tf_op jit(solution)/shard_map/ppermute | solution.py:27
  595.1 71.0 %copy-start.4 = (f32[16,8,512]{2,1,0:T(8,128)S(1)}, f32[16,8,512]{2,1,0:T(8,128)}, u32[]{:S(2)}) copy-start(f32[16,8,512]{2,1,0:T(8,128)} %get-tuple-element.47) | copy-start | bytes 786436
  595.1 71.0 %copy-start.5 = (f32[16,8,512]{2,1,0:T(8,128)S(1)}, f32[16,8,512]{2,1,0:T(8,128)}, u32[]{:S(2)}) copy-start(f32[16,8,512]{2,1,0:T(8,128)} %get-tuple-element.48) | copy-start | bytes 786436
  629.5 37.5 %copy-start.8 = (f32[8,512]{1,0:T(8,128)}, f32[8,512]{1,0:T(8,128)S(1)}, u32[]{:S(2)}) copy-start(f32[8,512]{1,0:T(8,128)S(1)} %multiply_add_fusion) | copy-start | bytes 49156
  629.7 36.3 %collective-permute-start.14 = (f32[1,1,1,512]{3,2,1,0:T(1,128)S(1)}, f32[1,1,1,512]{3,2,1,0:T(1,128)S(1)}, u32[]{:S(2)}, u32[]{:S(2)}) collective-permute-start(f32[1,1,1,512]{3,2,1,0:T(1,128)S(1)} %get-tuple-element.63), channel_id=1, source_target_pairs={{0,1},{1,2},{2,3},{3,4},{4,5},{5,6},{6,7},{7,8},{8,9},{9,10},{10,1... | collective-permute-start | bytes 6152 | tf_op jit(solution)/shard_map/ppermute | solution.py:26
  629.7 36.2 %collective-permute-start.15 = (f32[1,1,1,512]{3,2,1,0:T(1,128)S(1)}, f32[1,1,1,512]{3,2,1,0:T(1,128)S(1)}, u32[]{:S(2)}, u32[]{:S(2)}) collective-permute-start(f32[1,1,1,512]{3,2,1,0:T(1,128)S(1)} %get-tuple-element.64), channel_id=1, source_target_pairs={{1,0},{2,1},{3,2},{4,3},{5,4},{6,5},{7,6},{8,7},{9,8},{10,9},{11,1... | collective-permute-start | bytes 6152 | tf_op jit(solution)/shard_map/ppermute | solution.py:27
where the time goes:
time: 668 us; the launch traced here: 667 us
  blocking collectives  560 us (84%)
  other arithmetic  38.6 us (6%)
  starting transfers between devices  36.9 us (6%)
  between operations  16.3 us (2%)
  local copies, waits for them, and re-layouts  15 us (2%)
    unnamed x7, blocking collectives  207 us
    psum x6, blocking collectives, global_norm(): return lax.psum(jnp.sum(residual * residual), 'lon')  183 us
    psum x5, blocking collectives, body(): curvature = lax.psum(jnp.sum(direction * applied), 'lon')  151 us
    ppermute x8, starting transfers between devices, extended_2(): after = lax.ppermute(initial, axis, down)  36.5 us
    all_gather x1, blocking collectives, extend(): lax.all_gather(fields[:, :, :, NY - 1], 'lon', axis=2, tiled=True)  18.8 us
  transfers between devices with their start and end apart: 16, of which 0 were waited for; matrix products, arithmetic and copies ran while one was open for 3% of the time, Pallas kernels for 0%

commit v1 on v0

v1 whole, which is shorter than its diff:
```python
import functools

import jax
import jax.numpy as jnp
from jax import lax
from jax.experimental import pallas as pl
from jax.experimental.pallas import tpu as pltpu
from jax.sharding import PartitionSpec as P

K = 16
NY = 512
ITERS = 6
COLS = 8
EXT = 3 * COLS
LANES = 128
PACK = 80
BASIS = ITERS + 1

vertical_mix = 0.1
advection = 0.25
coriolis_scale = 0.3
gravity = 0.5
corner_weight = 0.25
shift = 5.0
scale = 4.0
LANE_P = 16
LANE_LC = 32
LANE_DIFF = 33
LANE_MT = 40
LANE_MU = 56
LANE_MV = 72

f32 = jnp.float32


def iota(shape, dim):
    return lax.broadcasted_iota(jnp.int32, shape, dim)


def thickness(k):
    return 0.5 * (0.5 + k / K)


def planetary(shape):
    latitude = (iota(shape, 1).astype(f32) + 0.5) / NY
    return coriolis_scale * (2.0 * latitude - 1.0)


def roll(value, amount, axis):
    return pltpu.roll(value, amount % value.shape[axis], axis)


def level_sum(value):
    weight = 0.5 * (0.5 + iota(value.shape, 0).astype(f32) / K)
    return jnp.sum(weight * value, axis=0, keepdims=True)


def two_sum(a, b):
    s = a + b
    t = s - a
    return s, (a - (s - t)) + (b - t)


def fast_two_sum(a, b):
    s = a + b
    return s, b - (s - a)


def split(a):
    c = 4097.0 * a
    high = c - (c - a)
    return high, a - high


def two_prod(a, b, a_parts=None, b_parts=None):
    ah, al = split(a) if a_parts is None else a_parts
    bh, bl = split(b) if b_parts is None else b_parts
    p = a * b
    return p, ((ah * bh - p) + ah * bl + al * bh) + al * bl


def pair_mul(a, b):
    p, e = two_prod(a[0], b[0])
    return p, e + (a[0] * b[1] + a[1] * b[0])


def pair_add(a, b):
    s, e = two_sum(a[0], b[0])
    return s, e + (a[1] + b[1])


def pair_norm(a):
    return fast_two_sum(a[0], a[1])


def pair_scale(a, factor):
    p, e = two_prod(a[0], factor)
    return p, e + a[1] * factor


def pair_tree(terms):
    while len(terms) > 1:
        pairs = [pair_add(terms[i], terms[i + 1]) for i in range(0, len(terms) - 1, 2)]
        terms = pairs + terms[len(terms) - len(terms) % 2:]
    return terms[0]


def pair_rows(a):
    for step in (4, 2, 1):
        a = pair_add(a, (roll(a[0], step, 0), roll(a[1], step, 0)))
    return a


def pack_kernel(tracer, zonal, meridional, count, diffusivity, surface, inner, outer):
    shape = (COLS, NY)
    even = lax.axis_index("lon") % 2 == 0
    lc = count[...].astype(f32)
    diff = diffusivity[...]
    row, lane = iota(shape, 0), iota(shape, 1)
    tile_lane = iota((COLS, LANES), 1)
    total = jnp.zeros(shape, f32)
    turn = jnp.zeros(shape, f32)
    flux_x = jnp.zeros(shape, f32)
    flux_y = jnp.zeros(shape, f32)
    fold = jnp.zeros((COLS, LANES), f32)

    def put(tile, at, column):
        return jnp.where(tile_lane == at, column, tile)

    for k in range(K):
        mask = (lc > k).astype(f32)
        u, v = zonal[k], meridional[k]
        mt, mu, mv = mask * tracer[k], mask * u, mask * v
        p = mu + mv
        total += thickness(k) * p
        turn += thickness(k) * (mv - mu)
        flux_x += thickness(k) * (mask * roll(p, -1, 0) - roll(mask, -1, 0) * p)
        flux_y += thickness(k) * (mask * roll(p, -1, 1) - roll(mask, -1, 1) * p)
        fold = put(fold, LANE_P + k, p[:, NY - 1:])
        for base, field in ((0, mt), (1, mu), (2, mv)):
            west, east = field[:1], field[COLS - 1:]
            at = 2 * COLS + base * K + k
            inner[at:at + 1] = jnp.where(even, east, west)
            outer[at:at + 1] = jnp.where(even, west, east)
            fold = put(fold, LANE_MT + base * K + k, field[:, NY - 1:])
    fold = put(fold, LANE_LC, lc[:, NY - 1:])
    fold = put(fold, LANE_DIFF, diff[:, NY - 1:])
    flux_x = jnp.where(row == COLS - 1, 0.0, flux_x)
    flux_y = jnp.where(lane == NY - 1, 0.0, flux_y)
    west_flux = jnp.where(row == 0, 0.0, roll(flux_x, 1, 0))
    south_flux = jnp.where(lane == 0, 0.0, roll(flux_y, 1, 1))
    forcing = total + planetary(shape) * turn + diff * (
        flux_x - west_flux + flux_y - south_flux
    )
    coded = jnp.where(lc > 0, surface[...], -1.0)
    zeros = jnp.zeros((COLS, NY - LANES), f32)
    for pack, mine, other in ((inner, COLS - 1, 0), (outer, 0, COLS - 1)):
        pack[0:COLS] = forcing
        pack[COLS:2 * COLS] = coded
        edge_lc = jnp.where(even, lc[mine:mine + 1], lc[other:other + 1])
        edge_diff = jnp.where(even, diff[mine:mine + 1], diff[other:other + 1])
        pack[64:72] = jnp.where(row == 0, edge_lc, jnp.where(row == 1, edge_diff, 0.0))
        pack[72:80] = jnp.concatenate([fold, zeros], axis=1)


def interface_flux(mine, theirs):
    level = iota((K, NY), 0).astype(f32)
    p_mine = mine[32:48] + mine[48:64]
    p_theirs = theirs[32:48] + theirs[48:64]
    return level_sum(
        jnp.where(level < mine[64:65], p_theirs, 0.0)
        - jnp.where(level < theirs[64:65], p_mine, 0.0)
    )


def halo_kernel(inner, outer, sibling, beyond, forcing, coded, tile, flipped):
    shape = (EXT, NY)
    even = lax.axis_index("lon") % 2 == 0
    flux_in = interface_flux(inner, sibling)
    flux_out = interface_flux(outer, beyond)
    row = iota(shape, 0)

    def arrange(at):
        own = inner[at:at + COLS]
        east, west = sibling[at:at + COLS], beyond[at:at + COLS]
        first = jnp.where(even, west, east)
        last = jnp.where(even, east, west)
        return jnp.concatenate([first, own, last], axis=0)

    def choose(a, b):
        return jnp.where(even, a, b)

    west_own = choose(outer[65:66] * flux_out, inner[65:66] * flux_in)
    west_far = choose(beyond[65:66] * flux_out, sibling[65:66] * flux_in)
    east_own = choose(inner[65:66] * flux_in, outer[65:66] * flux_out)
    east_far = choose(sibling[65:66] * flux_in, beyond[65:66] * flux_out)
    change = jnp.where(
        row == COLS - 1,
        -west_far,
        jnp.where(
            row == COLS,
            west_own,
            jnp.where(row == 2 * COLS - 1, east_own, jnp.where(row == 2 * COLS, -east_far, 0.0)),
        ),
    )
    full = arrange(0) + change
    code = arrange(COLS)
    forcing[...] = full
    coded[...] = code
    lane = iota((EXT, LANES), 1)
    fold = arrange(72)[:, :LANES]
    for j in range(COLS):
        at = NY - 1 - j
        fold = jnp.where(lane == j, full[:, at:at + 1], fold)
        fold = jnp.where(lane == COLS + j, code[:, at:at + 1], fold)
    tile[...] = fold
    flipped[...] = jnp.concatenate([fold[EXT - 1 - i:EXT - i] for i in range(EXT)], axis=0)


def basis_kernel(forcing, coded, tile, mirror, vectors, gram):
    width = NY + LANES
    lane = iota((EXT, LANES), 1)
    mine, theirs = tile[...], mirror[...]
    level = (lane - LANE_P).astype(f32)
    weight = jnp.where((lane >= LANE_P) & (lane < LANE_P + K), 0.5 * (0.5 + level / K), 0.0)
    mask_mine = (level < mine[:, LANE_LC:LANE_LC + 1]).astype(f32)
    mask_theirs = (level < theirs[:, LANE_LC:LANE_LC + 1]).astype(f32)
    flux = -jnp.sum(weight * (mask_mine * theirs + mask_theirs * mine), axis=1, keepdims=True)
    own_change = mine[:, LANE_DIFF:LANE_DIFF + 1] * flux
    far_change = theirs[:, LANE_DIFF:LANE_DIFF + 1] * flux
    north = jnp.where(lane < COLS, theirs, 0.0)
    north = north + jnp.where(lane == 0, far_change, 0.0)
    body_lane = iota((EXT, NY), 1)
    south = forcing[...] + jnp.where(body_lane == NY - 1, own_change, 0.0)
    north_code = jnp.where(lane < COLS, roll(theirs, -COLS, 1), -1.0)
    code = jnp.concatenate([coded[...], north_code], axis=1)
    ocean = code > 0
    centre = jnp.where(ocean, code / scale, 0.0)
    around = jnp.where(ocean, 1.0 / scale, 0.0)
    wide_lane = iota((EXT, width), 1)

    def operate(q):
        along = roll(q, -1, 1) + jnp.where(wide_lane == 0, 0.0, roll(q, 1, 1))
        beside = q + corner_weight * along
        return centre * q - around * (along + roll(beside, 1, 0) + roll(beside, -1, 0))

    v = [jnp.concatenate([south, north], axis=1)]
    v.append(operate(v[0]))
    for j in range(2, BASIS):
        v.append(2.0 * operate(v[-1]) - v[-2])
    for j in range(ITERS):
        vectors[j * EXT:(j + 1) * EXT] = v[j]
    own = [[q[COLS:2 * COLS, c * LANES:(c + 1) * LANES] for c in range(NY // LANES)] for q in v]
    parts = [[split(q) for q in row] for row in own]
    sub = iota((COLS, LANES), 0)
    tile_lane = iota((COLS, LANES), 1)
    sums = {}
    for i in range(BASIS):
        for j in range(i, BASIS):
            terms = [
                two_prod(own[i][c], own[j][c], parts[i][c], parts[j][c])
                for c in range(NY // LANES)
            ]
            sums[i, j] = sums[j, i] = pair_rows(pair_tree(terms))
    out = jnp.zeros((COLS, LANES), f32)
    for i in range(BASIS):
        column = (jnp.zeros((COLS, LANES), f32), jnp.zeros((COLS, LANES), f32))
        for j in range(BASIS):
            column = tuple(jnp.where(sub == j, s, c) for s, c in zip(sums[i, j], column))
        step = LANES // 2
        while step:
            column = pair_add(column, (roll(column[0], step, 1), roll(column[1], step, 1)))
            step //= 2
        column = pair_norm(column)
        out = jnp.where(tile_lane == i, column[0], out)
        out = jnp.where(tile_lane == LANES // 2 + i, column[1], out)
    gram[...] = out


def coefficients(gram):
    shape = (COLS, LANES)
    tiles = [gram[i * COLS:(i + 1) * COLS] for i in range(gram.shape[0] // COLS)]
    total = pair_norm(pair_tree([(t, roll(t, LANES // 2, 1)) for t in tiles]))
    wide = lambda column: jnp.broadcast_to(column, shape)
    matrix = [tuple(wide(part[:, j:j + 1]) for part in total) for j in range(BASIS)]
    sub = iota(shape, 0)
    first = (sub == 0).astype(f32)
    zero = jnp.zeros(shape, f32)

    def apply(b):
        half = scale / 2
        up = [half * jnp.where(sub == 0, 0.0, roll(part, 1, 0)) for part in b]
        up = [jnp.where(sub == 1, 2.0 * part, part) for part in up]
        down = [half * jnp.where(sub == COLS - 1, 0.0, roll(part, -1, 0)) for part in b]
        four = tuple(4.0 * part for part in b)
        return pair_norm(pair_add(pair_add(four, b), pair_add(tuple(up), tuple(down))))

    def times(vector, count):
        terms = []
        for j in range(count):
            at = tuple(wide(part[j:j + 1]) for part in vector)
            terms.append(pair_mul(matrix[j], at))
        return pair_norm(pair_tree(terms))

    def dot(a, b):
        s = pair_rows(pair_mul(a, b))
        return s[0] + s[1]

    residual = (first, zero)
    image = matrix[0]
    direction = residual
    solution = zero
    norm_now = wide(matrix[0][0][:1])
    floor = 1e-13 * norm_now
    alive = norm_now > 0
    for iteration in range(ITERS):
        applied = apply(direction)
        applied_image = times(applied, iteration + 2)
        curvature = dot(direction, applied_image)
        alive = alive & (curvature > 0)
        step = jnp.where(alive, norm_now / jnp.where(alive, curvature, 1.0), 0.0)
        solution = solution + step * direction[0]
        if iteration + 1 < ITERS:
            back = -step
            residual = pair_norm(pair_add(residual, pair_scale(applied, back)))
            image = pair_norm(pair_add(image, pair_scale(applied_image, back)))
            norm_next = dot(residual, image)
            ratio = jnp.where(alive, norm_next / jnp.where(alive, norm_now, 1.0), 0.0)
            direction = pair_norm(pair_add(residual, pair_scale(direction, ratio)))
            norm_now = norm_next
            alive = alive & (norm_now > floor)
    return solution


def finish_kernel(gram, vectors, zonal, meridional, count, zonal_next, meridional_next, height):
    x = coefficients(gram)
    total = jnp.zeros((EXT, NY + LANES), f32)
    for j in range(ITERS):
        total += x[j:j + 1, :1] * vectors[j * EXT:(j + 1) * EXT]
    own = total[COLS:2 * COLS, :NY]
    height[...] = own
    east = gravity * (roll(total, -1, 0)[COLS:2 * COLS, :NY] - own)
    north = gravity * (roll(total, -1, 1)[COLS:2 * COLS, :NY] - own)
    lc = count[...]
    for k in range(K):
        zonal_next[k] = zonal[k] - jnp.where(lc > k, east, 0.0)
        meridional_next[k] = meridional[k] - jnp.where(lc > k, north, 0.0)


def step_kernel(
    tracer, zonal, meridional, count, diffusivity, sibling, beyond, mirror,
    tracer_next, zonal_step, meridional_step,
):
    shape = (COLS, NY)
    even = lax.axis_index("lon") % 2 == 0
    row, lane = iota(shape, 0), iota(shape, 1)
    lc = count[...].astype(f32)
    diff = diffusivity[...]
    turn = planetary(shape)
    north_tile = mirror[COLS:2 * COLS]
    sib_lc, out_lc = sibling[64:65], beyond[64:65]
    west_lc, east_lc = jnp.where(even, out_lc, sib_lc), jnp.where(even, sib_lc, out_lc)
    north_lc = north_tile[:, LANE_LC:LANE_LC + 1]

    def around(field, west, east, north):
        return (
            jnp.where(row == COLS - 1, east, roll(field, -1, 0)),
            jnp.where(row == 0, west, roll(field, 1, 0)),
            jnp.where(lane == NY - 1, north, roll(field, -1, 1)),
            jnp.where(lane == 0, 0.0, roll(field, 1, 1)),
        )

    def edges(base, k):
        at = 2 * COLS + base * K + k
        a, b = sibling[at:at + 1], beyond[at:at + 1]
        return jnp.where(even, b, a), jnp.where(even, a, b)

    def masked(k):
        if k < 0 or k >= K:
            return jnp.zeros(shape, f32), jnp.zeros(shape, f32)
        mask = (lc > k).astype(f32)
        return mask, mask * tracer[k]

    below, here = masked(-1), masked(0)
    for k in range(K):
        above = masked(k + 1)
        mask, mt = here
        t, u, v = tracer[k], zonal[k], meridional[k]
        mask_sum = sum(
            around(
                mask,
                (west_lc > k).astype(f32),
                (east_lc > k).astype(f32),
                (north_lc > k).astype(f32),
            )
        )
        fields = []
        for base, field, sign in ((0, mt, 1.0), (1, mask * u, -1.0), (2, mask * v, -1.0)):
            at = LANE_MT + base * K + k
            fields.append(around(field, *edges(base, k), sign * north_tile[:, at:at + 1]))
        te, tw, tn, ts = fields[0]
        vertical = above[1] + below[1] - (above[0] + below[0]) * t
        tracer_next[k] = mask * (
            t
            + diff * (te + tw + tn + ts - mask_sum * t)
            + vertical_mix * vertical
            - advection * (u * (te - tw) + v * (tn - ts))
        )
        zonal_step[k] = mask * (u + diff * (sum(fields[1]) - mask_sum * u) + turn * v)
        meridional_step[k] = mask * (v + diff * (sum(fields[2]) - mask_sum * v) - turn * u)
        below, here = here, above


def call(kernel, shapes, *args, flops=0):
    moved = 4 * sum(a.size for a in args) + 4 * sum(
        functools.reduce(lambda x, y: x * y, s, 1) for s in shapes
    )
    space = pl.BlockSpec(memory_space=pltpu.VMEM)
    return pl.pallas_call(
        kernel,
        out_shape=[jax.ShapeDtypeStruct(s, f32) for s in shapes],
        in_specs=[space] * len(args),
        out_specs=[space] * len(shapes),
        compiler_params=pltpu.CompilerParams(vmem_limit_bytes=32 * 1024 * 1024),
        cost_estimate=pl.CostEstimate(flops=flops, bytes_accessed=moved, transcendentals=0),
    )(*args)


def body(tracer, zonal, meridional, count, diffusivity, surface):
    size = lax.axis_size("lon")
    block = (K, COLS, NY)

    def permute(value, pairs):
        return lax.ppermute(value, "lon", pairs)

    siblings = [(i, i ^ 1) for i in range(size)]
    outward = [(i, (i + 1 if i % 2 else i - 1) % size) for i in range(size)]
    mirrored = [(i, size - 1 - i) for i in range(size)]
    inner, outer = call(
        pack_kernel, [(PACK, NY)] * 2, tracer, zonal, meridional, count, diffusivity, surface
    )
    beyond = permute(outer, outward)
    sibling = permute(inner, siblings)
    forcing, coded, tile, flipped = call(
        halo_kernel,
        [(EXT, NY), (EXT, NY), (EXT, LANES), (EXT, LANES)],
        inner, outer, sibling, beyond,
    )
    mirror = permute(flipped, mirrored)
    vectors, gram = call(
        basis_kernel,
        [(ITERS * EXT, NY + LANES), (COLS, LANES)],
        forcing, coded, tile, mirror,
    )
    tracer_next, zonal_step, meridional_step = call(
        step_kernel, [block] * 3,
        tracer, zonal, meridional, count, diffusivity, sibling, beyond, mirror,
        flops=65536 * 80,
    )
    reach = 1
    while reach < size:
        across = reach ^ 1 if reach > 1 else 1
        gram = jnp.concatenate(
            [gram, permute(gram, [(i, i ^ across) for i in range(size)])], axis=0
        )
        reach *= 2
    zonal_next, meridional_next, height = call(
        finish_kernel, [block, block, (COLS, NY)],
        gram, vectors, zonal_step, meridional_step, count,
    )
    return tracer_next, zonal_next, meridional_next, height


def solution(mesh):
    column = P("lon", None)
    field = P("ens", "lon", None)
    return jax.shard_map(
        body,
        mesh=mesh,
        in_specs=(field, field, field, column, column, column),
        out_specs=(field, field, field, P("lon", "ens")),
        check_vma=False,
    )
```

time: 668 us -> 37.9 us (0.06)
  the two profiles are of different devices: /device:TPU:0 before, /device:TPU:1 now
where the time goes in v1:
time: 37.9 us; the launch traced here: 37.4 us
  waiting for transfers between devices  13.7 us (36%)
  starting transfers between devices  12.7 us (34%)
  Pallas kernels  5.33 us (14%)
  local copies, waits for them, and re-layouts  5.02 us (13%)
  between operations  0.68 us (2%)
    ppermute x7, waiting for transfers between devices, permute(): return lax.ppermute(value, 'lon', pairs)  13.7 us
    ppermute x7, starting transfers between devices, permute(): return lax.ppermute(value, 'lon', pairs)  12.7 us
    pallas_call x5, Pallas kernels, call(): pl.pallas_call(kernel, out_shape=[jax.ShapeDtypeStruct(s, f32) for s in s...  5.33 us
    unnamed x22, local copies, waits for them, and re-layouts  5.01 us
  transfers between devices with their start and end apart: 7, of which 5 were waited for; matrix products, arithmetic and copies ran while one was open for 0% of the time, Pallas kernels for 4%

profile of v1, /device:TPU:1, one launch (start us, length us, event | category | flops | bytes accessed | tf_op | source)
XLA Modules:
  0.0 37.4 jit_solution(3432484030039116863)
XLA Ops:
  0.6 0.0 copy-start
  0.6 0.9 %copy-done = f32[16,8,512]{2,1,0:T(8,128)S(1)} copy-done((f32[16,8,512]{2,1,0:T(8,128)S(1)}, f32[16,8,512]{2,1,0:T(8,128)}, u32[]{:S(2)}) %copy-start) | copy-done | bytes 262168
  1.6 0.0 copy-start.2
  1.6 0.9 %copy-done.2 = f32[16,8,512]{2,1,0:T(8,128)S(1)} copy-done((f32[16,8,512]{2,1,0:T(8,128)S(1)}, f32[16,8,512]{2,1,0:T(8,128)}, u32[]{:S(2)}) %copy-start.2) | copy-done | bytes 262168
  2.5 0.0 copy-start.4
  2.5 0.9 %copy-done.4 = f32[16,8,512]{2,1,0:T(8,128)S(1)} copy-done((f32[16,8,512]{2,1,0:T(8,128)S(1)}, f32[16,8,512]{2,1,0:T(8,128)}, u32[]{:S(2)}) %copy-start.4) | copy-done | bytes 262168
  3.5 0.0 copy-start.6
  3.5 0.7 %copy-done.6 = s32[8,512]{1,0:T(8,128)S(1)} copy-done((s32[8,512]{1,0:T(8,128)S(1)}, s32[8,512]{1,0:T(8,128)}, u32[]{:S(2)}) %copy-start.6) | copy-done | bytes 16408
  4.2 0.0 copy-start.7
  4.2 0.7 %copy-done.7 = f32[8,512]{1,0:T(8,128)S(1)} copy-done((f32[8,512]{1,0:T(8,128)S(1)}, f32[8,512]{1,0:T(8,128)}, u32[]{:S(2)}) %copy-start.7) | copy-done | bytes 16408
  4.9 0.0 copy-start.8
  4.9 0.7 %copy-done.8 = f32[8,512]{1,0:T(8,128)S(1)} copy-done((f32[8,512]{1,0:T(8,128)S(1)}, f32[8,512]{1,0:T(8,128)}, u32[]{:S(2)}) %copy-start.8) | copy-done | bytes 16408
  5.6 0.5 %shard_map.93 = (f32[80,512]{1,0:T(8,128)S(1)}, f32[80,512]{1,0:T(8,128)S(1)}) custom-call(f32[16,8,512]{2,1,0:T(8,128)S(1)} %copy-done, f32[16,8,512]{2,1,0:T(8,128)S(1)} %copy-done.2, f32[16,8,512]{2,1,0:T(8,128)S(1)} %copy-done.4, s32[8,512]{1,0:T(8,128)S(1)} %copy-done.6, f32[8,512]{1,0:T(8,128)S(1)} %copy-done.7, f32[8,512]{1,0:T(8,128)S(1)} %copy-done.8), custom_call_target="tpu_custom_call" | custom-call | bytes 1163264 | tf_op jit(solution)/shard_map/pallas_call | solution.py:419
  6.1 0.1 collective-permute-start
  6.2 0.0 copy-start.1
  6.2 0.0 copy-start.3
  6.2 0.0 copy-start.5
  6.2 2.7 %collective-permute-start.1 = (f32[80,512]{1,0:T(8,128)S(1)}, f32[80,512]{1,0:T(8,128)S(1)}, u32[]{:S(2)}, u32[]{:S(2)}) collective-permute-start(f32[80,512]{1,0:T(8,128)S(1)} %get-tuple-element.19.outer), channel_id=1, source_target_pairs={{0,15},{1,2},{2,1},{3,4},{4,3},{5,6},{6,5},{7,8},{8,7},{9,10},{10,... | collective-permute-start | bytes 491528 | tf_op jit(solution)/shard_map/ppermute | solution.py:434
  8.9 0.0 collective-permute-done.sibling
  8.9 3.0 %collective-permute-done.1.beyond = f32[80,512]{1,0:T(8,128)S(1)} collective-permute-done((f32[80,512]{1,0:T(8,128)S(1)}, f32[80,512]{1,0:T(8,128)S(1)}, u32[]{:S(2)}, u32[]{:S(2)}) %collective-permute-start.1) | collective-permute-done | bytes 163872 | tf_op jit(solution)/shard_map/ppermute | solution.py:434
  11.9 0.2 shard_map.94
  12.1 5.2 %collective-permute-start.2 = (f32[24,128]{1,0:T(8,128)S(1)}, f32[24,128]{1,0:T(8,128)S(1)}, u32[]{:S(2)}, u32[]{:S(2)}) collective-permute-start(f32[24,128]{1,0:T(8,128)S(1)} %get-tuple-element.20), channel_id=1, source_target_pairs={{0,15},{1,14},{2,13},{3,12},{4,11},{5,10},{6,9},{7,8},{8,7},{9,6},... | collective-permute-start | bytes 36872 | tf_op jit(solution)/shard_map/ppermute | solution.py:434
  17.3 1.4 %collective-permute-done.2.mirror = f32[24,128]{1,0:T(8,128)S(1)} collective-permute-done((f32[24,128]{1,0:T(8,128)S(1)}, f32[24,128]{1,0:T(8,128)S(1)}, u32[]{:S(2)}, u32[]{:S(2)}) %collective-permute-start.2) | collective-permute-done | bytes 12320 | tf_op jit(solution)/shard_map/ppermute | solution.py:434
  18.7 1.5 %shard_map.96 = (f32[144,640]{1,0:T(8,128)S(1)}, f32[8,128]{1,0:T(8,128)S(1)}) custom-call(f32[24,512]{1,0:T(8,128)S(1)} %get-tuple-element.22.forcing, f32[24,512]{1,0:T(8,128)S(1)} %get-tuple-element.23.coded, f32[24,128]{1,0:T(8,128)S(1)} %get-tuple-element.24.tile, f32[24,128]{1,0:T(8,128)S(1)} %collective-permute-done.2.mirror), custom_call_target="tpu_custom_call" | custom-call | bytes 495616 | tf_op jit(solution)/shard_map/pallas_call | solution.py:419
  20.2 2.8 %collective-permute-start.3 = (f32[8,128]{1,0:T(8,128)S(1)}, f32[8,128]{1,0:T(8,128)S(1)}, u32[]{:S(2)}, u32[]{:S(2)}) collective-permute-start(f32[8,128]{1,0:T(8,128)S(1)} %get-tuple-element.25), channel_id=1, source_target_pairs={{0,1},{1,0},{2,3},{3,2},{4,5},{5,4},{6,7},{7,6},{8,9},{9,8},{10,11... | collective-permute-start | bytes 12296 | tf_op jit(solution)/shard_map/ppermute | solution.py:434
  23.0 0.0 copy-done.1
  23.0 0.0 copy-done.3
  23.0 0.0 copy-done.5
  23.0 1.6 %shard_map.95 = (f32[16,8,512]{2,1,0:T(8,128)}, f32[16,8,512]{2,1,0:T(8,128)S(1)}, f32[16,8,512]{2,1,0:T(8,128)S(1)}) custom-call(f32[16,8,512]{2,1,0:T(8,128)S(1)} %copy-done.1, f32[16,8,512]{2,1,0:T(8,128)S(1)} %copy-done.3, f32[16,8,512]{2,1,0:T(8,128)S(1)} %copy-done.5, s32[8,512]{1,0:T(8,128)S(1)} %copy-done.6, f32[8,512]{1,0:T(8,128)S(1)} %copy-done.7, ...), custom_call_target="tpu_custom_call" | custom-call | flops 5242880 | bytes 1945600 | tf_op jit(solution)/shard_map/pallas_call | solution.py:419
  24.6 0.0 collective-permute-done.3
  24.6 0.1 collective-permute-start.4
  24.7 3.0 %collective-permute-done.4 = f32[16,128]{1,0:T(8,128)S(1)} collective-permute-done((f32[16,128]{1,0:T(8,128)S(1)}, f32[16,128]{1,0:T(8,128)S(1)}, u32[]{:S(2)}, u32[]{:S(2)}) %collective-permute-start.4) | collective-permute-done | bytes 8224 | tf_op jit(solution)/shard_map/ppermute | solution.py:434
  27.7 0.0 collective-permute-start.5
  27.7 3.2 %collective-permute-done.5 = f32[32,128]{1,0:T(8,128)S(1)} collective-permute-done((f32[32,128]{1,0:T(8,128)S(1)}, f32[32,128]{1,0:T(8,128)S(1)}, u32[]{:S(2)}, u32[]{:S(2)}) %collective-permute-start.5) | collective-permute-done | bytes 16416 | tf_op jit(solution)/shard_map/ppermute | solution.py:434
  30.8 1.8 %collective-permute-start.6 = (f32[64,128]{1,0:T(8,128)S(1)}, f32[64,128]{1,0:T(8,128)S(1)}, u32[]{:S(2)}, u32[]{:S(2)}) collective-permute-start(f32[64,128]{1,0:T(8,128)S(1)} %pad_maximum_fusion), channel_id=1, source_target_pairs={{0,9},{1,8},{2,11},{3,10},{4,13},{5,12},{6,15},{7,14},{8,1},{9,0},... | collective-permute-start | bytes 98312 | tf_op jit(solution)/shard_map/ppermute | solution.py:434
  32.6 3.1 %collective-permute-done.6 = f32[64,128]{1,0:T(8,128)S(1)} collective-permute-done((f32[64,128]{1,0:T(8,128)S(1)}, f32[64,128]{1,0:T(8,128)S(1)}, u32[]{:S(2)}, u32[]{:S(2)}) %collective-permute-start.6) | collective-permute-done | bytes 32800 | tf_op jit(solution)/shard_map/ppermute | solution.py:434
  35.8 1.6 %shard_map.97 = (f32[16,8,512]{2,1,0:T(8,128)}, f32[16,8,512]{2,1,0:T(8,128)}, f32[8,512]{1,0:T(8,128)}) custom-call(f32[128,128]{1,0:T(8,128)S(1)} %constant_dynamic-update-slice_fusion.gram, f32[144,640]{1,0:T(8,128)S(1)} %get-tuple-element.26.vectors, f32[16,8,512]{2,1,0:T(8,128)S(1)} %get-tuple-element.27.zonal, ...), custom_call_target="tpu_custom_call" | custom-call | bytes 1515520 | tf_op jit(solution)/shard_map/pallas_call | solution.py:419
  (8 shorter events, 0.0 us)
Async XLA Ops:
  0.6 1.0 %copy-start = (f32[16,8,512]{2,1,0:T(8,128)S(1)}, f32[16,8,512]{2,1,0:T(8,128)}, u32[]{:S(2)}) copy-start(f32[16,8,512]{2,1,0:T(8,128)} %tracer.3) | copy-start | bytes 786436
  1.6 0.9 %copy-start.2 = (f32[16,8,512]{2,1,0:T(8,128)S(1)}, f32[16,8,512]{2,1,0:T(8,128)}, u32[]{:S(2)}) copy-start(f32[16,8,512]{2,1,0:T(8,128)} %zonal.3) | copy-start | bytes 786436
  2.5 0.9 %copy-start.4 = (f32[16,8,512]{2,1,0:T(8,128)S(1)}, f32[16,8,512]{2,1,0:T(8,128)}, u32[]{:S(2)}) copy-start(f32[16,8,512]{2,1,0:T(8,128)} %meridional.3) | copy-start | bytes 786436
  3.5 0.7 %copy-start.6 = (s32[8,512]{1,0:T(8,128)S(1)}, s32[8,512]{1,0:T(8,128)}, u32[]{:S(2)}) copy-start(s32[8,512]{1,0:T(8,128)} %count.5) | copy-start | bytes 49156
  4.2 0.7 %copy-start.7 = (f32[8,512]{1,0:T(8,128)S(1)}, f32[8,512]{1,0:T(8,128)}, u32[]{:S(2)}) copy-start(f32[8,512]{1,0:T(8,128)} %diffusivity.3) | copy-start | bytes 49156
  4.9 0.7 %copy-start.8 = (f32[8,512]{1,0:T(8,128)S(1)}, f32[8,512]{1,0:T(8,128)}, u32[]{:S(2)}) copy-start(f32[8,512]{1,0:T(8,128)} %surface.1) | copy-start | bytes 49156
  6.1 2.8 %collective-permute-start = (f32[80,512]{1,0:T(8,128)S(1)}, f32[80,512]{1,0:T(8,128)S(1)}, u32[]{:S(2)}, u32[]{:S(2)}) collective-permute-start(f32[80,512]{1,0:T(8,128)S(1)} %get-tuple-element.18.inner), channel_id=1, source_target_pairs={{0,1},{1,0},{2,3},{3,2},{4,5},{5,4},{6,7},{7,6},{8,9},{9,8},{10,11... | collective-permute-start | bytes 491528 | tf_op jit(solution)/shard_map/ppermute | solution.py:434
  6.2 16.8 %copy-start.1 = (f32[16,8,512]{2,1,0:T(8,128)S(1)}, f32[16,8,512]{2,1,0:T(8,128)}, u32[]{:S(2)}) copy-start(f32[16,8,512]{2,1,0:T(8,128)} %tracer.3) | copy-start | bytes 786436
  6.2 16.8 %copy-start.3 = (f32[16,8,512]{2,1,0:T(8,128)S(1)}, f32[16,8,512]{2,1,0:T(8,128)}, u32[]{:S(2)}) copy-start(f32[16,8,512]{2,1,0:T(8,128)} %zonal.3) | copy-start | bytes 786436
  6.2 16.8 %copy-start.5 = (f32[16,8,512]{2,1,0:T(8,128)S(1)}, f32[16,8,512]{2,1,0:T(8,128)}, u32[]{:S(2)}) copy-start(f32[16,8,512]{2,1,0:T(8,128)} %meridional.3) | copy-start | bytes 786436
  6.2 5.7 %collective-permute-start.1 = (f32[80,512]{1,0:T(8,128)S(1)}, f32[80,512]{1,0:T(8,128)S(1)}, u32[]{:S(2)}, u32[]{:S(2)}) collective-permute-start(f32[80,512]{1,0:T(8,128)S(1)} %get-tuple-element.19.outer), channel_id=1, source_target_pairs={{0,15},{1,2},{2,1},{3,4},{4,3},{5,6},{6,5},{7,8},{8,7},{9,10},{10,... | collective-permute-start | bytes 491528 | tf_op jit(solution)/shard_map/ppermute | solution.py:434
  12.1 6.6 %collective-permute-start.2 = (f32[24,128]{1,0:T(8,128)S(1)}, f32[24,128]{1,0:T(8,128)S(1)}, u32[]{:S(2)}, u32[]{:S(2)}) collective-permute-start(f32[24,128]{1,0:T(8,128)S(1)} %get-tuple-element.20), channel_id=1, source_target_pairs={{0,15},{1,14},{2,13},{3,12},{4,11},{5,10},{6,9},{7,8},{8,7},{9,6},... | collective-permute-start | bytes 36872 | tf_op jit(solution)/shard_map/ppermute | solution.py:434
  20.2 4.4 %collective-permute-start.3 = (f32[8,128]{1,0:T(8,128)S(1)}, f32[8,128]{1,0:T(8,128)S(1)}, u32[]{:S(2)}, u32[]{:S(2)}) collective-permute-start(f32[8,128]{1,0:T(8,128)S(1)} %get-tuple-element.25), channel_id=1, source_target_pairs={{0,1},{1,0},{2,3},{3,2},{4,5},{5,4},{6,7},{7,6},{8,9},{9,8},{10,11... | collective-permute-start | bytes 12296 | tf_op jit(solution)/shard_map/ppermute | solution.py:434
  24.6 3.1 %collective-permute-start.4 = (f32[16,128]{1,0:T(8,128)S(1)}, f32[16,128]{1,0:T(8,128)S(1)}, u32[]{:S(2)}, u32[]{:S(2)}) collective-permute-start(f32[16,128]{1,0:T(8,128)S(1)} %pad_maximum_fusion.2), channel_id=1, source_target_pairs={{0,3},{1,2},{2,1},{3,0},{4,7},{5,6},{6,5},{7,4},{8,11},{9,10},{10,... | collective-permute-start | bytes 24584 | tf_op jit(solution)/shard_map/ppermute | solution.py:434
  27.7 3.2 %collective-permute-start.5 = (f32[32,128]{1,0:T(8,128)S(1)}, f32[32,128]{1,0:T(8,128)S(1)}, u32[]{:S(2)}, u32[]{:S(2)}) collective-permute-start(f32[32,128]{1,0:T(8,128)S(1)} %pad_maximum_fusion.1), channel_id=1, source_target_pairs={{0,5},{1,4},{2,7},{3,6},{4,1},{5,0},{6,3},{7,2},{8,13},{9,12},{10,... | collective-permute-start | bytes 49160 | tf_op jit(solution)/shard_map/ppermute | solution.py:434
  30.8 4.9 %collective-permute-start.6 = (f32[64,128]{1,0:T(8,128)S(1)}, f32[64,128]{1,0:T(8,128)S(1)}, u32[]{:S(2)}, u32[]{:S(2)}) collective-permute-start(f32[64,128]{1,0:T(8,128)S(1)} %pad_maximum_fusion), channel_id=1, source_target_pairs={{0,9},{1,8},{2,11},{3,10},{4,13},{5,12},{6,15},{7,14},{8,1},{9,0},... | collective-permute-start | bytes 98312 | tf_op jit(solution)/shard_map/ppermute | solution.py:434

commit v2 on v1

--- a/solution.py
+++ b/solution.py
@@ -15,6 +15,7 @@
 LANES = 128
 PACK = 80
 BASIS = ITERS + 1
+CHUNKS = 4
 
 vertical_mix = 0.1
 advection = 0.25
@@ -111,9 +112,33 @@
     return a
 
 
-def pack_kernel(tracer, zonal, meridional, count, diffusivity, surface, inner, outer):
+def pack_kernel(
+    tracer_in, zonal_in, meridional_in, count_in, diffusivity_in, surface_in, inner, outer,
+    tracer, zonal, meridional, count, diffusivity, surface, sems,
+):
     shape = (COLS, NY)
     even = lax.axis_index("lon") % 2 == 0
+    small = [
+        pltpu.make_async_copy(a, b, sems.at[i])
+        for i, (a, b) in enumerate(
+            ((count_in, count), (diffusivity_in, diffusivity), (surface_in, surface))
+        )
+    ]
+    large = []
+    for c in range(CHUNKS):
+        part = pl.ds(c * K // CHUNKS, K // CHUNKS)
+        large.append(
+            [
+                pltpu.make_async_copy(a.at[part], b.at[part], sems.at[3 + 3 * c + i])
+                for i, (a, b) in enumerate(
+                    ((zonal_in, zonal), (meridional_in, meridional), (tracer_in, tracer))
+                )
+            ]
+        )
+    for copy in small + sum(large, []):
+        copy.start()
+    for copy in small:
+        copy.wait()
     lc = count[...].astype(f32)
     diff = diffusivity[...]
     row, lane = iota(shape, 0), iota(shape, 1)
@@ -128,6 +153,9 @@
         return jnp.where(tile_lane == at, column, tile)
 
     for k in range(K):
+        if k % (K // CHUNKS) == 0:
+            for copy in large[k // (K // CHUNKS)]:
+                copy.wait()
         mask = (lc > k).astype(f32)
         u, v = zonal[k], meridional[k]
         mt, mu, mv = mask * tracer[k], mask * u, mask * v
@@ -332,7 +360,7 @@
     return solution
 
 
-def finish_kernel(gram, vectors, zonal, meridional, count, zonal_next, meridional_next, height):
+def finish_kernel(gram, vectors, zonal, meridional, levels, zonal_next, meridional_next, height):
     x = coefficients(gram)
     total = jnp.zeros((EXT, NY + LANES), f32)
     for j in range(ITERS):
@@ -341,26 +369,18 @@
     height[...] = own
     east = gravity * (roll(total, -1, 0)[COLS:2 * COLS, :NY] - own)
     north = gravity * (roll(total, -1, 1)[COLS:2 * COLS, :NY] - own)
-    lc = count[...]
+    lc = levels[...]
     for k in range(K):
         zonal_next[k] = zonal[k] - jnp.where(lc > k, east, 0.0)
         meridional_next[k] = meridional[k] - jnp.where(lc > k, north, 0.0)
 
 
-def step_kernel(
-    tracer, zonal, meridional, count, diffusivity, sibling, beyond, mirror,
-    tracer_next, zonal_step, meridional_step,
-):
+def neighbours(count, sibling, beyond, mirror):
     shape = (COLS, NY)
     even = lax.axis_index("lon") % 2 == 0
     row, lane = iota(shape, 0), iota(shape, 1)
     lc = count[...].astype(f32)
-    diff = diffusivity[...]
-    turn = planetary(shape)
     north_tile = mirror[COLS:2 * COLS]
-    sib_lc, out_lc = sibling[64:65], beyond[64:65]
-    west_lc, east_lc = jnp.where(even, out_lc, sib_lc), jnp.where(even, sib_lc, out_lc)
-    north_lc = north_tile[:, LANE_LC:LANE_LC + 1]
 
     def around(field, west, east, north):
         return (
@@ -370,14 +390,33 @@
             jnp.where(lane == 0, 0.0, roll(field, 1, 1)),
         )
 
-    def edges(base, k):
-        at = 2 * COLS + base * K + k
+    def edges(at):
         a, b = sibling[at:at + 1], beyond[at:at + 1]
         return jnp.where(even, b, a), jnp.where(even, a, b)
 
+    def padded(field, base, k, sign):
+        at = LANE_MT + base * K + k
+        return around(field, *edges(2 * COLS + base * K + k), sign * north_tile[:, at:at + 1])
+
+    west_lc, east_lc = edges(64)
+    north_lc = north_tile[:, LANE_LC:LANE_LC + 1]
+
+    def mask_sum(mask, k):
+        inside = [(c > k).astype(f32) for c in (west_lc, east_lc, north_lc)]
+        return sum(around(mask, *inside))
+
+    return lc, padded, mask_sum
+
+
+def tracer_kernel(
+    tracer, zonal, meridional, count, diffusivity, sibling, beyond, mirror, after, tracer_next
+):
+    lc, padded, mask_sum = neighbours(count, sibling, beyond, mirror)
+    diff = diffusivity[...]
+
     def masked(k):
         if k < 0 or k >= K:
-            return jnp.zeros(shape, f32), jnp.zeros(shape, f32)
+            return jnp.zeros_like(lc), jnp.zeros_like(lc)
         mask = (lc > k).astype(f32)
         return mask, mask * tracer[k]
 
@@ -386,41 +425,55 @@
         above = masked(k + 1)
         mask, mt = here
         t, u, v = tracer[k], zonal[k], meridional[k]
-        mask_sum = sum(
-            around(
-                mask,
-                (west_lc > k).astype(f32),
-                (east_lc > k).astype(f32),
-                (north_lc > k).astype(f32),
-            )
-        )
-        fields = []
-        for base, field, sign in ((0, mt, 1.0), (1, mask * u, -1.0), (2, mask * v, -1.0)):
-            at = LANE_MT + base * K + k
-            fields.append(around(field, *edges(base, k), sign * north_tile[:, at:at + 1]))
-        te, tw, tn, ts = fields[0]
+        te, tw, tn, ts = padded(mt, 0, k, 1.0)
         vertical = above[1] + below[1] - (above[0] + below[0]) * t
         tracer_next[k] = mask * (
             t
-            + diff * (te + tw + tn + ts - mask_sum * t)
+            + diff * (te + tw + tn + ts - mask_sum(mask, k) * t)
             + vertical_mix * vertical
             - advection * (u * (te - tw) + v * (tn - ts))
         )
-        zonal_step[k] = mask * (u + diff * (sum(fields[1]) - mask_sum * u) + turn * v)
-        meridional_step[k] = mask * (v + diff * (sum(fields[2]) - mask_sum * v) - turn * u)
         below, here = here, above
 
 
-def call(kernel, shapes, *args, flops=0):
+def flow_kernel(
+    zonal, meridional, count, diffusivity, sibling, beyond, mirror, after,
+    zonal_step, meridional_step, levels,
+):
+    lc, padded, mask_sum = neighbours(count, sibling, beyond, mirror)
+    diff = diffusivity[...]
+    turn = planetary(lc.shape)
+    levels[...] = lc
+    for k in range(K):
+        mask = (lc > k).astype(f32)
+        u, v = zonal[k], meridional[k]
+        sides = mask_sum(mask, k)
+        zonal_sum = sum(padded(mask * u, 1, k, -1.0))
+        meridional_sum = sum(padded(mask * v, 2, k, -1.0))
+        zonal_step[k] = mask * (u + diff * (zonal_sum - sides * u) + turn * v)
+        meridional_step[k] = mask * (v + diff * (meridional_sum - sides * v) - turn * u)
+
+
+def call(kernel, shapes, *args, flops=0, after=None, scratch=(), stay=0):
     moved = 4 * sum(a.size for a in args) + 4 * sum(
         functools.reduce(lambda x, y: x * y, s, 1) for s in shapes
     )
     space = pl.BlockSpec(memory_space=pltpu.VMEM)
+    anywhere = pl.BlockSpec(memory_space=pl.ANY)
+    in_specs = [space] * (len(args) - stay) + [pl.BlockSpec(memory_space=pltpu.HBM)] * stay
+    here = len(args) - stay
+    args = args[:here] + tuple(
+        pltpu.with_memory_space_constraint(a, pltpu.HBM) for a in args[here:]
+    )
+    if after is not None:
+        in_specs.append(anywhere)
+        args = args + (after,)
     return pl.pallas_call(
         kernel,
         out_shape=[jax.ShapeDtypeStruct(s, f32) for s in shapes],
-        in_specs=[space] * len(args),
+        in_specs=in_specs,
         out_specs=[space] * len(shapes),
+        scratch_shapes=list(scratch),
         compiler_params=pltpu.CompilerParams(vmem_limit_bytes=32 * 1024 * 1024),
         cost_estimate=pl.CostEstimate(flops=flops, bytes_accessed=moved, transcendentals=0),
     )(*args)
@@ -436,8 +489,11 @@
     siblings = [(i, i ^ 1) for i in range(size)]
     outward = [(i, (i + 1 if i % 2 else i - 1) % size) for i in range(size)]
     mirrored = [(i, size - 1 - i) for i in range(size)]
+    arguments = (tracer, zonal, meridional, count, diffusivity, surface)
     inner, outer = call(
-        pack_kernel, [(PACK, NY)] * 2, tracer, zonal, meridional, count, diffusivity, surface
+        pack_kernel, [(PACK, NY)] * 2, *arguments,
+        scratch=[pltpu.VMEM(a.shape, a.dtype) for a in arguments]
+        + [pltpu.SemaphoreType.DMA((3 + 3 * CHUNKS,))], stay=len(arguments),
     )
     beyond = permute(outer, outward)
     sibling = permute(inner, siblings)
@@ -452,21 +508,26 @@
         [(ITERS * EXT, NY + LANES), (COLS, LANES)],
         forcing, coded, tile, mirror,
     )
-    tracer_next, zonal_step, meridional_step = call(
-        step_kernel, [block] * 3,
-        tracer, zonal, meridional, count, diffusivity, sibling, beyond, mirror,
-        flops=65536 * 80,
-    )
+    sums = [gram]
     reach = 1
     while reach < size:
-        across = reach ^ 1 if reach > 1 else 1
-        gram = jnp.concatenate(
-            [gram, permute(gram, [(i, i ^ across) for i in range(size)])], axis=0
-        )
+        other = permute(sums[-1], [(i, i ^ (reach ^ 1 if reach > 1 else 1)) for i in range(size)])
+        sums.append(jnp.concatenate([sums[-1], other], axis=0))
         reach *= 2
+    halos = (sibling, beyond, mirror)
+    tracer_next, = call(
+        tracer_kernel, [block],
+        tracer, zonal, meridional, count, diffusivity, *halos,
+        flops=65536 * 40, after=sums[min(2, len(sums) - 1)],
+    )
+    zonal_step, meridional_step, levels = call(
+        flow_kernel, [block, block, (COLS, NY)],
+        zonal, meridional, count, diffusivity, *halos,
+        flops=65536 * 40, after=sums[min(3, len(sums) - 1)],
+    )
     zonal_next, meridional_next, height = call(
         finish_kernel, [block, block, (COLS, NY)],
-        gram, vectors, zonal_step, meridional_step, count,
+        sums[-1], vectors, zonal_step, meridional_step, levels,
     )
     return tracer_next, zonal_next, meridional_next, height
 

time: 37.9 us -> 33.2 us (0.88)
  the two profiles are of different devices: /device:TPU:1 before, /device:TPU:0 now
where the time goes in v2:
time: 33.2 us; the launch traced here: 32.5 us
  starting transfers between devices  12.7 us (38%)
  waiting for transfers between devices  12.2 us (37%)
  Pallas kernels  6.84 us (21%)
  between operations  0.71 us (2%)
    ppermute x7, starting transfers between devices, permute(): return lax.ppermute(value, 'lon', pairs)  12.7 us
    ppermute x7, waiting for transfers between devices, permute(): return lax.ppermute(value, 'lon', pairs)  12.2 us
    pallas_call x6, Pallas kernels, call(): pl.pallas_call(kernel, out_shape=[jax.ShapeDtypeStruct(s, f32) for s in s...  6.84 us
  transfers between devices with their start and end apart: 7, of which 6 were waited for; matrix products, arithmetic and copies ran while one was open for 0% of the time, Pallas kernels for 6%

profile of v2, /device:TPU:0, one launch (start us, length us, event | category | flops | bytes accessed | tf_op | source)
XLA Modules:
  0.0 32.5 jit_solution(436135694495232440)
XLA Ops:
  0.6 1.8 %shard_map.93 = (f32[80,512]{1,0:T(8,128)S(1)}, f32[80,512]{1,0:T(8,128)S(1)}) custom-call(f32[16,8,512]{2,1,0:T(8,128)} %tracer.1, f32[16,8,512]{2,1,0:T(8,128)} %zonal.3, f32[16,8,512]{2,1,0:T(8,128)} %meridional.3, s32[8,512]{1,0:T(8,128)} %count.3, f32[8,512]{1,0:T(8,128)} %diffusivity.3, f32[8,512]{1,0:T(8,128)} %surface_in.1), custom_call_target="tpu_custom_call" | custom-call | bytes 1163264 | tf_op jit(solution)/shard_map/pallas_call | solution.py:471
  2.4 0.5 %collective-permute-start = (f32[80,512]{1,0:T(8,128)S(1)}, f32[80,512]{1,0:T(8,128)S(1)}, u32[]{:S(2)}, u32[]{:S(2)}) collective-permute-start(f32[80,512]{1,0:T(8,128)S(1)} %get-tuple-element.18.inner), channel_id=1, source_target_pairs={{0,1},{1,0},{2,3},{3,2},{4,5},{5,4},{6,7},{7,6},{8,9},{9,8},{10,11... | collective-permute-start | bytes 491528 | tf_op jit(solution)/shard_map/ppermute | solution.py:487
  2.9 5.7 %collective-permute-start.1 = (f32[80,512]{1,0:T(8,128)S(1)}, f32[80,512]{1,0:T(8,128)S(1)}, u32[]{:S(2)}, u32[]{:S(2)}) collective-permute-start(f32[80,512]{1,0:T(8,128)S(1)} %get-tuple-element.19.outer), channel_id=1, source_target_pairs={{0,15},{1,2},{2,1},{3,4},{4,3},{5,6},{6,5},{7,8},{8,7},{9,10},{10,... | collective-permute-start | bytes 491528 | tf_op jit(solution)/shard_map/ppermute | solution.py:487
  8.6 0.0 collective-permute-done.sibling
  8.6 3.0 %collective-permute-done.1.beyond = f32[80,512]{1,0:T(8,128)S(1)} collective-permute-done((f32[80,512]{1,0:T(8,128)S(1)}, f32[80,512]{1,0:T(8,128)S(1)}, u32[]{:S(2)}, u32[]{:S(2)}) %collective-permute-start.1) | collective-permute-done | bytes 163872 | tf_op jit(solution)/shard_map/ppermute | solution.py:487
  11.6 0.0 copy-start.1
  11.6 0.0 copy-start.2
  11.6 0.0 copy-start.4
  11.6 0.2 shard_map.94
  11.8 0.0 copy-start
  11.8 4.5 %collective-permute-start.2 = (f32[24,128]{1,0:T(8,128)S(1)}, f32[24,128]{1,0:T(8,128)S(1)}, u32[]{:S(2)}, u32[]{:S(2)}) collective-permute-start(f32[24,128]{1,0:T(8,128)S(1)} %get-tuple-element.20), channel_id=1, source_target_pairs={{0,15},{1,14},{2,13},{3,12},{4,11},{5,10},{6,9},{7,8},{8,7},{9,6},... | collective-permute-start | bytes 36872 | tf_op jit(solution)/shard_map/ppermute | solution.py:487
  16.3 1.4 %collective-permute-done.2.mirror = f32[24,128]{1,0:T(8,128)S(1)} collective-permute-done((f32[24,128]{1,0:T(8,128)S(1)}, f32[24,128]{1,0:T(8,128)S(1)}, u32[]{:S(2)}, u32[]{:S(2)}) %collective-permute-start.2) | collective-permute-done | bytes 12320 | tf_op jit(solution)/shard_map/ppermute | solution.py:487
  17.7 1.5 %shard_map.95 = (f32[144,640]{1,0:T(8,128)S(1)}, f32[8,128]{1,0:T(8,128)S(1)}) custom-call(f32[24,512]{1,0:T(8,128)S(1)} %get-tuple-element.21.forcing, f32[24,512]{1,0:T(8,128)S(1)} %get-tuple-element.22.coded, f32[24,128]{1,0:T(8,128)S(1)} %get-tuple-element.23.tile, f32[24,128]{1,0:T(8,128)S(1)} %collective-permute-done.2.mirror), custom_call_target="tpu_custom_call" | custom-call | bytes 495616 | tf_op jit(solution)/shard_map/pallas_call | solution.py:471
  19.2 0.1 collective-permute-start.3
  19.3 1.1 %collective-permute-done.3 = f32[8,128]{1,0:T(8,128)S(1)} collective-permute-done((f32[8,128]{1,0:T(8,128)S(1)}, f32[8,128]{1,0:T(8,128)S(1)}, u32[]{:S(2)}, u32[]{:S(2)}) %collective-permute-start.3) | collective-permute-done | bytes 4128 | tf_op jit(solution)/shard_map/ppermute | solution.py:487
  20.4 0.2 collective-permute-start.4
  20.6 2.9 %collective-permute-done.4 = f32[16,128]{1,0:T(8,128)S(1)} collective-permute-done((f32[16,128]{1,0:T(8,128)S(1)}, f32[16,128]{1,0:T(8,128)S(1)}, u32[]{:S(2)}, u32[]{:S(2)}) %collective-permute-start.4) | collective-permute-done | bytes 8224 | tf_op jit(solution)/shard_map/ppermute | solution.py:487
  23.5 0.0 collective-permute-start.5
  23.5 3.2 %collective-permute-done.5 = f32[32,128]{1,0:T(8,128)S(1)} collective-permute-done((f32[32,128]{1,0:T(8,128)S(1)}, f32[32,128]{1,0:T(8,128)S(1)}, u32[]{:S(2)}, u32[]{:S(2)}) %collective-permute-start.5) | collective-permute-done | bytes 16416 | tf_op jit(solution)/shard_map/ppermute | solution.py:487
  26.7 0.0 copy-start.3
  26.7 1.8 %collective-permute-start.6 = (f32[64,128]{1,0:T(8,128)S(1)}, f32[64,128]{1,0:T(8,128)S(1)}, u32[]{:S(2)}, u32[]{:S(2)}) collective-permute-start(f32[64,128]{1,0:T(8,128)S(1)} %get-tuple-element.32.after), channel_id=1, source_target_pairs={{0,9},{1,8},{2,11},{3,10},{4,13},{5,12},{6,15},{7,14},{8,1},{9,0},... | collective-permute-start | bytes 98312 | tf_op jit(solution)/shard_map/ppermute | solution.py:487
  28.5 0.0 copy-done.1
  28.5 0.0 copy-done.2
  28.5 0.0 copy-done.4
  28.5 0.0 copy-done
  28.5 0.0 copy-done.3
  28.5 1.2 %shard_map.96 = f32[16,8,512]{2,1,0:T(8,128)} custom-call(f32[16,8,512]{2,1,0:T(8,128)S(1)} %copy-done.2, f32[16,8,512]{2,1,0:T(8,128)S(1)} %copy-done, f32[16,8,512]{2,1,0:T(8,128)S(1)} %copy-done.1, s32[8,512]{1,0:T(8,128)S(1)} %copy-done.3, f32[8,512]{1,0:T(8,128)S(1)} %copy-done.4, f32[80,512]{1,0:T(8,128)S(1)} %collective-permute-done.sibling, ...), custom_call_target="tpu_custom_call" | custom-call | flops 2621440 | bytes 1421312 | tf_op jit(solution)/shard_map/pallas_call | solution.py:471
  29.7 0.6 %shard_map.97 = (f32[16,8,512]{2,1,0:T(8,128)S(1)}, f32[16,8,512]{2,1,0:T(8,128)S(1)}, f32[8,512]{1,0:T(8,128)S(1)}) custom-call(f32[16,8,512]{2,1,0:T(8,128)S(1)} %copy-done, f32[16,8,512]{2,1,0:T(8,128)S(1)} %copy-done.1, s32[8,512]{1,0:T(8,128)S(1)} %copy-done.3, f32[8,512]{1,0:T(8,128)S(1)} %copy-done.4, f32[80,512]{1,0:T(8,128)S(1)} %collective-permute-done.sibling, ...), custom_call_target="tpu_custom_call" | custom-call | flops 2621440 | bytes 1437696 | tf_op jit(solution)/shard_map/pallas_call | solution.py:471
  30.3 0.6 %collective-permute-done.6 = f32[64,128]{1,0:T(8,128)S(1)} collective-permute-done((f32[64,128]{1,0:T(8,128)S(1)}, f32[64,128]{1,0:T(8,128)S(1)}, u32[]{:S(2)}, u32[]{:S(2)}) %collective-permute-start.6) | collective-permute-done | bytes 32800 | tf_op jit(solution)/shard_map/ppermute | solution.py:487
  30.9 1.6 %shard_map.98 = (f32[16,8,512]{2,1,0:T(8,128)}, f32[16,8,512]{2,1,0:T(8,128)}, f32[8,512]{1,0:T(8,128)}) custom-call(f32[128,128]{1,0:T(8,128)S(1)} %constant_dynamic-update-slice_fusion.7.gram, f32[144,640]{1,0:T(8,128)S(1)} %get-tuple-element.25.vectors, f32[16,8,512]{2,1,0:T(8,128)S(1)} %get-tuple-element.26.zonal, ...), custom_call_target="tpu_custom_call" | custom-call | bytes 1515520 | tf_op jit(solution)/shard_map/pallas_call | solution.py:471
  (6 shorter events, 0.0 us)
Async XLA Ops:
  2.4 6.2 %collective-permute-start = (f32[80,512]{1,0:T(8,128)S(1)}, f32[80,512]{1,0:T(8,128)S(1)}, u32[]{:S(2)}, u32[]{:S(2)}) collective-permute-start(f32[80,512]{1,0:T(8,128)S(1)} %get-tuple-element.18.inner), channel_id=1, source_target_pairs={{0,1},{1,0},{2,3},{3,2},{4,5},{5,4},{6,7},{7,6},{8,9},{9,8},{10,11... | collective-permute-start | bytes 491528 | tf_op jit(solution)/shard_map/ppermute | solution.py:487
  2.9 8.7 %collective-permute-start.1 = (f32[80,512]{1,0:T(8,128)S(1)}, f32[80,512]{1,0:T(8,128)S(1)}, u32[]{:S(2)}, u32[]{:S(2)}) collective-permute-start(f32[80,512]{1,0:T(8,128)S(1)} %get-tuple-element.19.outer), channel_id=1, source_target_pairs={{0,15},{1,2},{2,1},{3,4},{4,3},{5,6},{6,5},{7,8},{8,7},{9,10},{10,... | collective-permute-start | bytes 491528 | tf_op jit(solution)/shard_map/ppermute | solution.py:487
  11.6 16.9 %copy-start.1 = (f32[16,8,512]{2,1,0:T(8,128)S(1)}, f32[16,8,512]{2,1,0:T(8,128)}, u32[]{:S(2)}) copy-start(f32[16,8,512]{2,1,0:T(8,128)} %meridional.3) | copy-start | bytes 786436
  11.6 16.9 %copy-start.2 = (f32[16,8,512]{2,1,0:T(8,128)S(1)}, f32[16,8,512]{2,1,0:T(8,128)}, u32[]{:S(2)}) copy-start(f32[16,8,512]{2,1,0:T(8,128)} %tracer.1) | copy-start | bytes 786436
  11.6 16.9 %copy-start.4 = (f32[8,512]{1,0:T(8,128)S(1)}, f32[8,512]{1,0:T(8,128)}, u32[]{:S(2)}) copy-start(f32[8,512]{1,0:T(8,128)} %diffusivity.3) | copy-start | bytes 49156
  11.8 16.7 %copy-start = (f32[16,8,512]{2,1,0:T(8,128)S(1)}, f32[16,8,512]{2,1,0:T(8,128)}, u32[]{:S(2)}) copy-start(f32[16,8,512]{2,1,0:T(8,128)} %zonal.3) | copy-start | bytes 786436
  11.8 5.9 %collective-permute-start.2 = (f32[24,128]{1,0:T(8,128)S(1)}, f32[24,128]{1,0:T(8,128)S(1)}, u32[]{:S(2)}, u32[]{:S(2)}) collective-permute-start(f32[24,128]{1,0:T(8,128)S(1)} %get-tuple-element.20), channel_id=1, source_target_pairs={{0,15},{1,14},{2,13},{3,12},{4,11},{5,10},{6,9},{7,8},{8,7},{9,6},... | collective-permute-start | bytes 36872 | tf_op jit(solution)/shard_map/ppermute | solution.py:487
  19.2 1.2 %collective-permute-start.3 = (f32[8,128]{1,0:T(8,128)S(1)}, f32[8,128]{1,0:T(8,128)S(1)}, u32[]{:S(2)}, u32[]{:S(2)}) collective-permute-start(f32[8,128]{1,0:T(8,128)S(1)} %get-tuple-element.24), channel_id=1, source_target_pairs={{0,1},{1,0},{2,3},{3,2},{4,5},{5,4},{6,7},{7,6},{8,9},{9,8},{10,11... | collective-permute-start | bytes 12296 | tf_op jit(solution)/shard_map/ppermute | solution.py:487
  20.4 3.1 %collective-permute-start.4 = (f32[16,128]{1,0:T(8,128)S(1)}, f32[16,128]{1,0:T(8,128)S(1)}, u32[]{:S(2)}, u32[]{:S(2)}) collective-permute-start(f32[16,128]{1,0:T(8,128)S(1)} %pad_maximum_fusion), channel_id=1, source_target_pairs={{0,3},{1,2},{2,1},{3,0},{4,7},{5,6},{6,5},{7,4},{8,11},{9,10},{10,... | collective-permute-start | bytes 24584 | tf_op jit(solution)/shard_map/ppermute | solution.py:487
  23.5 3.2 %collective-permute-start.5 = (f32[32,128]{1,0:T(8,128)S(1)}, f32[32,128]{1,0:T(8,128)S(1)}, u32[]{:S(2)}, u32[]{:S(2)}) collective-permute-start(f32[32,128]{1,0:T(8,128)S(1)} %get-tuple-element.36.after), channel_id=1, source_target_pairs={{0,5},{1,4},{2,7},{3,6},{4,1},{5,0},{6,3},{7,2},{8,13},{9,12},{10,... | collective-permute-start | bytes 49160 | tf_op jit(solution)/shard_map/ppermute | solution.py:487
  26.7 1.8 %copy-start.3 = (s32[8,512]{1,0:T(8,128)S(1)}, s32[8,512]{1,0:T(8,128)}, u32[]{:S(2)}) copy-start(s32[8,512]{1,0:T(8,128)} %count.3) | copy-start | bytes 49156
  26.7 4.2 %collective-permute-start.6 = (f32[64,128]{1,0:T(8,128)S(1)}, f32[64,128]{1,0:T(8,128)S(1)}, u32[]{:S(2)}, u32[]{:S(2)}) collective-permute-start(f32[64,128]{1,0:T(8,128)S(1)} %get-tuple-element.32.after), channel_id=1, source_target_pairs={{0,9},{1,8},{2,11},{3,10},{4,13},{5,12},{6,15},{7,14},{8,1},{9,0},... | collective-permute-start | bytes 98312 | tf_op jit(solution)/shard_map/ppermute | solution.py:487

commit v3 on v2

--- a/solution.py
+++ b/solution.py
@@ -30,6 +30,7 @@
 LANE_MT = 40
 LANE_MU = 56
 LANE_MV = 72
+LANE_EDGE = 88
 
 f32 = jnp.float32
 
@@ -117,7 +118,7 @@
     tracer, zonal, meridional, count, diffusivity, surface, sems,
 ):
     shape = (COLS, NY)
-    even = lax.axis_index("lon") % 2 == 0
+    even = is_even()
     small = [
         pltpu.make_async_copy(a, b, sems.at[i])
         for i, (a, b) in enumerate(
@@ -201,54 +202,88 @@
     )
 
 
-def halo_kernel(inner, outer, sibling, beyond, forcing, coded, tile, flipped):
-    shape = (EXT, NY)
-    even = lax.axis_index("lon") % 2 == 0
-    flux_in = interface_flux(inner, sibling)
-    flux_out = interface_flux(outer, beyond)
-    row = iota(shape, 0)
-
-    def arrange(at):
-        own = inner[at:at + COLS]
-        east, west = sibling[at:at + COLS], beyond[at:at + COLS]
-        first = jnp.where(even, west, east)
-        last = jnp.where(even, east, west)
-        return jnp.concatenate([first, own, last], axis=0)
-
-    def choose(a, b):
-        return jnp.where(even, a, b)
-
-    west_own = choose(outer[65:66] * flux_out, inner[65:66] * flux_in)
-    west_far = choose(beyond[65:66] * flux_out, sibling[65:66] * flux_in)
-    east_own = choose(inner[65:66] * flux_in, outer[65:66] * flux_out)
-    east_far = choose(sibling[65:66] * flux_in, beyond[65:66] * flux_out)
+def is_even():
+    return lax.axis_index("lon") % 2 == 0
+
+
+def beside(even, west, east):
+    return jnp.concatenate([jnp.where(even, west, east), jnp.where(even, east, west)], axis=0)
+
+
+def chip_kernel(inner, outer, sibling, forcing, coded, tile, flipped):
+    even = is_even()
+    flux = interface_flux(inner, sibling)
+    own, far = inner[65:66] * flux, -sibling[65:66] * flux
+    row = iota((2 * COLS, NY), 0)
     change = jnp.where(
         row == COLS - 1,
-        -west_far,
-        jnp.where(
-            row == COLS,
-            west_own,
-            jnp.where(row == 2 * COLS - 1, east_own, jnp.where(row == 2 * COLS, -east_far, 0.0)),
-        ),
-    )
-    full = arrange(0) + change
-    code = arrange(COLS)
+        jnp.where(even, own, far),
+        jnp.where(row == COLS, jnp.where(even, far, own), 0.0),
+    )
+    full = beside(even, inner[:COLS], sibling[:COLS]) + change
+    code = beside(even, inner[COLS:2 * COLS], sibling[COLS:2 * COLS])
+    fold = beside(even, inner[72:80, :LANES], sibling[72:80, :LANES])
     forcing[...] = full
     coded[...] = code
-    lane = iota((EXT, LANES), 1)
-    fold = arrange(72)[:, :LANES]
+    tile[...] = fold
+    lane = iota((2 * COLS, LANES), 1)
     for j in range(COLS):
         at = NY - 1 - j
         fold = jnp.where(lane == j, full[:, at:at + 1], fold)
         fold = jnp.where(lane == COLS + j, code[:, at:at + 1], fold)
-    tile[...] = fold
-    flipped[...] = jnp.concatenate([fold[EXT - 1 - i:EXT - i] for i in range(EXT)], axis=0)
-
-
-def basis_kernel(forcing, coded, tile, mirror, vectors, gram):
+    fold = jnp.concatenate(
+        [fold[i:i + 1] for i in range(2 * COLS - 1, -1, -1)], axis=0
+    )
+    edge = outer[32:48, NY - LANES:] + outer[48:64, NY - LANES:]
+    for j in range(COLS):
+        at = LANES - 1 - j
+        fold = jnp.where(lane == LANE_EDGE + j, edge[:, at:at + 1], fold)
+        for base, source in ((1, 64), (2, 65)):
+            value = outer[source:source + 1, NY - 1 - j:NY - j]
+            fold = jnp.where(lane == LANE_EDGE + base * COLS + j, value, fold)
+    flipped[...] = fold
+
+
+def across_fold(even, chip, far):
+    shape = (2 * COLS, LANES)
+    level = iota(shape, 0).astype(f32)
+    lane = iota((1, LANES), 1)
+    flux = level_sum(
+        jnp.where(level < roll(chip, -COLS, 1), far, 0.0)
+        - jnp.where(level < roll(far, -COLS, 1), chip, 0.0)
+    )
+
+    def change(tile):
+        return jnp.where(lane < COLS, roll(roll(tile[:1], -2 * COLS, 1) * flux, -LANE_EDGE, 1), 0.0)
+
+    chip_change, far_change = change(chip), -change(far)
+    tile = extend(even, far[COLS:], chip, far[:COLS])
+    row = iota((EXT, LANES), 0)
+    west = jnp.where(row == COLS - 1, far_change, jnp.where(row == COLS, chip_change, 0.0))
+    east = jnp.where(
+        row == 2 * COLS - 1, chip_change, jnp.where(row == 2 * COLS, far_change, 0.0)
+    )
+    return tile + jnp.where(even, west, east)
+
+
+def extend(even, west, chip, east):
+    return jnp.concatenate(
+        [
+            jnp.where(even, west, chip[:COLS]),
+            jnp.where(even, chip[:COLS], chip[COLS:]),
+            jnp.where(even, chip[COLS:], east),
+        ],
+        axis=0,
+    )
+
+
+def basis_kernel(outer, beyond, forcing, coded, tile, mirror, mirror_far, vectors, gram):
     width = NY + LANES
+    even = is_even()
     lane = iota((EXT, LANES), 1)
-    mine, theirs = tile[...], mirror[...]
+    mine = beyond[72:80, :LANES]
+    mine = extend(even, mine, tile[...], mine)
+    theirs = across_fold(even, mirror[...], mirror_far[...])
     level = (lane - LANE_P).astype(f32)
     weight = jnp.where((lane >= LANE_P) & (lane < LANE_P + K), 0.5 * (0.5 + level / K), 0.0)
     mask_mine = (level < mine[:, LANE_LC:LANE_LC + 1]).astype(f32)
@@ -256,12 +291,20 @@
     flux = -jnp.sum(weight * (mask_mine * theirs + mask_theirs * mine), axis=1, keepdims=True)
     own_change = mine[:, LANE_DIFF:LANE_DIFF + 1] * flux
     far_change = theirs[:, LANE_DIFF:LANE_DIFF + 1] * flux
+    flux_out = interface_flux(outer, beyond)
+    own, far = outer[65:66] * flux_out, -beyond[65:66] * flux_out
+    row = iota((EXT, NY), 0)
+    west = jnp.where(row == COLS - 1, far, jnp.where(row == COLS, own, 0.0))
+    east = jnp.where(row == 2 * COLS - 1, own, jnp.where(row == 2 * COLS, far, 0.0))
+    far_forcing, far_code = beyond[:COLS], beyond[COLS:2 * COLS]
+    south = extend(even, far_forcing, forcing[...], far_forcing) + jnp.where(even, west, east)
+    south_code = extend(even, far_code, coded[...], far_code)
     north = jnp.where(lane < COLS, theirs, 0.0)
     north = north + jnp.where(lane == 0, far_change, 0.0)
     body_lane = iota((EXT, NY), 1)
-    south = forcing[...] + jnp.where(body_lane == NY - 1, own_change, 0.0)
+    south = south + jnp.where(body_lane == NY - 1, own_change, 0.0)
     north_code = jnp.where(lane < COLS, roll(theirs, -COLS, 1), -1.0)
-    code = jnp.concatenate([coded[...], north_code], axis=1)
+    code = jnp.concatenate([south_code, north_code], axis=1)
     ocean = code > 0
     centre = jnp.where(ocean, code / scale, 0.0)
     around = jnp.where(ocean, 1.0 / scale, 0.0)
@@ -269,8 +312,8 @@
 
     def operate(q):
         along = roll(q, -1, 1) + jnp.where(wide_lane == 0, 0.0, roll(q, 1, 1))
-        beside = q + corner_weight * along
-        return centre * q - around * (along + roll(beside, 1, 0) + roll(beside, -1, 0))
+        side = q + corner_weight * along
+        return centre * q - around * (along + roll(side, 1, 0) + roll(side, -1, 0))
 
     v = [jnp.concatenate([south, north], axis=1)]
     v.append(operate(v[0]))
@@ -377,10 +420,10 @@
 
 def neighbours(count, sibling, beyond, mirror):
     shape = (COLS, NY)
-    even = lax.axis_index("lon") % 2 == 0
+    even = is_even()
     row, lane = iota(shape, 0), iota(shape, 1)
     lc = count[...].astype(f32)
-    north_tile = mirror[COLS:2 * COLS]
+    north_tile = jnp.where(even, mirror[:COLS], mirror[COLS:])
 
     def around(field, west, east, north):
         return (
@@ -489,6 +532,7 @@
     siblings = [(i, i ^ 1) for i in range(size)]
     outward = [(i, (i + 1 if i % 2 else i - 1) % size) for i in range(size)]
     mirrored = [(i, size - 1 - i) for i in range(size)]
+    mirrored_far = [(i, (size - 2 * (i % 2) - i) % size) for i in range(size)]
     arguments = (tracer, zonal, meridional, count, diffusivity, surface)
     inner, outer = call(
         pack_kernel, [(PACK, NY)] * 2, *arguments,
@@ -497,16 +541,16 @@
     )
     beyond = permute(outer, outward)
     sibling = permute(inner, siblings)
+    chip = (2 * COLS, NY)
     forcing, coded, tile, flipped = call(
-        halo_kernel,
-        [(EXT, NY), (EXT, NY), (EXT, LANES), (EXT, LANES)],
-        inner, outer, sibling, beyond,
+        chip_kernel, [chip, chip, (2 * COLS, LANES), (2 * COLS, LANES)], inner, outer, sibling
     )
     mirror = permute(flipped, mirrored)
+    mirror_far = permute(flipped, mirrored_far)
     vectors, gram = call(
         basis_kernel,
         [(ITERS * EXT, NY + LANES), (COLS, LANES)],
-        forcing, coded, tile, mirror,
+        outer, beyond, forcing, coded, tile, mirror, mirror_far,
     )
     sums = [gram]
     reach = 1

time: 33.2 us -> 32.5 us (0.979); the launches traced: 32.5 us -> 32.2 us
  starting transfers between devices: 12.7 us -> 11.3 us
  local copies, waits for them, and re-layouts: 0.04 us -> 0.64 us
  waiting for transfers between devices: 12.2 us -> 12.6 us
    ppermute x7 -> x8, starting transfers between devices: 12.7 us -> 11.3 us  [permute(): return lax.ppermute(value, 'lon', pairs)]
    unnamed x13, local copies, waits for them, and re-layouts: 0.03 us -> 0.64 us
    ppermute x7 -> x8, waiting for transfers between devices: 12.2 us -> 12.6 us  [permute(): return lax.ppermute(value, 'lon', pairs)]
  transfers between devices with their start and end apart: 7 -> 8, of which waited for: 6 -> 6; matrix products, arithmetic and copies ran while one was open for 0% -> 0% of each run, Pallas kernels for 6% -> 6%
where the time goes in v3:
time: 32.5 us; the launch traced here: 32.2 us
  waiting for transfers between devices  12.6 us (39%)
  starting transfers between devices  11.3 us (35%)
  Pallas kernels  6.99 us (22%)
  between operations  0.71 us (2%)
  local copies, waits for them, and re-layouts  0.64 us (2%)
    ppermute x8, waiting for transfers between devices, permute(): return lax.ppermute(value, 'lon', pairs)  12.6 us
    ppermute x8, starting transfers between devices, permute(): return lax.ppermute(value, 'lon', pairs)  11.3 us
    pallas_call x6, Pallas kernels, call(): pl.pallas_call(kernel, out_shape=[jax.ShapeDtypeStruct(s, f32) for s in s...  6.99 us
  transfers between devices with their start and end apart: 8, of which 6 were waited for; matrix products, arithmetic and copies ran while one was open for 0% of the time, Pallas kernels for 6%

profile of v3, /device:TPU:0, one launch (start us, length us, event | category | flops | bytes accessed | tf_op | source)
XLA Modules:
  0.0 32.2 jit_solution(10746670864011519656)
XLA Ops:
  0.6 1.8 %shard_map.93 = (f32[80,512]{1,0:T(8,128)S(1)}, f32[80,512]{1,0:T(8,128)S(1)}) custom-call(f32[16,8,512]{2,1,0:T(8,128)} %tracer.1, f32[16,8,512]{2,1,0:T(8,128)} %zonal.3, f32[16,8,512]{2,1,0:T(8,128)} %meridional.3, s32[8,512]{1,0:T(8,128)} %count.3, f32[8,512]{1,0:T(8,128)} %diffusivity.3, f32[8,512]{1,0:T(8,128)} %surface_in.1), custom_call_target="tpu_custom_call" | custom-call | bytes 1163264 | tf_op jit(solution)/shard_map/pallas_call | solution.py:514
  2.4 0.5 %collective-permute-start = (f32[80,512]{1,0:T(8,128)S(1)}, f32[80,512]{1,0:T(8,128)S(1)}, u32[]{:S(2)}, u32[]{:S(2)}) collective-permute-start(f32[80,512]{1,0:T(8,128)S(1)} %get-tuple-element.18.inner), channel_id=1, source_target_pairs={{0,1},{1,0},{2,3},{3,2},{4,5},{5,4},{6,7},{7,6},{8,9},{9,8},{10,11... | collective-permute-start | bytes 491528 | tf_op jit(solution)/shard_map/ppermute | solution.py:530
  2.9 5.7 %collective-permute-start.1 = (f32[80,512]{1,0:T(8,128)S(1)}, f32[80,512]{1,0:T(8,128)S(1)}, u32[]{:S(2)}, u32[]{:S(2)}) collective-permute-start(f32[80,512]{1,0:T(8,128)S(1)} %get-tuple-element.19.outer), channel_id=1, source_target_pairs={{0,15},{1,2},{2,1},{3,4},{4,3},{5,6},{6,5},{7,8},{8,7},{9,10},{10,... | collective-permute-start | bytes 491528 | tf_op jit(solution)/shard_map/ppermute | solution.py:530
  8.6 0.0 collective-permute-done.sibling
  8.6 0.0 copy-start.2
  8.6 0.2 shard_map.94
  8.8 0.7 %collective-permute-start.3 = (f32[16,128]{1,0:T(8,128)S(1)}, f32[16,128]{1,0:T(8,128)S(1)}, u32[]{:S(2)}, u32[]{:S(2)}) collective-permute-start(f32[16,128]{1,0:T(8,128)S(1)} %get-tuple-element.20), channel_id=1, source_target_pairs={{0,0},{1,13},{2,14},{3,11},{4,12},{5,9},{6,10},{7,7},{8,8},{9,5},{... | collective-permute-start | bytes 24584 | tf_op jit(solution)/shard_map/ppermute | solution.py:530
  9.4 1.1 %collective-permute-start.2 = (f32[16,128]{1,0:T(8,128)S(1)}, f32[16,128]{1,0:T(8,128)S(1)}, u32[]{:S(2)}, u32[]{:S(2)}) collective-permute-start(f32[16,128]{1,0:T(8,128)S(1)} %get-tuple-element.20), channel_id=1, source_target_pairs={{0,15},{1,14},{2,13},{3,12},{4,11},{5,10},{6,9},{7,8},{8,7},{9,6},... | collective-permute-start | bytes 24584 | tf_op jit(solution)/shard_map/ppermute | solution.py:530
  10.5 1.1 %collective-permute-done.1.beyond = f32[80,512]{1,0:T(8,128)S(1)} collective-permute-done((f32[80,512]{1,0:T(8,128)S(1)}, f32[80,512]{1,0:T(8,128)S(1)}, u32[]{:S(2)}, u32[]{:S(2)}) %collective-permute-start.1) | collective-permute-done | bytes 163872 | tf_op jit(solution)/shard_map/ppermute | solution.py:530
  11.6 0.0 collective-permute-done.3.mirror_far
  11.6 3.7 %collective-permute-done.2.mirror = f32[16,128]{1,0:T(8,128)S(1)} collective-permute-done((f32[16,128]{1,0:T(8,128)S(1)}, f32[16,128]{1,0:T(8,128)S(1)}, u32[]{:S(2)}, u32[]{:S(2)}) %collective-permute-start.2) | collective-permute-done | bytes 8224 | tf_op jit(solution)/shard_map/ppermute | solution.py:530
  15.3 0.0 copy-start
  15.3 0.0 copy-start.1
  15.3 1.6 %shard_map.95 = (f32[144,640]{1,0:T(8,128)S(1)}, f32[8,128]{1,0:T(8,128)S(1)}) custom-call(f32[80,512]{1,0:T(8,128)S(1)} %get-tuple-element.19.outer, f32[80,512]{1,0:T(8,128)S(1)} %collective-permute-done.1.beyond, f32[16,512]{1,0:T(8,128)S(1)} %get-tuple-element.21.forcing, f32[16,512]{1,0:T(8,128)S(1)} %get-tuple-element.22.coded, ...), custom_call_target="tpu_custom_call" | custom-call | bytes 790528 | tf_op jit(solution)/shard_map/pallas_call | solution.py:514
  16.9 1.7 %collective-permute-start.4 = (f32[8,128]{1,0:T(8,128)S(1)}, f32[8,128]{1,0:T(8,128)S(1)}, u32[]{:S(2)}, u32[]{:S(2)}) collective-permute-start(f32[8,128]{1,0:T(8,128)S(1)} %get-tuple-element.24), channel_id=1, source_target_pairs={{0,1},{1,0},{2,3},{3,2},{4,5},{5,4},{6,7},{7,6},{8,9},{9,8},{10,11... | collective-permute-start | bytes 12296 | tf_op jit(solution)/shard_map/ppermute | solution.py:530
  18.6 0.8 %collective-permute-done.4 = f32[8,128]{1,0:T(8,128)S(1)} collective-permute-done((f32[8,128]{1,0:T(8,128)S(1)}, f32[8,128]{1,0:T(8,128)S(1)}, u32[]{:S(2)}, u32[]{:S(2)}) %collective-permute-start.4) | collective-permute-done | bytes 4128 | tf_op jit(solution)/shard_map/ppermute | solution.py:530
  19.4 1.6 %collective-permute-start.5 = (f32[16,128]{1,0:T(8,128)S(1)}, f32[16,128]{1,0:T(8,128)S(1)}, u32[]{:S(2)}, u32[]{:S(2)}) collective-permute-start(f32[16,128]{1,0:T(8,128)S(1)} %pad_maximum_fusion), channel_id=1, source_target_pairs={{0,3},{1,2},{2,1},{3,0},{4,7},{5,6},{6,5},{7,4},{8,11},{9,10},{10,... | collective-permute-start | bytes 24584 | tf_op jit(solution)/shard_map/ppermute | solution.py:530
  21.0 1.5 %collective-permute-done.5 = f32[16,128]{1,0:T(8,128)S(1)} collective-permute-done((f32[16,128]{1,0:T(8,128)S(1)}, f32[16,128]{1,0:T(8,128)S(1)}, u32[]{:S(2)}, u32[]{:S(2)}) %collective-permute-start.5) | collective-permute-done | bytes 8224 | tf_op jit(solution)/shard_map/ppermute | solution.py:530
  22.5 0.0 collective-permute-start.6
  22.5 3.2 %collective-permute-done.6 = f32[32,128]{1,0:T(8,128)S(1)} collective-permute-done((f32[32,128]{1,0:T(8,128)S(1)}, f32[32,128]{1,0:T(8,128)S(1)}, u32[]{:S(2)}, u32[]{:S(2)}) %collective-permute-start.6) | collective-permute-done | bytes 16416 | tf_op jit(solution)/shard_map/ppermute | solution.py:530
  25.7 0.0 copy-start.3
  25.7 0.0 copy-start.4
  25.7 0.1 collective-permute-start.7
  25.8 0.0 copy-done.2
  25.8 0.0 copy-done
  25.8 0.0 copy-done.1
  25.8 0.6 %copy-done.3 = s32[8,512]{1,0:T(8,128)S(1)} copy-done((s32[8,512]{1,0:T(8,128)S(1)}, s32[8,512]{1,0:T(8,128)}, u32[]{:S(2)}) %copy-start.3) | copy-done | bytes 16408
  26.4 0.0 copy-done.4
  26.4 1.2 %shard_map.96 = f32[16,8,512]{2,1,0:T(8,128)} custom-call(f32[16,8,512]{2,1,0:T(8,128)S(1)} %copy-done.2, f32[16,8,512]{2,1,0:T(8,128)S(1)} %copy-done, f32[16,8,512]{2,1,0:T(8,128)S(1)} %copy-done.1, s32[8,512]{1,0:T(8,128)S(1)} %copy-done.3, f32[8,512]{1,0:T(8,128)S(1)} %copy-done.4, f32[80,512]{1,0:T(8,128)S(1)} %collective-permute-done.sibling, ...), custom_call_target="tpu_custom_call" | custom-call | flops 2621440 | bytes 1417216 | tf_op jit(solution)/shard_map/pallas_call | solution.py:514
  27.6 0.6 %shard_map.97 = (f32[16,8,512]{2,1,0:T(8,128)S(1)}, f32[16,8,512]{2,1,0:T(8,128)S(1)}, f32[8,512]{1,0:T(8,128)S(1)}) custom-call(f32[16,8,512]{2,1,0:T(8,128)S(1)} %copy-done, f32[16,8,512]{2,1,0:T(8,128)S(1)} %copy-done.1, s32[8,512]{1,0:T(8,128)S(1)} %copy-done.3, f32[8,512]{1,0:T(8,128)S(1)} %copy-done.4, f32[80,512]{1,0:T(8,128)S(1)} %collective-permute-done.sibling, ...), custom_call_target="tpu_custom_call" | custom-call | flops 2621440 | bytes 1433600 | tf_op jit(solution)/shard_map/pallas_call | solution.py:514
  28.2 2.4 %collective-permute-done.7 = f32[64,128]{1,0:T(8,128)S(1)} collective-permute-done((f32[64,128]{1,0:T(8,128)S(1)}, f32[64,128]{1,0:T(8,128)S(1)}, u32[]{:S(2)}, u32[]{:S(2)}) %collective-permute-start.7) | collective-permute-done | bytes 32800 | tf_op jit(solution)/shard_map/ppermute | solution.py:530
  30.6 1.6 %shard_map.98 = (f32[16,8,512]{2,1,0:T(8,128)}, f32[16,8,512]{2,1,0:T(8,128)}, f32[8,512]{1,0:T(8,128)}) custom-call(f32[128,128]{1,0:T(8,128)S(1)} %constant_dynamic-update-slice_fusion.7.gram, f32[144,640]{1,0:T(8,128)S(1)} %get-tuple-element.25.vectors, f32[16,8,512]{2,1,0:T(8,128)S(1)} %get-tuple-element.26.zonal, ...), custom_call_target="tpu_custom_call" | custom-call | bytes 1515520 | tf_op jit(solution)/shard_map/pallas_call | solution.py:514
  (6 shorter events, 0.0 us)
Async XLA Ops:
  2.4 6.2 %collective-permute-start = (f32[80,512]{1,0:T(8,128)S(1)}, f32[80,512]{1,0:T(8,128)S(1)}, u32[]{:S(2)}, u32[]{:S(2)}) collective-permute-start(f32[80,512]{1,0:T(8,128)S(1)} %get-tuple-element.18.inner), channel_id=1, source_target_pairs={{0,1},{1,0},{2,3},{3,2},{4,5},{5,4},{6,7},{7,6},{8,9},{9,8},{10,11... | collective-permute-start | bytes 491528 | tf_op jit(solution)/shard_map/ppermute | solution.py:530
  2.9 8.7 %collective-permute-start.1 = (f32[80,512]{1,0:T(8,128)S(1)}, f32[80,512]{1,0:T(8,128)S(1)}, u32[]{:S(2)}, u32[]{:S(2)}) collective-permute-start(f32[80,512]{1,0:T(8,128)S(1)} %get-tuple-element.19.outer), channel_id=1, source_target_pairs={{0,15},{1,2},{2,1},{3,4},{4,3},{5,6},{6,5},{7,8},{8,7},{9,10},{10,... | collective-permute-start | bytes 491528 | tf_op jit(solution)/shard_map/ppermute | solution.py:530
  8.6 17.2 %copy-start.2 = (f32[16,8,512]{2,1,0:T(8,128)S(1)}, f32[16,8,512]{2,1,0:T(8,128)}, u32[]{:S(2)}) copy-start(f32[16,8,512]{2,1,0:T(8,128)} %tracer.1) | copy-start | bytes 786436
  8.8 2.8 %collective-permute-start.3 = (f32[16,128]{1,0:T(8,128)S(1)}, f32[16,128]{1,0:T(8,128)S(1)}, u32[]{:S(2)}, u32[]{:S(2)}) collective-permute-start(f32[16,128]{1,0:T(8,128)S(1)} %get-tuple-element.20), channel_id=1, source_target_pairs={{0,0},{1,13},{2,14},{3,11},{4,12},{5,9},{6,10},{7,7},{8,8},{9,5},{... | collective-permute-start | bytes 24584 | tf_op jit(solution)/shard_map/ppermute | solution.py:530
  9.4 5.8 %collective-permute-start.2 = (f32[16,128]{1,0:T(8,128)S(1)}, f32[16,128]{1,0:T(8,128)S(1)}, u32[]{:S(2)}, u32[]{:S(2)}) collective-permute-start(f32[16,128]{1,0:T(8,128)S(1)} %get-tuple-element.20), channel_id=1, source_target_pairs={{0,15},{1,14},{2,13},{3,12},{4,11},{5,10},{6,9},{7,8},{8,7},{9,6},... | collective-permute-start | bytes 24584 | tf_op jit(solution)/shard_map/ppermute | solution.py:530
  15.3 10.5 %copy-start = (f32[16,8,512]{2,1,0:T(8,128)S(1)}, f32[16,8,512]{2,1,0:T(8,128)}, u32[]{:S(2)}) copy-start(f32[16,8,512]{2,1,0:T(8,128)} %zonal.3) | copy-start | bytes 786436
  15.3 10.5 %copy-start.1 = (f32[16,8,512]{2,1,0:T(8,128)S(1)}, f32[16,8,512]{2,1,0:T(8,128)}, u32[]{:S(2)}) copy-start(f32[16,8,512]{2,1,0:T(8,128)} %meridional.3) | copy-start | bytes 786436
  16.9 2.5 %collective-permute-start.4 = (f32[8,128]{1,0:T(8,128)S(1)}, f32[8,128]{1,0:T(8,128)S(1)}, u32[]{:S(2)}, u32[]{:S(2)}) collective-permute-start(f32[8,128]{1,0:T(8,128)S(1)} %get-tuple-element.24), channel_id=1, source_target_pairs={{0,1},{1,0},{2,3},{3,2},{4,5},{5,4},{6,7},{7,6},{8,9},{9,8},{10,11... | collective-permute-start | bytes 12296 | tf_op jit(solution)/shard_map/ppermute | solution.py:530
  19.4 3.1 %collective-permute-start.5 = (f32[16,128]{1,0:T(8,128)S(1)}, f32[16,128]{1,0:T(8,128)S(1)}, u32[]{:S(2)}, u32[]{:S(2)}) collective-permute-start(f32[16,128]{1,0:T(8,128)S(1)} %pad_maximum_fusion), channel_id=1, source_target_pairs={{0,3},{1,2},{2,1},{3,0},{4,7},{5,6},{6,5},{7,4},{8,11},{9,10},{10,... | collective-permute-start | bytes 24584 | tf_op jit(solution)/shard_map/ppermute | solution.py:530
  22.5 3.2 %collective-permute-start.6 = (f32[32,128]{1,0:T(8,128)S(1)}, f32[32,128]{1,0:T(8,128)S(1)}, u32[]{:S(2)}, u32[]{:S(2)}) collective-permute-start(f32[32,128]{1,0:T(8,128)S(1)} %get-tuple-element.36.after), channel_id=1, source_target_pairs={{0,5},{1,4},{2,7},{3,6},{4,1},{5,0},{6,3},{7,2},{8,13},{9,12},{10,... | collective-permute-start | bytes 49160 | tf_op jit(solution)/shard_map/ppermute | solution.py:530
  25.7 0.7 %copy-start.3 = (s32[8,512]{1,0:T(8,128)S(1)}, s32[8,512]{1,0:T(8,128)}, u32[]{:S(2)}) copy-start(s32[8,512]{1,0:T(8,128)} %count.3) | copy-start | bytes 49156
  25.7 0.7 %copy-start.4 = (f32[8,512]{1,0:T(8,128)S(1)}, f32[8,512]{1,0:T(8,128)}, u32[]{:S(2)}) copy-start(f32[8,512]{1,0:T(8,128)} %diffusivity.3) | copy-start | bytes 49156
  25.7 4.9 %collective-permute-start.7 = (f32[64,128]{1,0:T(8,128)S(1)}, f32[64,128]{1,0:T(8,128)S(1)}, u32[]{:S(2)}, u32[]{:S(2)}) collective-permute-start(f32[64,128]{1,0:T(8,128)S(1)} %get-tuple-element.32.after), channel_id=1, source_target_pairs={{0,9},{1,8},{2,11},{3,10},{4,13},{5,12},{6,15},{7,14},{8,1},{9,0},... | collective-permute-start | bytes 98312 | tf_op jit(solution)/shard_map/ppermute | solution.py:530

commit v4 on v3

--- a/solution.py
+++ b/solution.py
@@ -182,14 +182,26 @@
         flux_x - west_flux + flux_y - south_flux
     )
     coded = jnp.where(lc > 0, surface[...], -1.0)
-    zeros = jnp.zeros((COLS, NY - LANES), f32)
+    edge = jnp.zeros((K, LANES), f32)
+    edge_lane = iota((K, LANES), 1)
+    p = outer[32:48, NY - LANES:] + outer[48:64, NY - LANES:]
+    edge_lc = jnp.where(even, lc[:1], lc[COLS - 1:])
+    edge_diff = jnp.where(even, diff[:1], diff[COLS - 1:])
+    for j in range(COLS):
+        at = NY - 1 - j
+        here = LANE_EDGE + j
+        edge = jnp.where(edge_lane == here, p[:, LANES - 1 - j:LANES - j], edge)
+        edge = jnp.where(edge_lane == here + COLS, edge_lc[:, at:at + 1], edge)
+        edge = jnp.where(edge_lane == here + 2 * COLS, edge_diff[:, at:at + 1], edge)
+    edge = [edge[:COLS], edge[COLS:]]
+    zeros = jnp.zeros((COLS, NY - 3 * LANES), f32)
     for pack, mine, other in ((inner, COLS - 1, 0), (outer, 0, COLS - 1)):
         pack[0:COLS] = forcing
         pack[COLS:2 * COLS] = coded
         edge_lc = jnp.where(even, lc[mine:mine + 1], lc[other:other + 1])
         edge_diff = jnp.where(even, diff[mine:mine + 1], diff[other:other + 1])
         pack[64:72] = jnp.where(row == 0, edge_lc, jnp.where(row == 1, edge_diff, 0.0))
-        pack[72:80] = jnp.concatenate([fold, zeros], axis=1)
+        pack[72:80] = jnp.concatenate([fold, *edge, zeros], axis=1)
 
 
 def interface_flux(mine, theirs):
@@ -210,15 +222,15 @@
     return jnp.concatenate([jnp.where(even, west, east), jnp.where(even, east, west)], axis=0)
 
 
-def chip_kernel(inner, outer, sibling, forcing, coded, tile, flipped):
+def chip_kernel(inner, sibling, forcing, coded, tile, near, far):
     even = is_even()
     flux = interface_flux(inner, sibling)
-    own, far = inner[65:66] * flux, -sibling[65:66] * flux
+    own, other = inner[65:66] * flux, -sibling[65:66] * flux
     row = iota((2 * COLS, NY), 0)
     change = jnp.where(
         row == COLS - 1,
-        jnp.where(even, own, far),
-        jnp.where(row == COLS, jnp.where(even, far, own), 0.0),
+        jnp.where(even, own, other),
+        jnp.where(row == COLS, jnp.where(even, other, own), 0.0),
     )
     full = beside(even, inner[:COLS], sibling[:COLS]) + change
     code = beside(even, inner[COLS:2 * COLS], sibling[COLS:2 * COLS])
@@ -234,14 +246,11 @@
     fold = jnp.concatenate(
         [fold[i:i + 1] for i in range(2 * COLS - 1, -1, -1)], axis=0
     )
-    edge = outer[32:48, NY - LANES:] + outer[48:64, NY - LANES:]
-    for j in range(COLS):
-        at = LANES - 1 - j
-        fold = jnp.where(lane == LANE_EDGE + j, edge[:, at:at + 1], fold)
-        for base, source in ((1, 64), (2, 65)):
-            value = outer[source:source + 1, NY - 1 - j:NY - j]
-            fold = jnp.where(lane == LANE_EDGE + base * COLS + j, value, fold)
-    flipped[...] = fold
+    for out, source in ((near, inner), (far, sibling)):
+        edge = jnp.concatenate(
+            [source[72:80, LANES:2 * LANES], source[72:80, 2 * LANES:3 * LANES]], axis=0
+        )
+        out[...] = jnp.where(lane >= LANE_EDGE, edge, fold)
 
 
 def across_fold(even, chip, far):
@@ -342,19 +351,25 @@
         while step:
             column = pair_add(column, (roll(column[0], step, 1), roll(column[1], step, 1)))
             step //= 2
-        column = pair_norm(column)
-        out = jnp.where(tile_lane == i, column[0], out)
-        out = jnp.where(tile_lane == LANES // 2 + i, column[1], out)
-    gram[...] = out
+        for part, base in zip(pair_norm(column), (0, LANES // 2)):
+            out = jnp.where(tile_lane - (base + i * COLS) == sub, part, out)
+    gram[...] = jnp.sum(out, axis=0, keepdims=True)
 
 
 def coefficients(gram):
     shape = (COLS, LANES)
     tiles = [gram[i * COLS:(i + 1) * COLS] for i in range(gram.shape[0] // COLS)]
-    total = pair_norm(pair_tree([(t, roll(t, LANES // 2, 1)) for t in tiles]))
+    total = pair_norm(pair_rows(pair_tree([(t, roll(t, LANES // 2, 1)) for t in tiles])))
     wide = lambda column: jnp.broadcast_to(column, shape)
-    matrix = [tuple(wide(part[:, j:j + 1]) for part in total) for j in range(BASIS)]
     sub = iota(shape, 0)
+    entry = iota(shape, 1) - sub
+    matrix = [
+        tuple(
+            wide(jnp.sum(jnp.where(entry == j * COLS, part, 0.0), axis=1, keepdims=True))
+            for part in total
+        )
+        for j in range(BASIS)
+    ]
     first = (sub == 0).astype(f32)
     zero = jnp.zeros(shape, f32)
 
@@ -532,7 +547,7 @@
     siblings = [(i, i ^ 1) for i in range(size)]
     outward = [(i, (i + 1 if i % 2 else i - 1) % size) for i in range(size)]
     mirrored = [(i, size - 1 - i) for i in range(size)]
-    mirrored_far = [(i, (size - 2 * (i % 2) - i) % size) for i in range(size)]
+    mirrored_far = [((size + 1 - 4 * (i % 2) - i) % size, i) for i in range(size)]
     arguments = (tracer, zonal, meridional, count, diffusivity, surface)
     inner, outer = call(
         pack_kernel, [(PACK, NY)] * 2, *arguments,
@@ -542,36 +557,39 @@
     beyond = permute(outer, outward)
     sibling = permute(inner, siblings)
     chip = (2 * COLS, NY)
-    forcing, coded, tile, flipped = call(
-        chip_kernel, [chip, chip, (2 * COLS, LANES), (2 * COLS, LANES)], inner, outer, sibling
-    )
-    mirror = permute(flipped, mirrored)
-    mirror_far = permute(flipped, mirrored_far)
+    forcing, coded, tile, near, far = call(
+        chip_kernel, [chip, chip] + [(2 * COLS, LANES)] * 3, inner, sibling
+    )
+    mirror = permute(near, mirrored)
+    mirror_far = permute(far, mirrored_far)
     vectors, gram = call(
         basis_kernel,
-        [(ITERS * EXT, NY + LANES), (COLS, LANES)],
+        [(ITERS * EXT, NY + LANES), (1, LANES)],
         outer, beyond, forcing, coded, tile, mirror, mirror_far,
     )
-    sums = [gram]
+    halos = (sibling, beyond, mirror)
     reach = 1
+    tracer_next = None
     while reach < size:
-        other = permute(sums[-1], [(i, i ^ (reach ^ 1 if reach > 1 else 1)) for i in range(size)])
-        sums.append(jnp.concatenate([sums[-1], other], axis=0))
+        if 8 * reach >= size and tracer_next is None and reach > 1:
+            tracer_next, = call(
+                tracer_kernel, [block],
+                tracer, zonal, meridional, count, diffusivity, *halos,
+                flops=65536 * 40, after=gram,
+            )
+        other = permute(gram, [(i, i ^ (reach ^ 1 if reach > 1 else 1)) for i in range(size)])
+        gram = jnp.concatenate([gram, other], axis=0)
         reach *= 2
-    halos = (sibling, beyond, mirror)
-    tracer_next, = call(
-        tracer_kernel, [block],
-        tracer, zonal, meridional, count, diffusivity, *halos,
-        flops=65536 * 40, after=sums[min(2, len(sums) - 1)],
-    )
-    zonal_step, meridional_step, levels = call(
-        flow_kernel, [block, block, (COLS, NY)],
-        zonal, meridional, count, diffusivity, *halos,
-        flops=65536 * 40, after=sums[min(3, len(sums) - 1)],
-    )
+        if 2 * reach == size:
+            gram, tracer_next = lax.optimization_barrier((gram, tracer_next))
+            zonal_step, meridional_step, levels = call(
+                flow_kernel, [block, block, (COLS, NY)],
+                zonal, meridional, count, diffusivity, *halos,
+                flops=65536 * 40, after=gram,
+            )
     zonal_next, meridional_next, height = call(
         finish_kernel, [block, block, (COLS, NY)],
-        sums[-1], vectors, zonal_step, meridional_step, levels,
+        gram, vectors, zonal_step, meridional_step, levels,
     )
     return tracer_next, zonal_next, meridional_next, height
 

time: 32.5 us -> 29.6 us (0.911)
  starting transfers between devices: 11.3 us -> 8.6 us
  local copies, waits for them, and re-layouts: 0.64 us -> 0.02 us
  waiting for transfers between devices: 12.6 us -> 13 us
    ppermute x8, starting transfers between devices: 11.3 us -> 8.6 us  [permute(): return lax.ppermute(value, 'lon', pairs)]
    unnamed x13 -> x10, local copies, waits for them, and re-layouts: 0.64 us -> 0.02 us
    ppermute x8, waiting for transfers between devices: 12.6 us -> 13 us  [permute(): return lax.ppermute(value, 'lon', pairs)]
  transfers between devices with their start and end apart: 8 -> 8, of which waited for: 6 -> 6; matrix products, arithmetic and copies ran while one was open for 0% -> 0% of each run, Pallas kernels for 6% -> 7%
where the time goes in v4:
time: 29.6 us; the launch traced here: 29.4 us
  waiting for transfers between devices  13 us (44%)
  starting transfers between devices  8.6 us (29%)
  Pallas kernels  7.02 us (24%)
  between operations  0.74 us (2%)
    ppermute x8, waiting for transfers between devices, permute(): return lax.ppermute(value, 'lon', pairs)  13 us
    ppermute x8, starting transfers between devices, permute(): return lax.ppermute(value, 'lon', pairs)  8.6 us
    pallas_call x6, Pallas kernels, call(): pl.pallas_call(kernel, out_shape=[jax.ShapeDtypeStruct(s, f32) for s in s...  7.02 us
  transfers between devices with their start and end apart: 8, of which 6 were waited for; matrix products, arithmetic and copies ran while one was open for 0% of the time, Pallas kernels for 7%

profile of v4, /device:TPU:0, one launch (start us, length us, event | category | flops | bytes accessed | tf_op | source)
XLA Modules:
  0.0 29.4 jit_solution(9356709053853988134)
XLA Ops:
  0.6 0.0 copy-start.2
  0.6 1.8 %shard_map.93 = (f32[80,512]{1,0:T(8,128)S(1)}, f32[80,512]{1,0:T(8,128)S(1)}) custom-call(f32[16,8,512]{2,1,0:T(8,128)} %tracer.1, f32[16,8,512]{2,1,0:T(8,128)} %zonal.3, f32[16,8,512]{2,1,0:T(8,128)} %meridional.3, s32[8,512]{1,0:T(8,128)} %count.3, f32[8,512]{1,0:T(8,128)} %diffusivity.3, f32[8,512]{1,0:T(8,128)} %surface_in.1), custom_call_target="tpu_custom_call" | custom-call | bytes 1163264 | tf_op jit(solution)/shard_map/pallas_call | solution.py:529
  2.5 0.5 %collective-permute-start.1 = (f32[80,512]{1,0:T(8,128)S(1)}, f32[80,512]{1,0:T(8,128)S(1)}, u32[]{:S(2)}, u32[]{:S(2)}) collective-permute-start(f32[80,512]{1,0:T(8,128)S(1)} %get-tuple-element.22.inner), channel_id=1, source_target_pairs={{0,1},{1,0},{2,3},{3,2},{4,5},{5,4},{6,7},{7,6},{8,9},{9,8},{10,11... | collective-permute-start | bytes 491528 | tf_op jit(solution)/shard_map/ppermute | solution.py:545
  3.0 5.7 %collective-permute-start = (f32[80,512]{1,0:T(8,128)S(1)}, f32[80,512]{1,0:T(8,128)S(1)}, u32[]{:S(2)}, u32[]{:S(2)}) collective-permute-start(f32[80,512]{1,0:T(8,128)S(1)} %get-tuple-element.21.outer), channel_id=1, source_target_pairs={{0,15},{1,2},{2,1},{3,4},{4,3},{5,6},{6,5},{7,8},{8,7},{9,10},{10,... | collective-permute-start | bytes 491528 | tf_op jit(solution)/shard_map/ppermute | solution.py:545
  8.6 0.0 collective-permute-done.1.sibling
  8.6 0.0 copy-start.1
  8.6 0.1 shard_map.94
  8.8 0.0 copy-start
  8.8 1.1 %collective-permute-start.2 = (f32[16,128]{1,0:T(8,128)S(1)}, f32[16,128]{1,0:T(8,128)S(1)}, u32[]{:S(2)}, u32[]{:S(2)}) collective-permute-start(f32[16,128]{1,0:T(8,128)S(1)} %get-tuple-element.26), channel_id=1, source_target_pairs={{0,15},{1,14},{2,13},{3,12},{4,11},{5,10},{6,9},{7,8},{8,7},{9,6},... | collective-permute-start | bytes 24584 | tf_op jit(solution)/shard_map/ppermute | solution.py:545
  9.9 0.2 collective-permute-start.3
  10.1 1.7 %collective-permute-done.beyond = f32[80,512]{1,0:T(8,128)S(1)} collective-permute-done((f32[80,512]{1,0:T(8,128)S(1)}, f32[80,512]{1,0:T(8,128)S(1)}, u32[]{:S(2)}, u32[]{:S(2)}) %collective-permute-start) | collective-permute-done | bytes 163872 | tf_op jit(solution)/shard_map/ppermute | solution.py:545
  11.7 2.9 %collective-permute-done.2.mirror = f32[16,128]{1,0:T(8,128)S(1)} collective-permute-done((f32[16,128]{1,0:T(8,128)S(1)}, f32[16,128]{1,0:T(8,128)S(1)}, u32[]{:S(2)}, u32[]{:S(2)}) %collective-permute-start.2) | collective-permute-done | bytes 8224 | tf_op jit(solution)/shard_map/ppermute | solution.py:545
  14.6 0.0 collective-permute-done.3.mirror_far
  14.6 0.0 copy-start.3
  14.6 0.0 copy-start.4
  14.6 1.6 %shard_map.95 = (f32[144,640]{1,0:T(8,128)S(1)}, f32[1,128]{1,0:T(1,128)S(1)}) custom-call(f32[80,512]{1,0:T(8,128)S(1)} %get-tuple-element.21.outer, f32[80,512]{1,0:T(8,128)S(1)} %collective-permute-done.beyond, f32[16,512]{1,0:T(8,128)S(1)} %get-tuple-element.23.forcing, f32[16,512]{1,0:T(8,128)S(1)} %get-tuple-element.24.coded, ...), custom_call_target="tpu_custom_call" | custom-call | bytes 786944 | tf_op jit(solution)/shard_map/pallas_call | solution.py:529
  16.3 0.6 %collective-permute-start.4 = (f32[1,128]{1,0:T(1,128)S(1)}, f32[1,128]{1,0:T(1,128)S(1)}, u32[]{:S(2)}, u32[]{:S(2)}) collective-permute-start(f32[1,128]{1,0:T(1,128)S(1)} %get-tuple-element.28), channel_id=1, source_target_pairs={{0,1},{1,0},{2,3},{3,2},{4,5},{5,4},{6,7},{7,6},{8,9},{9,8},{10,11... | collective-permute-start | bytes 1544 | tf_op jit(solution)/shard_map/ppermute | solution.py:545
  16.8 0.8 %collective-permute-done.4 = f32[1,128]{1,0:T(1,128)S(1)} collective-permute-done((f32[1,128]{1,0:T(1,128)S(1)}, f32[1,128]{1,0:T(1,128)S(1)}, u32[]{:S(2)}, u32[]{:S(2)}) %collective-permute-start.4) | collective-permute-done | bytes 544 | tf_op jit(solution)/shard_map/ppermute | solution.py:545
  17.7 0.4 %collective-permute-start.5 = (f32[2,128]{1,0:T(2,128)S(1)}, f32[2,128]{1,0:T(2,128)S(1)}, u32[]{:S(2)}, u32[]{:S(2)}) collective-permute-start(f32[2,128]{1,0:T(2,128)S(1)} %pad_maximum_fusion.3.after), channel_id=1, source_target_pairs={{0,3},{1,2},{2,1},{3,0},{4,7},{5,6},{6,5},{7,4},{8,11},{9,10},{10,... | collective-permute-start | bytes 3080 | tf_op jit(solution)/shard_map/ppermute | solution.py:545
  18.1 2.6 %collective-permute-done.5 = f32[2,128]{1,0:T(2,128)S(1)} collective-permute-done((f32[2,128]{1,0:T(2,128)S(1)}, f32[2,128]{1,0:T(2,128)S(1)}, u32[]{:S(2)}, u32[]{:S(2)}) %collective-permute-start.5) | collective-permute-done | bytes 1056 | tf_op jit(solution)/shard_map/ppermute | solution.py:545
  20.7 0.1 collective-permute-start.6
  20.8 0.0 copy-done.2
  20.8 0.0 copy-done.1
  20.8 0.0 copy-done
  20.8 0.0 copy-done.3
  20.8 0.0 copy-done.4
  20.8 1.2 %shard_map.96 = f32[16,8,512]{2,1,0:T(8,128)} custom-call(f32[16,8,512]{2,1,0:T(8,128)S(1)} %copy-done.2, f32[16,8,512]{2,1,0:T(8,128)S(1)} %copy-done, f32[16,8,512]{2,1,0:T(8,128)S(1)} %copy-done.1, s32[8,512]{1,0:T(8,128)S(1)} %copy-done.3, f32[8,512]{1,0:T(8,128)S(1)} %copy-done.4, f32[80,512]{1,0:T(8,128)S(1)} %collective-permute-done.1.sibling, ...), custom_call_target="tpu_custom_call" | custom-call | flops 2621440 | bytes 1417216 | tf_op jit(solution)/shard_map/pallas_call | solution.py:529
  22.0 1.8 %collective-permute-done.6 = f32[4,128]{1,0:T(4,128)S(1)} collective-permute-done((f32[4,128]{1,0:T(4,128)S(1)}, f32[4,128]{1,0:T(4,128)S(1)}, u32[]{:S(2)}, u32[]{:S(2)}) %collective-permute-start.6) | collective-permute-done | bytes 2080 | tf_op jit(solution)/shard_map/ppermute | solution.py:545
  23.8 0.1 collective-permute-start.7
  23.8 0.6 %shard_map.97 = (f32[16,8,512]{2,1,0:T(8,128)S(1)}, f32[16,8,512]{2,1,0:T(8,128)S(1)}, f32[8,512]{1,0:T(8,128)S(1)}) custom-call(f32[16,8,512]{2,1,0:T(8,128)S(1)} %copy-done, f32[16,8,512]{2,1,0:T(8,128)S(1)} %copy-done.1, s32[8,512]{1,0:T(8,128)S(1)} %copy-done.3, f32[8,512]{1,0:T(8,128)S(1)} %copy-done.4, f32[80,512]{1,0:T(8,128)S(1)} %collective-permute-done.1.sibling, ...), custom_call_target="tpu_custom_call" | custom-call | flops 2621440 | bytes 1433600 | tf_op jit(solution)/shard_map/pallas_call | solution.py:529
  24.5 3.3 %collective-permute-done.7 = f32[8,128]{1,0:T(8,128)S(1)} collective-permute-done((f32[8,128]{1,0:T(8,128)S(1)}, f32[8,128]{1,0:T(8,128)S(1)}, u32[]{:S(2)}, u32[]{:S(2)}) %collective-permute-start.7) | collective-permute-done | bytes 4128 | tf_op jit(solution)/shard_map/ppermute | solution.py:545
  27.8 1.6 %shard_map.98 = (f32[16,8,512]{2,1,0:T(8,128)}, f32[16,8,512]{2,1,0:T(8,128)}, f32[8,512]{1,0:T(8,128)}) custom-call(f32[16,128]{1,0:T(8,128)S(1)} %pad_maximum_fusion.gram, f32[144,640]{1,0:T(8,128)S(1)} %get-tuple-element.31.vectors, f32[16,8,512]{2,1,0:T(8,128)S(1)} %get-tuple-element.32.zonal, f32[16,8,512]{2,1,0:T(8,128)S(1)} %get-tuple-element.33.meridional, ...), custom_call_target="tpu_custom_call" | custom-call | bytes 1458176 | tf_op jit(solution)/shard_map/pallas_call | solution.py:529
  (4 shorter events, 0.0 us)
Async XLA Ops:
  0.6 20.1 %copy-start.2 = (f32[16,8,512]{2,1,0:T(8,128)S(1)}, f32[16,8,512]{2,1,0:T(8,128)}, u32[]{:S(2)}) copy-start(f32[16,8,512]{2,1,0:T(8,128)} %tracer.1) | copy-start | bytes 786436
  2.5 6.2 %collective-permute-start.1 = (f32[80,512]{1,0:T(8,128)S(1)}, f32[80,512]{1,0:T(8,128)S(1)}, u32[]{:S(2)}, u32[]{:S(2)}) collective-permute-start(f32[80,512]{1,0:T(8,128)S(1)} %get-tuple-element.22.inner), channel_id=1, source_target_pairs={{0,1},{1,0},{2,3},{3,2},{4,5},{5,4},{6,7},{7,6},{8,9},{9,8},{10,11... | collective-permute-start | bytes 491528 | tf_op jit(solution)/shard_map/ppermute | solution.py:545
  3.0 8.8 %collective-permute-start = (f32[80,512]{1,0:T(8,128)S(1)}, f32[80,512]{1,0:T(8,128)S(1)}, u32[]{:S(2)}, u32[]{:S(2)}) collective-permute-start(f32[80,512]{1,0:T(8,128)S(1)} %get-tuple-element.21.outer), channel_id=1, source_target_pairs={{0,15},{1,2},{2,1},{3,4},{4,3},{5,6},{6,5},{7,8},{8,7},{9,10},{10,... | collective-permute-start | bytes 491528 | tf_op jit(solution)/shard_map/ppermute | solution.py:545
  8.6 12.1 %copy-start.1 = (f32[16,8,512]{2,1,0:T(8,128)S(1)}, f32[16,8,512]{2,1,0:T(8,128)}, u32[]{:S(2)}) copy-start(f32[16,8,512]{2,1,0:T(8,128)} %meridional.3) | copy-start | bytes 786436
  8.8 12.0 %copy-start = (f32[16,8,512]{2,1,0:T(8,128)S(1)}, f32[16,8,512]{2,1,0:T(8,128)}, u32[]{:S(2)}) copy-start(f32[16,8,512]{2,1,0:T(8,128)} %zonal.3) | copy-start | bytes 786436
  8.8 5.8 %collective-permute-start.2 = (f32[16,128]{1,0:T(8,128)S(1)}, f32[16,128]{1,0:T(8,128)S(1)}, u32[]{:S(2)}, u32[]{:S(2)}) collective-permute-start(f32[16,128]{1,0:T(8,128)S(1)} %get-tuple-element.26), channel_id=1, source_target_pairs={{0,15},{1,14},{2,13},{3,12},{4,11},{5,10},{6,9},{7,8},{8,7},{9,6},... | collective-permute-start | bytes 24584 | tf_op jit(solution)/shard_map/ppermute | solution.py:545
  9.9 4.8 %collective-permute-start.3 = (f32[16,128]{1,0:T(8,128)S(1)}, f32[16,128]{1,0:T(8,128)S(1)}, u32[]{:S(2)}, u32[]{:S(2)}) collective-permute-start(f32[16,128]{1,0:T(8,128)S(1)} %get-tuple-element.27), channel_id=1, source_target_pairs={{1,0},{12,1},{15,2},{10,3},{13,4},{8,5},{11,6},{6,7},{9,8},{4,9},{... | collective-permute-start | bytes 24584 | tf_op jit(solution)/shard_map/ppermute | solution.py:545
  14.6 6.2 %copy-start.3 = (s32[8,512]{1,0:T(8,128)S(1)}, s32[8,512]{1,0:T(8,128)}, u32[]{:S(2)}) copy-start(s32[8,512]{1,0:T(8,128)} %count.3) | copy-start | bytes 49156
  14.6 6.2 %copy-start.4 = (f32[8,512]{1,0:T(8,128)S(1)}, f32[8,512]{1,0:T(8,128)}, u32[]{:S(2)}) copy-start(f32[8,512]{1,0:T(8,128)} %diffusivity.3) | copy-start | bytes 49156
  16.3 1.4 %collective-permute-start.4 = (f32[1,128]{1,0:T(1,128)S(1)}, f32[1,128]{1,0:T(1,128)S(1)}, u32[]{:S(2)}, u32[]{:S(2)}) collective-permute-start(f32[1,128]{1,0:T(1,128)S(1)} %get-tuple-element.28), channel_id=1, source_target_pairs={{0,1},{1,0},{2,3},{3,2},{4,5},{5,4},{6,7},{7,6},{8,9},{9,8},{10,11... | collective-permute-start | bytes 1544 | tf_op jit(solution)/shard_map/ppermute | solution.py:545
  17.7 3.0 %collective-permute-start.5 = (f32[2,128]{1,0:T(2,128)S(1)}, f32[2,128]{1,0:T(2,128)S(1)}, u32[]{:S(2)}, u32[]{:S(2)}) collective-permute-start(f32[2,128]{1,0:T(2,128)S(1)} %pad_maximum_fusion.3.after), channel_id=1, source_target_pairs={{0,3},{1,2},{2,1},{3,0},{4,7},{5,6},{6,5},{7,4},{8,11},{9,10},{10,... | collective-permute-start | bytes 3080 | tf_op jit(solution)/shard_map/ppermute | solution.py:545
  20.7 3.1 %collective-permute-start.6 = (f32[4,128]{1,0:T(4,128)S(1)}, f32[4,128]{1,0:T(4,128)S(1)}, u32[]{:S(2)}, u32[]{:S(2)}) collective-permute-start(f32[4,128]{1,0:T(4,128)S(1)} %pad_maximum_fusion.2), channel_id=1, source_target_pairs={{0,5},{1,4},{2,7},{3,6},{4,1},{5,0},{6,3},{7,2},{8,13},{9,12},{10,... | collective-permute-start | bytes 6152 | tf_op jit(solution)/shard_map/ppermute | solution.py:545
  23.8 4.0 %collective-permute-start.7 = (f32[8,128]{1,0:T(8,128)S(1)}, f32[8,128]{1,0:T(8,128)S(1)}, u32[]{:S(2)}, u32[]{:S(2)}) collective-permute-start(f32[8,128]{1,0:T(8,128)S(1)} %pad_maximum_fusion.1.after), channel_id=1, source_target_pairs={{0,9},{1,8},{2,11},{3,10},{4,13},{5,12},{6,15},{7,14},{8,1},{9,0},... | collective-permute-start | bytes 12296 | tf_op jit(solution)/shard_map/ppermute | solution.py:545

commit v5 on v4

--- a/solution.py
+++ b/solution.py
@@ -15,7 +15,9 @@
 LANES = 128
 PACK = 80
 BASIS = ITERS + 1
-CHUNKS = 4
+NEAR = 384
+GROUPS = (BASIS * (BASIS + 1) // 2 + COLS - 1) // COLS
+CHUNKS = 2
 
 vertical_mix = 0.1
 advection = 0.25
@@ -113,9 +115,27 @@
     return a
 
 
+def pair_pack(terms):
+    shape = (COLS, LANES)
+    sub = iota(shape, 0)
+    zero = (jnp.zeros(shape, f32),) * 2
+    terms = terms + [zero] * (COLS - len(terms))
+    for step in (4, 2, 1):
+        low = (sub & step) == 0
+        merged = []
+        for x, y in zip(terms[:step], terms[step:]):
+            a = tuple(jnp.where(low, p, q) for p, q in zip(x, y))
+            b = tuple(
+                jnp.where(low, roll(p, -step, 0), roll(q, step, 0)) for p, q in zip(x, y)
+            )
+            merged.append(pair_add(a, b))
+        terms = merged
+    return terms[0]
+
+
 def pack_kernel(
     tracer_in, zonal_in, meridional_in, count_in, diffusivity_in, surface_in, inner, outer,
-    tracer, zonal, meridional, count, diffusivity, surface, sems,
+    tracer, zonal, meridional, count, diffusivity, surface, edges, sems,
 ):
     shape = (COLS, NY)
     even = is_even()
@@ -136,7 +156,14 @@
                 )
             ]
         )
-    for copy in small + sum(large, []):
+    rows = [
+        pltpu.make_async_copy(
+            field.at[:, x], edges.at[2 * base + i], sems.at[3 + 3 * CHUNKS + 2 * base + i]
+        )
+        for base, field in enumerate((tracer_in, zonal_in, meridional_in))
+        for i, x in enumerate((0, COLS - 1))
+    ]
+    for copy in small + sum(large, []) + rows:
         copy.start()
     for copy in small:
         copy.wait()
@@ -144,36 +171,45 @@
     diff = diffusivity[...]
     row, lane = iota(shape, 0), iota(shape, 1)
     tile_lane = iota((COLS, LANES), 1)
+    lc_east, lc_north = roll(lc, -1, 0), roll(lc, -1, 1)
     total = jnp.zeros(shape, f32)
     turn = jnp.zeros(shape, f32)
     flux_x = jnp.zeros(shape, f32)
     flux_y = jnp.zeros(shape, f32)
     fold = jnp.zeros((COLS, LANES), f32)
-
-    def put(tile, at, column):
-        return jnp.where(tile_lane == at, column, tile)
-
     for k in range(K):
         if k % (K // CHUNKS) == 0:
             for copy in large[k // (K // CHUNKS)]:
                 copy.wait()
-        mask = (lc > k).astype(f32)
-        u, v = zonal[k], meridional[k]
-        mt, mu, mv = mask * tracer[k], mask * u, mask * v
-        p = mu + mv
-        total += thickness(k) * p
+        mask = lc > k
+        t, u, v = tracer[k], zonal[k], meridional[k]
+        for base, field in ((LANE_MT, t), (LANE_MU, u), (LANE_MV, v)):
+            fold = jnp.where(tile_lane == base + k, field[:, NY - 1:], fold)
+        mu, mv = jnp.where(mask, u, 0.0), jnp.where(mask, v, 0.0)
+        p = thickness(k) * (mu + mv)
+        total += p
         turn += thickness(k) * (mv - mu)
-        flux_x += thickness(k) * (mask * roll(p, -1, 0) - roll(mask, -1, 0) * p)
-        flux_y += thickness(k) * (mask * roll(p, -1, 1) - roll(mask, -1, 1) * p)
-        fold = put(fold, LANE_P + k, p[:, NY - 1:])
-        for base, field in ((0, mt), (1, mu), (2, mv)):
-            west, east = field[:1], field[COLS - 1:]
-            at = 2 * COLS + base * K + k
-            inner[at:at + 1] = jnp.where(even, east, west)
-            outer[at:at + 1] = jnp.where(even, west, east)
-            fold = put(fold, LANE_MT + base * K + k, field[:, NY - 1:])
-    fold = put(fold, LANE_LC, lc[:, NY - 1:])
-    fold = put(fold, LANE_DIFF, diff[:, NY - 1:])
+        flux_x += jnp.where(mask, roll(p, -1, 0), 0.0) - jnp.where(lc_east > k, p, 0.0)
+        flux_y += jnp.where(mask, roll(p, -1, 1), 0.0) - jnp.where(lc_north > k, p, 0.0)
+    lc_fold = lc[:, NY - 1:]
+    level = tile_lane - jnp.where(
+        tile_lane < LANE_MU, LANE_MT, jnp.where(tile_lane < LANE_MV, LANE_MU, LANE_MV)
+    )
+    fold = jnp.where(level.astype(f32) < lc_fold, fold, 0.0)
+    momentum = roll(fold, LANE_P - LANE_MU, 1) + roll(fold, LANE_P - LANE_MV, 1)
+    fold = jnp.where((tile_lane >= LANE_P) & (tile_lane < LANE_P + K), momentum, fold)
+    fold = jnp.where(tile_lane == LANE_LC, lc_fold, fold)
+    fold = jnp.where(tile_lane == LANE_DIFF, diff[:, NY - 1:], fold)
+    edge_level = iota((K, NY), 0).astype(f32)
+    for copy in rows:
+        copy.wait()
+    for base in range(3):
+        west, east = edges[2 * base], edges[2 * base + 1]
+        west = jnp.where(edge_level < lc[:1], west, 0.0)
+        east = jnp.where(edge_level < lc[COLS - 1:], east, 0.0)
+        at = pl.ds(2 * COLS + base * K, K)
+        inner[at] = jnp.where(even, east, west)
+        outer[at] = jnp.where(even, west, east)
     flux_x = jnp.where(row == COLS - 1, 0.0, flux_x)
     flux_y = jnp.where(lane == NY - 1, 0.0, flux_y)
     west_flux = jnp.where(row == 0, 0.0, roll(flux_x, 1, 0))
@@ -286,8 +322,58 @@
     )
 
 
-def basis_kernel(outer, beyond, forcing, coded, tile, mirror, mirror_far, vectors, gram):
-    width = NY + LANES
+def basis(start, code):
+    ocean = code > 0
+    centre = jnp.where(ocean, code / scale, 0.0)
+    around = jnp.where(ocean, 1.0 / scale, 0.0)
+    lane = iota(start.shape, 1)
+
+    def operate(q):
+        along = roll(q, -1, 1) + jnp.where(lane == 0, 0.0, roll(q, 1, 1))
+        side = q + corner_weight * along
+        return centre * q - around * (along + roll(side, 1, 0) + roll(side, -1, 0))
+
+    v = [start, operate(start)]
+    for j in range(2, BASIS):
+        v.append(2.0 * operate(v[-1]) - v[-2])
+    return v
+
+
+def gram_rows(v, blocks):
+    own = [[q[COLS:2 * COLS, c * LANES:(c + 1) * LANES] for c in blocks] for q in v]
+    parts = [[split(q) for q in row] for row in own]
+    entries = []
+    for i in range(BASIS):
+        for j in range(i, BASIS):
+            terms = [
+                two_prod(own[i][c], own[j][c], parts[i][c], parts[j][c])
+                for c in range(len(blocks))
+            ]
+            entries.append(pair_tree(terms))
+    return [pair_pack(entries[g:g + COLS]) for g in range(0, len(entries), COLS)]
+
+
+def inner_kernel(outer, beyond, forcing, coded, last, last_code, vectors, partial):
+    even = is_even()
+    flux_out = interface_flux(outer, beyond)
+    own, far = outer[65:66] * flux_out, -beyond[65:66] * flux_out
+    row = iota((EXT, NY), 0)
+    west = jnp.where(row == COLS - 1, far, jnp.where(row == COLS, own, 0.0))
+    east = jnp.where(row == 2 * COLS - 1, own, jnp.where(row == 2 * COLS, far, 0.0))
+    far_forcing, far_code = beyond[:COLS], beyond[COLS:2 * COLS]
+    south = extend(even, far_forcing, forcing[...], far_forcing) + jnp.where(even, west, east)
+    code = extend(even, far_code, coded[...], far_code)
+    last[...] = south[:, NEAR - LANES:]
+    last_code[...] = code[:, NEAR - LANES:]
+    v = basis(south, code)
+    for j in range(ITERS):
+        vectors[j * EXT:(j + 1) * EXT] = v[j][:, :NEAR]
+    for g, pair in enumerate(gram_rows(v, range(NEAR // LANES))):
+        for at, part in zip((0, GROUPS * COLS), pair):
+            partial[at + g * COLS:at + (g + 1) * COLS] = part
+
+
+def fold_kernel(last, last_code, beyond, tile, mirror, mirror_far, partial, vectors, gram):
     even = is_even()
     lane = iota((EXT, LANES), 1)
     mine = beyond[72:80, :LANES]
@@ -300,76 +386,49 @@
     flux = -jnp.sum(weight * (mask_mine * theirs + mask_theirs * mine), axis=1, keepdims=True)
     own_change = mine[:, LANE_DIFF:LANE_DIFF + 1] * flux
     far_change = theirs[:, LANE_DIFF:LANE_DIFF + 1] * flux
-    flux_out = interface_flux(outer, beyond)
-    own, far = outer[65:66] * flux_out, -beyond[65:66] * flux_out
-    row = iota((EXT, NY), 0)
-    west = jnp.where(row == COLS - 1, far, jnp.where(row == COLS, own, 0.0))
-    east = jnp.where(row == 2 * COLS - 1, own, jnp.where(row == 2 * COLS, far, 0.0))
-    far_forcing, far_code = beyond[:COLS], beyond[COLS:2 * COLS]
-    south = extend(even, far_forcing, forcing[...], far_forcing) + jnp.where(even, west, east)
-    south_code = extend(even, far_code, coded[...], far_code)
     north = jnp.where(lane < COLS, theirs, 0.0)
     north = north + jnp.where(lane == 0, far_change, 0.0)
-    body_lane = iota((EXT, NY), 1)
-    south = south + jnp.where(body_lane == NY - 1, own_change, 0.0)
+    width = NY - NEAR + LANES
+    south = last[...] + jnp.where(iota((EXT, width), 1) == width - 1, own_change, 0.0)
     north_code = jnp.where(lane < COLS, roll(theirs, -COLS, 1), -1.0)
-    code = jnp.concatenate([south_code, north_code], axis=1)
-    ocean = code > 0
-    centre = jnp.where(ocean, code / scale, 0.0)
-    around = jnp.where(ocean, 1.0 / scale, 0.0)
-    wide_lane = iota((EXT, width), 1)
-
-    def operate(q):
-        along = roll(q, -1, 1) + jnp.where(wide_lane == 0, 0.0, roll(q, 1, 1))
-        side = q + corner_weight * along
-        return centre * q - around * (along + roll(side, 1, 0) + roll(side, -1, 0))
-
-    v = [jnp.concatenate([south, north], axis=1)]
-    v.append(operate(v[0]))
-    for j in range(2, BASIS):
-        v.append(2.0 * operate(v[-1]) - v[-2])
+    v = basis(
+        jnp.concatenate([south, north], axis=1),
+        jnp.concatenate([last_code[...], north_code], axis=1),
+    )
     for j in range(ITERS):
-        vectors[j * EXT:(j + 1) * EXT] = v[j]
-    own = [[q[COLS:2 * COLS, c * LANES:(c + 1) * LANES] for c in range(NY // LANES)] for q in v]
-    parts = [[split(q) for q in row] for row in own]
+        vectors[j * EXT:(j + 1) * EXT] = v[j][:, LANES:]
     sub = iota((COLS, LANES), 0)
     tile_lane = iota((COLS, LANES), 1)
-    sums = {}
-    for i in range(BASIS):
-        for j in range(i, BASIS):
-            terms = [
-                two_prod(own[i][c], own[j][c], parts[i][c], parts[j][c])
-                for c in range(NY // LANES)
-            ]
-            sums[i, j] = sums[j, i] = pair_rows(pair_tree(terms))
     out = jnp.zeros((COLS, LANES), f32)
-    for i in range(BASIS):
-        column = (jnp.zeros((COLS, LANES), f32), jnp.zeros((COLS, LANES), f32))
-        for j in range(BASIS):
-            column = tuple(jnp.where(sub == j, s, c) for s, c in zip(sums[i, j], column))
+    for g, pair in enumerate(gram_rows(v, range(1, width // LANES))):
+        at, low = g * COLS, (GROUPS + g) * COLS
+        pair = pair_add(pair, (partial[at:at + COLS], partial[low:low + COLS]))
         step = LANES // 2
         while step:
-            column = pair_add(column, (roll(column[0], step, 1), roll(column[1], step, 1)))
+            pair = pair_add(pair, tuple(roll(part, step, 1) for part in pair))
             step //= 2
-        for part, base in zip(pair_norm(column), (0, LANES // 2)):
-            out = jnp.where(tile_lane - (base + i * COLS) == sub, part, out)
+        for part, base in zip(pair_norm(pair), (at, low)):
+            out = jnp.where(tile_lane - base == sub, part, out)
     gram[...] = jnp.sum(out, axis=0, keepdims=True)
 
 
 def coefficients(gram):
     shape = (COLS, LANES)
     tiles = [gram[i * COLS:(i + 1) * COLS] for i in range(gram.shape[0] // COLS)]
-    total = pair_norm(pair_rows(pair_tree([(t, roll(t, LANES // 2, 1)) for t in tiles])))
+    total = pair_norm(pair_rows(pair_tree([(t, roll(t, -GROUPS * COLS, 1)) for t in tiles])))
     wide = lambda column: jnp.broadcast_to(column, shape)
     sub = iota(shape, 0)
-    entry = iota(shape, 1) - sub
-    matrix = [
-        tuple(
-            wide(jnp.sum(jnp.where(entry == j * COLS, part, 0.0), axis=1, keepdims=True))
-            for part in total
+    tile_lane = iota(shape, 1)
+
+    def column(j):
+        low, high = jnp.minimum(sub, j), jnp.maximum(sub, j)
+        entry = ((low * (2 * BASIS - 1 - low)) >> 1) + high
+        here = (tile_lane == entry) & (sub < BASIS)
+        return tuple(
+            wide(jnp.sum(jnp.where(here, part, 0.0), axis=1, keepdims=True)) for part in total
         )
-        for j in range(BASIS)
-    ]
+
+    matrix = [column(j) for j in range(BASIS)]
     first = (sub == 0).astype(f32)
     zero = jnp.zeros(shape, f32)
 
@@ -379,14 +438,14 @@
         up = [jnp.where(sub == 1, 2.0 * part, part) for part in up]
         down = [half * jnp.where(sub == COLS - 1, 0.0, roll(part, -1, 0)) for part in b]
         four = tuple(4.0 * part for part in b)
-        return pair_norm(pair_add(pair_add(four, b), pair_add(tuple(up), tuple(down))))
+        return pair_add(pair_add(four, b), pair_add(tuple(up), tuple(down)))
 
     def times(vector, count):
         terms = []
         for j in range(count):
             at = tuple(wide(part[j:j + 1]) for part in vector)
             terms.append(pair_mul(matrix[j], at))
-        return pair_norm(pair_tree(terms))
+        return pair_tree(terms)
 
     def dot(a, b):
         s = pair_rows(pair_mul(a, b))
@@ -418,11 +477,15 @@
     return solution
 
 
-def finish_kernel(gram, vectors, zonal, meridional, levels, zonal_next, meridional_next, height):
+def finish_kernel(
+    gram, vectors, vectors_last, zonal, meridional, levels, zonal_next, meridional_next, height
+):
     x = coefficients(gram)
-    total = jnp.zeros((EXT, NY + LANES), f32)
-    for j in range(ITERS):
-        total += x[j:j + 1, :1] * vectors[j * EXT:(j + 1) * EXT]
+    total = []
+    for part in (vectors, vectors_last):
+        at = [x[j:j + 1, :1] * part[j * EXT:(j + 1) * EXT] for j in range(ITERS)]
+        total.append(sum(at[1:], at[0]))
+    total = jnp.concatenate(total, axis=1)
     own = total[COLS:2 * COLS, :NY]
     height[...] = own
     east = gravity * (roll(total, -1, 0)[COLS:2 * COLS, :NY] - own)
@@ -552,7 +615,7 @@
     inner, outer = call(
         pack_kernel, [(PACK, NY)] * 2, *arguments,
         scratch=[pltpu.VMEM(a.shape, a.dtype) for a in arguments]
-        + [pltpu.SemaphoreType.DMA((3 + 3 * CHUNKS,))], stay=len(arguments),
+        + [pltpu.VMEM((6, K, NY), f32), pltpu.SemaphoreType.DMA((9 + 3 * CHUNKS,))], stay=len(arguments),
     )
     beyond = permute(outer, outward)
     sibling = permute(inner, siblings)
@@ -562,10 +625,16 @@
     )
     mirror = permute(near, mirrored)
     mirror_far = permute(far, mirrored_far)
-    vectors, gram = call(
-        basis_kernel,
-        [(ITERS * EXT, NY + LANES), (1, LANES)],
-        outer, beyond, forcing, coded, tile, mirror, mirror_far,
+    last_rows = (EXT, NY - NEAR + LANES)
+    last, last_code, vectors, partial = call(
+        inner_kernel,
+        [last_rows, last_rows, (ITERS * EXT, NEAR), (2 * GROUPS * COLS, LANES)],
+        outer, beyond, forcing, coded, flops=8192 * 100,
+    )
+    vectors_last, gram = call(
+        fold_kernel,
+        [(ITERS * EXT, NY - NEAR + LANES), (1, LANES)],
+        last, last_code, beyond, tile, mirror, mirror_far, partial,
     )
     halos = (sibling, beyond, mirror)
     reach = 1
@@ -589,7 +658,7 @@
             )
     zonal_next, meridional_next, height = call(
         finish_kernel, [block, block, (COLS, NY)],
-        gram, vectors, zonal_step, meridional_step, levels,
+        gram, vectors, vectors_last, zonal_step, meridional_step, levels,
     )
     return tracer_next, zonal_next, meridional_next, height
 

time: 29.6 us -> 29.3 us (0.990)
  waiting for transfers between devices: 13 us -> 12.3 us
  Pallas kernels: 7.02 us -> 7.41 us
    ppermute x8, waiting for transfers between devices: 13 us -> 12.3 us  [permute(): return lax.ppermute(value, 'lon', pairs)]
    pallas_call x6 -> x7, Pallas kernels: 7.02 us -> 7.41 us  [call(): pl.pallas_call(kernel, out_shape=[jax.ShapeDtypeStruct(s, f32) for s in s...]
  transfers between devices with their start and end apart: 8 -> 8, of which waited for: 6 -> 6; matrix products, arithmetic and copies ran while one was open for 0% -> 0% of each run, Pallas kernels for 7% -> 9%
where the time goes in v5:
time: 29.3 us; the launch traced here: 29 us
  waiting for transfers between devices  12.3 us (42%)
  starting transfers between devices  8.59 us (29%)
  Pallas kernels  7.41 us (25%)
  between operations  0.73 us (2%)
    ppermute x8, waiting for transfers between devices, permute(): return lax.ppermute(value, 'lon', pairs)  12.3 us
    ppermute x8, starting transfers between devices, permute(): return lax.ppermute(value, 'lon', pairs)  8.59 us
    pallas_call x7, Pallas kernels, call(): pl.pallas_call(kernel, out_shape=[jax.ShapeDtypeStruct(s, f32) for s in s...  7.41 us
  transfers between devices with their start and end apart: 8, of which 6 were waited for; matrix products, arithmetic and copies ran while one was open for 0% of the time, Pallas kernels for 9%

profile of v5, /device:TPU:0, one launch (start us, length us, event | category | flops | bytes accessed | tf_op | source)
XLA Modules:
  0.0 29.0 jit_solution(14494786728492210287)
XLA Ops:
  0.6 1.7 %shard_map.93 = (f32[80,512]{1,0:T(8,128)S(1)}, f32[80,512]{1,0:T(8,128)S(1)}) custom-call(f32[16,8,512]{2,1,0:T(8,128)} %tracer.1, f32[16,8,512]{2,1,0:T(8,128)} %zonal.3, f32[16,8,512]{2,1,0:T(8,128)} %meridional.3, s32[8,512]{1,0:T(8,128)} %count.3, f32[8,512]{1,0:T(8,128)} %diffusivity.3, f32[8,512]{1,0:T(8,128)} %surface_in.1), custom_call_target="tpu_custom_call" | custom-call | bytes 1163264 | tf_op jit(solution)/shard_map/pallas_call | solution.py:592
  2.3 0.5 %collective-permute-start.1 = (f32[80,512]{1,0:T(8,128)S(1)}, f32[80,512]{1,0:T(8,128)S(1)}, u32[]{:S(2)}, u32[]{:S(2)}) collective-permute-start(f32[80,512]{1,0:T(8,128)S(1)} %get-tuple-element.26.inner), channel_id=1, source_target_pairs={{0,1},{1,0},{2,3},{3,2},{4,5},{5,4},{6,7},{7,6},{8,9},{9,8},{10,11... | collective-permute-start | bytes 491528 | tf_op jit(solution)/shard_map/ppermute | solution.py:608
  2.8 5.7 %collective-permute-start = (f32[80,512]{1,0:T(8,128)S(1)}, f32[80,512]{1,0:T(8,128)S(1)}, u32[]{:S(2)}, u32[]{:S(2)}) collective-permute-start(f32[80,512]{1,0:T(8,128)S(1)} %get-tuple-element.25.outer), channel_id=1, source_target_pairs={{0,15},{1,2},{2,1},{3,4},{4,3},{5,6},{6,5},{7,8},{8,7},{9,10},{10,... | collective-permute-start | bytes 491528 | tf_op jit(solution)/shard_map/ppermute | solution.py:608
  8.5 0.0 collective-permute-done.1.sibling
  8.5 0.0 copy-start.2
  8.5 0.1 shard_map.94
  8.7 1.1 %collective-permute-start.2 = (f32[16,128]{1,0:T(8,128)S(1)}, f32[16,128]{1,0:T(8,128)S(1)}, u32[]{:S(2)}, u32[]{:S(2)}) collective-permute-start(f32[16,128]{1,0:T(8,128)S(1)} %get-tuple-element.32), channel_id=1, source_target_pairs={{0,15},{1,14},{2,13},{3,12},{4,11},{5,10},{6,9},{7,8},{8,7},{9,6},... | collective-permute-start | bytes 24584 | tf_op jit(solution)/shard_map/ppermute | solution.py:608
  9.7 0.2 collective-permute-start.3
  9.9 1.7 %collective-permute-done.beyond = f32[80,512]{1,0:T(8,128)S(1)} collective-permute-done((f32[80,512]{1,0:T(8,128)S(1)}, f32[80,512]{1,0:T(8,128)S(1)}, u32[]{:S(2)}, u32[]{:S(2)}) %collective-permute-start) | collective-permute-done | bytes 163872 | tf_op jit(solution)/shard_map/ppermute | solution.py:608
  11.6 0.0 copy-start
  11.6 0.0 copy-start.1
  11.6 0.7 %shard_map.95 = (f32[24,256]{1,0:T(8,128)S(1)}, f32[24,256]{1,0:T(8,128)S(1)}, f32[144,384]{1,0:T(8,128)S(1)}, f32[64,128]{1,0:T(8,128)S(1)}) custom-call(f32[80,512]{1,0:T(8,128)S(1)} %get-tuple-element.25.outer, f32[80,512]{1,0:T(8,128)S(1)} %collective-permute-done.beyond, f32[16,512]{1,0:T(8,128)S(1)} %get-tuple-element.27.forcing, ...), custom_call_target="tpu_custom_call" | custom-call | flops 819200 | bytes 696320 | tf_op jit(solution)/shard_map/pallas_call | solution.py:592
  12.4 2.1 %collective-permute-done.2.mirror = f32[16,128]{1,0:T(8,128)S(1)} collective-permute-done((f32[16,128]{1,0:T(8,128)S(1)}, f32[16,128]{1,0:T(8,128)S(1)}, u32[]{:S(2)}, u32[]{:S(2)}) %collective-permute-start.2) | collective-permute-done | bytes 8224 | tf_op jit(solution)/shard_map/ppermute | solution.py:608
  14.5 0.0 collective-permute-done.3.mirror_far
  14.5 0.0 copy-start.3
  14.5 0.0 copy-start.4
  14.5 1.5 %shard_map.96 = (f32[144,256]{1,0:T(8,128)S(1)}, f32[1,128]{1,0:T(1,128)S(1)}) custom-call(f32[24,256]{1,0:T(8,128)S(1)} %get-tuple-element.29.last, f32[24,256]{1,0:T(8,128)S(1)} %get-tuple-element.30.last_code, f32[80,512]{1,0:T(8,128)S(1)} %collective-permute-done.beyond, f32[16,128]{1,0:T(8,128)S(1)} %get-tuple-element.31.tile, ...), custom_call_target="tpu_custom_call" | custom-call | bytes 418304 | tf_op jit(solution)/shard_map/pallas_call | solution.py:592
  16.0 0.6 %collective-permute-start.4 = (f32[1,128]{1,0:T(1,128)S(1)}, f32[1,128]{1,0:T(1,128)S(1)}, u32[]{:S(2)}, u32[]{:S(2)}) collective-permute-start(f32[1,128]{1,0:T(1,128)S(1)} %get-tuple-element.35), channel_id=1, source_target_pairs={{0,1},{1,0},{2,3},{3,2},{4,5},{5,4},{6,7},{7,6},{8,9},{9,8},{10,11... | collective-permute-start | bytes 1544 | tf_op jit(solution)/shard_map/ppermute | solution.py:608
  16.5 0.8 %collective-permute-done.4 = f32[1,128]{1,0:T(1,128)S(1)} collective-permute-done((f32[1,128]{1,0:T(1,128)S(1)}, f32[1,128]{1,0:T(1,128)S(1)}, u32[]{:S(2)}, u32[]{:S(2)}) %collective-permute-start.4) | collective-permute-done | bytes 544 | tf_op jit(solution)/shard_map/ppermute | solution.py:608
  17.4 0.4 %collective-permute-start.5 = (f32[2,128]{1,0:T(2,128)S(1)}, f32[2,128]{1,0:T(2,128)S(1)}, u32[]{:S(2)}, u32[]{:S(2)}) collective-permute-start(f32[2,128]{1,0:T(2,128)S(1)} %pad_maximum_fusion.3.after), channel_id=1, source_target_pairs={{0,3},{1,2},{2,1},{3,0},{4,7},{5,6},{6,5},{7,4},{8,11},{9,10},{10,... | collective-permute-start | bytes 3080 | tf_op jit(solution)/shard_map/ppermute | solution.py:608
  17.8 2.6 %collective-permute-done.5 = f32[2,128]{1,0:T(2,128)S(1)} collective-permute-done((f32[2,128]{1,0:T(2,128)S(1)}, f32[2,128]{1,0:T(2,128)S(1)}, u32[]{:S(2)}, u32[]{:S(2)}) %collective-permute-start.5) | collective-permute-done | bytes 1056 | tf_op jit(solution)/shard_map/ppermute | solution.py:608
  20.4 0.1 collective-permute-start.6
  20.5 0.0 copy-done.2
  20.5 0.0 copy-done
  20.5 0.0 copy-done.1
  20.5 0.0 copy-done.3
  20.5 0.0 copy-done.4
  20.5 1.2 %shard_map.97 = f32[16,8,512]{2,1,0:T(8,128)} custom-call(f32[16,8,512]{2,1,0:T(8,128)S(1)} %copy-done.2, f32[16,8,512]{2,1,0:T(8,128)S(1)} %copy-done, f32[16,8,512]{2,1,0:T(8,128)S(1)} %copy-done.1, s32[8,512]{1,0:T(8,128)S(1)} %copy-done.3, f32[8,512]{1,0:T(8,128)S(1)} %copy-done.4, f32[80,512]{1,0:T(8,128)S(1)} %collective-permute-done.1.sibling, ...), custom_call_target="tpu_custom_call" | custom-call | flops 2621440 | bytes 1417216 | tf_op jit(solution)/shard_map/pallas_call | solution.py:592
  21.7 1.8 %collective-permute-done.6 = f32[4,128]{1,0:T(4,128)S(1)} collective-permute-done((f32[4,128]{1,0:T(4,128)S(1)}, f32[4,128]{1,0:T(4,128)S(1)}, u32[]{:S(2)}, u32[]{:S(2)}) %collective-permute-start.6) | collective-permute-done | bytes 2080 | tf_op jit(solution)/shard_map/ppermute | solution.py:608
  23.5 0.1 collective-permute-start.7
  23.5 0.6 %shard_map.98 = (f32[16,8,512]{2,1,0:T(8,128)S(1)}, f32[16,8,512]{2,1,0:T(8,128)S(1)}, f32[8,512]{1,0:T(8,128)S(1)}) custom-call(f32[16,8,512]{2,1,0:T(8,128)S(1)} %copy-done, f32[16,8,512]{2,1,0:T(8,128)S(1)} %copy-done.1, s32[8,512]{1,0:T(8,128)S(1)} %copy-done.3, f32[8,512]{1,0:T(8,128)S(1)} %copy-done.4, f32[80,512]{1,0:T(8,128)S(1)} %collective-permute-done.1.sibling, ...), custom_call_target="tpu_custom_call" | custom-call | flops 2621440 | bytes 1433600 | tf_op jit(solution)/shard_map/pallas_call | solution.py:592
  24.2 3.3 %collective-permute-done.7 = f32[8,128]{1,0:T(8,128)S(1)} collective-permute-done((f32[8,128]{1,0:T(8,128)S(1)}, f32[8,128]{1,0:T(8,128)S(1)}, u32[]{:S(2)}, u32[]{:S(2)}) %collective-permute-start.7) | collective-permute-done | bytes 4128 | tf_op jit(solution)/shard_map/ppermute | solution.py:608
  27.5 1.6 %shard_map.99 = (f32[16,8,512]{2,1,0:T(8,128)}, f32[16,8,512]{2,1,0:T(8,128)}, f32[8,512]{1,0:T(8,128)}) custom-call(f32[16,128]{1,0:T(8,128)S(1)} %pad_maximum_fusion.gram, f32[144,384]{1,0:T(8,128)S(1)} %get-tuple-element.38.vectors, f32[144,256]{1,0:T(8,128)S(1)} %get-tuple-element.39.vectors_last, f32[16,8,512]{2,1,0:T(8,128)S(1)} %get-tuple-element.40.zonal, ...), custom_call_target="tpu_custom_call" | custom-call | bytes 1458176 | tf_op jit(solution)/shard_map/pallas_call | solution.py:592
  (4 shorter events, 0.0 us)
Async XLA Ops:
  2.3 6.2 %collective-permute-start.1 = (f32[80,512]{1,0:T(8,128)S(1)}, f32[80,512]{1,0:T(8,128)S(1)}, u32[]{:S(2)}, u32[]{:S(2)}) collective-permute-start(f32[80,512]{1,0:T(8,128)S(1)} %get-tuple-element.26.inner), channel_id=1, source_target_pairs={{0,1},{1,0},{2,3},{3,2},{4,5},{5,4},{6,7},{7,6},{8,9},{9,8},{10,11... | collective-permute-start | bytes 491528 | tf_op jit(solution)/shard_map/ppermute | solution.py:608
  2.8 8.8 %collective-permute-start = (f32[80,512]{1,0:T(8,128)S(1)}, f32[80,512]{1,0:T(8,128)S(1)}, u32[]{:S(2)}, u32[]{:S(2)}) collective-permute-start(f32[80,512]{1,0:T(8,128)S(1)} %get-tuple-element.25.outer), channel_id=1, source_target_pairs={{0,15},{1,2},{2,1},{3,4},{4,3},{5,6},{6,5},{7,8},{8,7},{9,10},{10,... | collective-permute-start | bytes 491528 | tf_op jit(solution)/shard_map/ppermute | solution.py:608
  8.5 11.9 %copy-start.2 = (f32[16,8,512]{2,1,0:T(8,128)S(1)}, f32[16,8,512]{2,1,0:T(8,128)}, u32[]{:S(2)}) copy-start(f32[16,8,512]{2,1,0:T(8,128)} %tracer.1) | copy-start | bytes 786436
  8.7 5.8 %collective-permute-start.2 = (f32[16,128]{1,0:T(8,128)S(1)}, f32[16,128]{1,0:T(8,128)S(1)}, u32[]{:S(2)}, u32[]{:S(2)}) collective-permute-start(f32[16,128]{1,0:T(8,128)S(1)} %get-tuple-element.32), channel_id=1, source_target_pairs={{0,15},{1,14},{2,13},{3,12},{4,11},{5,10},{6,9},{7,8},{8,7},{9,6},... | collective-permute-start | bytes 24584 | tf_op jit(solution)/shard_map/ppermute | solution.py:608
  9.7 4.8 %collective-permute-start.3 = (f32[16,128]{1,0:T(8,128)S(1)}, f32[16,128]{1,0:T(8,128)S(1)}, u32[]{:S(2)}, u32[]{:S(2)}) collective-permute-start(f32[16,128]{1,0:T(8,128)S(1)} %get-tuple-element.33), channel_id=1, source_target_pairs={{1,0},{12,1},{15,2},{10,3},{13,4},{8,5},{11,6},{6,7},{9,8},{4,9},{... | collective-permute-start | bytes 24584 | tf_op jit(solution)/shard_map/ppermute | solution.py:608
  11.6 8.9 %copy-start = (f32[16,8,512]{2,1,0:T(8,128)S(1)}, f32[16,8,512]{2,1,0:T(8,128)}, u32[]{:S(2)}) copy-start(f32[16,8,512]{2,1,0:T(8,128)} %zonal.3) | copy-start | bytes 786436
  11.6 8.9 %copy-start.1 = (f32[16,8,512]{2,1,0:T(8,128)S(1)}, f32[16,8,512]{2,1,0:T(8,128)}, u32[]{:S(2)}) copy-start(f32[16,8,512]{2,1,0:T(8,128)} %meridional.3) | copy-start | bytes 786436
  14.5 6.0 %copy-start.3 = (s32[8,512]{1,0:T(8,128)S(1)}, s32[8,512]{1,0:T(8,128)}, u32[]{:S(2)}) copy-start(s32[8,512]{1,0:T(8,128)} %count.3) | copy-start | bytes 49156
  14.5 6.0 %copy-start.4 = (f32[8,512]{1,0:T(8,128)S(1)}, f32[8,512]{1,0:T(8,128)}, u32[]{:S(2)}) copy-start(f32[8,512]{1,0:T(8,128)} %diffusivity.3) | copy-start | bytes 49156
  16.0 1.4 %collective-permute-start.4 = (f32[1,128]{1,0:T(1,128)S(1)}, f32[1,128]{1,0:T(1,128)S(1)}, u32[]{:S(2)}, u32[]{:S(2)}) collective-permute-start(f32[1,128]{1,0:T(1,128)S(1)} %get-tuple-element.35), channel_id=1, source_target_pairs={{0,1},{1,0},{2,3},{3,2},{4,5},{5,4},{6,7},{7,6},{8,9},{9,8},{10,11... | collective-permute-start | bytes 1544 | tf_op jit(solution)/shard_map/ppermute | solution.py:608
  17.4 3.0 %collective-permute-start.5 = (f32[2,128]{1,0:T(2,128)S(1)}, f32[2,128]{1,0:T(2,128)S(1)}, u32[]{:S(2)}, u32[]{:S(2)}) collective-permute-start(f32[2,128]{1,0:T(2,128)S(1)} %pad_maximum_fusion.3.after), channel_id=1, source_target_pairs={{0,3},{1,2},{2,1},{3,0},{4,7},{5,6},{6,5},{7,4},{8,11},{9,10},{10,... | collective-permute-start | bytes 3080 | tf_op jit(solution)/shard_map/ppermute | solution.py:608
  20.4 3.1 %collective-permute-start.6 = (f32[4,128]{1,0:T(4,128)S(1)}, f32[4,128]{1,0:T(4,128)S(1)}, u32[]{:S(2)}, u32[]{:S(2)}) collective-permute-start(f32[4,128]{1,0:T(4,128)S(1)} %pad_maximum_fusion.2), channel_id=1, source_target_pairs={{0,5},{1,4},{2,7},{3,6},{4,1},{5,0},{6,3},{7,2},{8,13},{9,12},{10,... | collective-permute-start | bytes 6152 | tf_op jit(solution)/shard_map/ppermute | solution.py:608
  23.5 4.0 %collective-permute-start.7 = (f32[8,128]{1,0:T(8,128)S(1)}, f32[8,128]{1,0:T(8,128)S(1)}, u32[]{:S(2)}, u32[]{:S(2)}) collective-permute-start(f32[8,128]{1,0:T(8,128)S(1)} %pad_maximum_fusion.1.after), channel_id=1, source_target_pairs={{0,9},{1,8},{2,11},{3,10},{4,13},{5,12},{6,15},{7,14},{8,1},{9,0},... | collective-permute-start | bytes 12296 | tf_op jit(solution)/shard_map/ppermute | solution.py:608

commit v6 on v5

--- a/solution.py
+++ b/solution.py
@@ -152,7 +152,11 @@
             [
                 pltpu.make_async_copy(a.at[part], b.at[part], sems.at[3 + 3 * c + i])
                 for i, (a, b) in enumerate(
-                    ((zonal_in, zonal), (meridional_in, meridional), (tracer_in, tracer))
+                    (
+                        (zonal_in, zonal),
+                        (meridional_in, meridional),
+                        (tracer_in.at[:, :, NY - LANES:], tracer),
+                    )
                 )
             ]
         )
@@ -184,7 +188,7 @@
         mask = lc > k
         t, u, v = tracer[k], zonal[k], meridional[k]
         for base, field in ((LANE_MT, t), (LANE_MU, u), (LANE_MV, v)):
-            fold = jnp.where(tile_lane == base + k, field[:, NY - 1:], fold)
+            fold = jnp.where(tile_lane == base + k, field[:, -1:], fold)
         mu, mv = jnp.where(mask, u, 0.0), jnp.where(mask, v, 0.0)
         p = thickness(k) * (mu + mv)
         total += p
@@ -308,7 +312,7 @@
     east = jnp.where(
         row == 2 * COLS - 1, chip_change, jnp.where(row == 2 * COLS, far_change, 0.0)
     )
-    return tile + jnp.where(even, west, east)
+    return tile, jnp.where(even, west, east)
 
 
 def extend(even, west, chip, east):
@@ -378,7 +382,7 @@
     lane = iota((EXT, LANES), 1)
     mine = beyond[72:80, :LANES]
     mine = extend(even, mine, tile[...], mine)
-    theirs = across_fold(even, mirror[...], mirror_far[...])
+    theirs, between = across_fold(even, mirror[...], mirror_far[...])
     level = (lane - LANE_P).astype(f32)
     weight = jnp.where((lane >= LANE_P) & (lane < LANE_P + K), 0.5 * (0.5 + level / K), 0.0)
     mask_mine = (level < mine[:, LANE_LC:LANE_LC + 1]).astype(f32)
@@ -386,7 +390,7 @@
     flux = -jnp.sum(weight * (mask_mine * theirs + mask_theirs * mine), axis=1, keepdims=True)
     own_change = mine[:, LANE_DIFF:LANE_DIFF + 1] * flux
     far_change = theirs[:, LANE_DIFF:LANE_DIFF + 1] * flux
-    north = jnp.where(lane < COLS, theirs, 0.0)
+    north = jnp.where(lane < COLS, theirs, 0.0) + between
     north = north + jnp.where(lane == 0, far_change, 0.0)
     width = NY - NEAR + LANES
     south = last[...] + jnp.where(iota((EXT, width), 1) == width - 1, own_change, 0.0)
@@ -397,19 +401,18 @@
     )
     for j in range(ITERS):
         vectors[j * EXT:(j + 1) * EXT] = v[j][:, LANES:]
-    sub = iota((COLS, LANES), 0)
-    tile_lane = iota((COLS, LANES), 1)
-    out = jnp.zeros((COLS, LANES), f32)
+    size = GROUPS * COLS
+    high, low = [], []
     for g, pair in enumerate(gram_rows(v, range(1, width // LANES))):
-        at, low = g * COLS, (GROUPS + g) * COLS
-        pair = pair_add(pair, (partial[at:at + COLS], partial[low:low + COLS]))
-        step = LANES // 2
-        while step:
-            pair = pair_add(pair, tuple(roll(part, step, 1) for part in pair))
-            step //= 2
-        for part, base in zip(pair_norm(pair), (at, low)):
-            out = jnp.where(tile_lane - base == sub, part, out)
-    gram[...] = jnp.sum(out, axis=0, keepdims=True)
+        at = g * COLS
+        pair = pair_add(pair, (partial[at:at + COLS], partial[size + at:size + at + COLS]))
+        high.append(pair[0])
+        low.append(pair[1])
+    turned = jnp.concatenate(high + low + [jnp.zeros((LANES - 2 * size, LANES), f32)], axis=0).T
+    terms = [turned[i * COLS:(i + 1) * COLS] for i in range(LANES // COLS)]
+    high, low = pair_norm(pair_rows(pair_tree([(t, roll(t, -size, 1)) for t in terms])))
+    row = jnp.where(iota((COLS, LANES), 1) < size, high, roll(low, size, 1))
+    gram[...] = row[:1]
 
 
 def coefficients(gram):
@@ -614,7 +617,8 @@
     arguments = (tracer, zonal, meridional, count, diffusivity, surface)
     inner, outer = call(
         pack_kernel, [(PACK, NY)] * 2, *arguments,
-        scratch=[pltpu.VMEM(a.shape, a.dtype) for a in arguments]
+        scratch=[pltpu.VMEM((K, COLS, LANES), f32)]
+        + [pltpu.VMEM(a.shape, a.dtype) for a in arguments[1:]]
         + [pltpu.VMEM((6, K, NY), f32), pltpu.SemaphoreType.DMA((9 + 3 * CHUNKS,))], stay=len(arguments),
     )
     beyond = permute(outer, outward)

time: 29.3 us -> 28.7 us (0.980)
  Pallas kernels: 7.41 us -> 6.93 us
    pallas_call x7, Pallas kernels: 7.41 us -> 6.93 us  [call(): pl.pallas_call(kernel, out_shape=[jax.ShapeDtypeStruct(s, f32) for s in s...]
where the time goes in v6:
time: 28.7 us; the launch traced here: 28.5 us
  waiting for transfers between devices  12.3 us (43%)
  starting transfers between devices  8.54 us (30%)
  Pallas kernels  6.93 us (24%)
  between operations  0.73 us (3%)
    ppermute x8, waiting for transfers between devices, permute(): return lax.ppermute(value, 'lon', pairs)  12.3 us
    ppermute x8, starting transfers between devices, permute(): return lax.ppermute(value, 'lon', pairs)  8.54 us
    pallas_call x7, Pallas kernels, call(): pl.pallas_call(kernel, out_shape=[jax.ShapeDtypeStruct(s, f32) for s in s...  6.93 us
  transfers between devices with their start and end apart: 8, of which 6 were waited for; matrix products, arithmetic and copies ran while one was open for 0% of the time, Pallas kernels for 9%

profile of v6, /device:TPU:0, one launch (start us, length us, event | category | flops | bytes accessed | tf_op | source)
XLA Modules:
  0.0 28.5 jit_solution(6259894729142146852)
XLA Ops:
  0.6 1.6 %shard_map.93 = (f32[80,512]{1,0:T(8,128)S(1)}, f32[80,512]{1,0:T(8,128)S(1)}) custom-call(f32[16,8,512]{2,1,0:T(8,128)} %tracer.1, f32[16,8,512]{2,1,0:T(8,128)} %zonal.3, f32[16,8,512]{2,1,0:T(8,128)} %meridional.3, s32[8,512]{1,0:T(8,128)} %count.3, f32[8,512]{1,0:T(8,128)} %diffusivity.3, f32[8,512]{1,0:T(8,128)} %surface_in.1), custom_call_target="tpu_custom_call" | custom-call | bytes 1163264 | tf_op jit(solution)/shard_map/pallas_call | solution.py:595
  2.2 0.5 %collective-permute-start.1 = (f32[80,512]{1,0:T(8,128)S(1)}, f32[80,512]{1,0:T(8,128)S(1)}, u32[]{:S(2)}, u32[]{:S(2)}) collective-permute-start(f32[80,512]{1,0:T(8,128)S(1)} %get-tuple-element.26.inner), channel_id=1, source_target_pairs={{0,1},{1,0},{2,3},{3,2},{4,5},{5,4},{6,7},{7,6},{8,9},{9,8},{10,11... | collective-permute-start | bytes 491528 | tf_op jit(solution)/shard_map/ppermute | solution.py:611
  2.8 5.7 %collective-permute-start = (f32[80,512]{1,0:T(8,128)S(1)}, f32[80,512]{1,0:T(8,128)S(1)}, u32[]{:S(2)}, u32[]{:S(2)}) collective-permute-start(f32[80,512]{1,0:T(8,128)S(1)} %get-tuple-element.25.outer), channel_id=1, source_target_pairs={{0,15},{1,2},{2,1},{3,4},{4,3},{5,6},{6,5},{7,8},{8,7},{9,10},{10,... | collective-permute-start | bytes 491528 | tf_op jit(solution)/shard_map/ppermute | solution.py:611
  8.4 0.0 collective-permute-done.1.sibling
  8.4 0.0 copy-start.2
  8.4 0.1 shard_map.94
  8.6 1.1 %collective-permute-start.2 = (f32[16,128]{1,0:T(8,128)S(1)}, f32[16,128]{1,0:T(8,128)S(1)}, u32[]{:S(2)}, u32[]{:S(2)}) collective-permute-start(f32[16,128]{1,0:T(8,128)S(1)} %get-tuple-element.32), channel_id=1, source_target_pairs={{0,15},{1,14},{2,13},{3,12},{4,11},{5,10},{6,9},{7,8},{8,7},{9,6},... | collective-permute-start | bytes 24584 | tf_op jit(solution)/shard_map/ppermute | solution.py:611
  9.7 0.2 collective-permute-start.3
  9.9 1.7 %collective-permute-done.beyond = f32[80,512]{1,0:T(8,128)S(1)} collective-permute-done((f32[80,512]{1,0:T(8,128)S(1)}, f32[80,512]{1,0:T(8,128)S(1)}, u32[]{:S(2)}, u32[]{:S(2)}) %collective-permute-start) | collective-permute-done | bytes 163872 | tf_op jit(solution)/shard_map/ppermute | solution.py:611
  11.5 0.0 copy-start
  11.5 0.0 copy-start.1
  11.5 0.7 %shard_map.95 = (f32[24,256]{1,0:T(8,128)S(1)}, f32[24,256]{1,0:T(8,128)S(1)}, f32[144,384]{1,0:T(8,128)S(1)}, f32[64,128]{1,0:T(8,128)S(1)}) custom-call(f32[80,512]{1,0:T(8,128)S(1)} %get-tuple-element.25.outer, f32[80,512]{1,0:T(8,128)S(1)} %collective-permute-done.beyond, f32[16,512]{1,0:T(8,128)S(1)} %get-tuple-element.27.forcing, ...), custom_call_target="tpu_custom_call" | custom-call | flops 819200 | bytes 696320 | tf_op jit(solution)/shard_map/pallas_call | solution.py:595
  12.3 2.1 %collective-permute-done.2.mirror = f32[16,128]{1,0:T(8,128)S(1)} collective-permute-done((f32[16,128]{1,0:T(8,128)S(1)}, f32[16,128]{1,0:T(8,128)S(1)}, u32[]{:S(2)}, u32[]{:S(2)}) %collective-permute-start.2) | collective-permute-done | bytes 8224 | tf_op jit(solution)/shard_map/ppermute | solution.py:611
  14.4 0.0 collective-permute-done.3.mirror_far
  14.4 0.0 copy-start.3
  14.4 0.0 copy-start.4
  14.4 1.1 %shard_map.96 = (f32[144,256]{1,0:T(8,128)S(1)}, f32[1,128]{1,0:T(1,128)S(1)}) custom-call(f32[24,256]{1,0:T(8,128)S(1)} %get-tuple-element.29.last, f32[24,256]{1,0:T(8,128)S(1)} %get-tuple-element.30.last_code, f32[80,512]{1,0:T(8,128)S(1)} %collective-permute-done.beyond, f32[16,128]{1,0:T(8,128)S(1)} %get-tuple-element.31.tile, ...), custom_call_target="tpu_custom_call" | custom-call | bytes 418304 | tf_op jit(solution)/shard_map/pallas_call | solution.py:595
  15.5 0.5 %collective-permute-start.4 = (f32[1,128]{1,0:T(1,128)S(1)}, f32[1,128]{1,0:T(1,128)S(1)}, u32[]{:S(2)}, u32[]{:S(2)}) collective-permute-start(f32[1,128]{1,0:T(1,128)S(1)} %get-tuple-element.35), channel_id=1, source_target_pairs={{0,1},{1,0},{2,3},{3,2},{4,5},{5,4},{6,7},{7,6},{8,9},{9,8},{10,11... | collective-permute-start | bytes 1544 | tf_op jit(solution)/shard_map/ppermute | solution.py:611
  16.0 0.8 %collective-permute-done.4 = f32[1,128]{1,0:T(1,128)S(1)} collective-permute-done((f32[1,128]{1,0:T(1,128)S(1)}, f32[1,128]{1,0:T(1,128)S(1)}, u32[]{:S(2)}, u32[]{:S(2)}) %collective-permute-start.4) | collective-permute-done | bytes 544 | tf_op jit(solution)/shard_map/ppermute | solution.py:611
  16.8 0.4 %collective-permute-start.5 = (f32[2,128]{1,0:T(2,128)S(1)}, f32[2,128]{1,0:T(2,128)S(1)}, u32[]{:S(2)}, u32[]{:S(2)}) collective-permute-start(f32[2,128]{1,0:T(2,128)S(1)} %pad_maximum_fusion.3.after), channel_id=1, source_target_pairs={{0,3},{1,2},{2,1},{3,0},{4,7},{5,6},{6,5},{7,4},{8,11},{9,10},{10,... | collective-permute-start | bytes 3080 | tf_op jit(solution)/shard_map/ppermute | solution.py:611
  17.3 2.6 %collective-permute-done.5 = f32[2,128]{1,0:T(2,128)S(1)} collective-permute-done((f32[2,128]{1,0:T(2,128)S(1)}, f32[2,128]{1,0:T(2,128)S(1)}, u32[]{:S(2)}, u32[]{:S(2)}) %collective-permute-start.5) | collective-permute-done | bytes 1056 | tf_op jit(solution)/shard_map/ppermute | solution.py:611
  19.8 0.1 collective-permute-start.6
  19.9 0.0 copy-done.2
  19.9 0.0 copy-done
  19.9 0.0 copy-done.1
  19.9 0.0 copy-done.3
  20.0 0.0 copy-done.4
  20.0 1.2 %shard_map.97 = f32[16,8,512]{2,1,0:T(8,128)} custom-call(f32[16,8,512]{2,1,0:T(8,128)S(1)} %copy-done.2, f32[16,8,512]{2,1,0:T(8,128)S(1)} %copy-done, f32[16,8,512]{2,1,0:T(8,128)S(1)} %copy-done.1, s32[8,512]{1,0:T(8,128)S(1)} %copy-done.3, f32[8,512]{1,0:T(8,128)S(1)} %copy-done.4, f32[80,512]{1,0:T(8,128)S(1)} %collective-permute-done.1.sibling, ...), custom_call_target="tpu_custom_call" | custom-call | flops 2621440 | bytes 1417216 | tf_op jit(solution)/shard_map/pallas_call | solution.py:595
  21.1 1.8 %collective-permute-done.6 = f32[4,128]{1,0:T(4,128)S(1)} collective-permute-done((f32[4,128]{1,0:T(4,128)S(1)}, f32[4,128]{1,0:T(4,128)S(1)}, u32[]{:S(2)}, u32[]{:S(2)}) %collective-permute-start.6) | collective-permute-done | bytes 2080 | tf_op jit(solution)/shard_map/ppermute | solution.py:611
  22.9 0.1 collective-permute-start.7
  23.0 0.6 %shard_map.98 = (f32[16,8,512]{2,1,0:T(8,128)S(1)}, f32[16,8,512]{2,1,0:T(8,128)S(1)}, f32[8,512]{1,0:T(8,128)S(1)}) custom-call(f32[16,8,512]{2,1,0:T(8,128)S(1)} %copy-done, f32[16,8,512]{2,1,0:T(8,128)S(1)} %copy-done.1, s32[8,512]{1,0:T(8,128)S(1)} %copy-done.3, f32[8,512]{1,0:T(8,128)S(1)} %copy-done.4, f32[80,512]{1,0:T(8,128)S(1)} %collective-permute-done.1.sibling, ...), custom_call_target="tpu_custom_call" | custom-call | flops 2621440 | bytes 1433600 | tf_op jit(solution)/shard_map/pallas_call | solution.py:595
  23.6 3.3 %collective-permute-done.7 = f32[8,128]{1,0:T(8,128)S(1)} collective-permute-done((f32[8,128]{1,0:T(8,128)S(1)}, f32[8,128]{1,0:T(8,128)S(1)}, u32[]{:S(2)}, u32[]{:S(2)}) %collective-permute-start.7) | collective-permute-done | bytes 4128 | tf_op jit(solution)/shard_map/ppermute | solution.py:611
  26.9 1.6 %shard_map.99 = (f32[16,8,512]{2,1,0:T(8,128)}, f32[16,8,512]{2,1,0:T(8,128)}, f32[8,512]{1,0:T(8,128)}) custom-call(f32[16,128]{1,0:T(8,128)S(1)} %pad_maximum_fusion.gram, f32[144,384]{1,0:T(8,128)S(1)} %get-tuple-element.38.vectors, f32[144,256]{1,0:T(8,128)S(1)} %get-tuple-element.39.vectors_last, f32[16,8,512]{2,1,0:T(8,128)S(1)} %get-tuple-element.40.zonal, ...), custom_call_target="tpu_custom_call" | custom-call | bytes 1458176 | tf_op jit(solution)/shard_map/pallas_call | solution.py:595
  (4 shorter events, 0.0 us)
Async XLA Ops:
  2.2 6.2 %collective-permute-start.1 = (f32[80,512]{1,0:T(8,128)S(1)}, f32[80,512]{1,0:T(8,128)S(1)}, u32[]{:S(2)}, u32[]{:S(2)}) collective-permute-start(f32[80,512]{1,0:T(8,128)S(1)} %get-tuple-element.26.inner), channel_id=1, source_target_pairs={{0,1},{1,0},{2,3},{3,2},{4,5},{5,4},{6,7},{7,6},{8,9},{9,8},{10,11... | collective-permute-start | bytes 491528 | tf_op jit(solution)/shard_map/ppermute | solution.py:611
  2.8 8.8 %collective-permute-start = (f32[80,512]{1,0:T(8,128)S(1)}, f32[80,512]{1,0:T(8,128)S(1)}, u32[]{:S(2)}, u32[]{:S(2)}) collective-permute-start(f32[80,512]{1,0:T(8,128)S(1)} %get-tuple-element.25.outer), channel_id=1, source_target_pairs={{0,15},{1,2},{2,1},{3,4},{4,3},{5,6},{6,5},{7,8},{8,7},{9,10},{10,... | collective-permute-start | bytes 491528 | tf_op jit(solution)/shard_map/ppermute | solution.py:611
  8.4 11.5 %copy-start.2 = (f32[16,8,512]{2,1,0:T(8,128)S(1)}, f32[16,8,512]{2,1,0:T(8,128)}, u32[]{:S(2)}) copy-start(f32[16,8,512]{2,1,0:T(8,128)} %tracer.1) | copy-start | bytes 786436
  8.6 5.8 %collective-permute-start.2 = (f32[16,128]{1,0:T(8,128)S(1)}, f32[16,128]{1,0:T(8,128)S(1)}, u32[]{:S(2)}, u32[]{:S(2)}) collective-permute-start(f32[16,128]{1,0:T(8,128)S(1)} %get-tuple-element.32), channel_id=1, source_target_pairs={{0,15},{1,14},{2,13},{3,12},{4,11},{5,10},{6,9},{7,8},{8,7},{9,6},... | collective-permute-start | bytes 24584 | tf_op jit(solution)/shard_map/ppermute | solution.py:611
  9.7 4.8 %collective-permute-start.3 = (f32[16,128]{1,0:T(8,128)S(1)}, f32[16,128]{1,0:T(8,128)S(1)}, u32[]{:S(2)}, u32[]{:S(2)}) collective-permute-start(f32[16,128]{1,0:T(8,128)S(1)} %get-tuple-element.33), channel_id=1, source_target_pairs={{1,0},{12,1},{15,2},{10,3},{13,4},{8,5},{11,6},{6,7},{9,8},{4,9},{... | collective-permute-start | bytes 24584 | tf_op jit(solution)/shard_map/ppermute | solution.py:611
  11.5 8.4 %copy-start = (f32[16,8,512]{2,1,0:T(8,128)S(1)}, f32[16,8,512]{2,1,0:T(8,128)}, u32[]{:S(2)}) copy-start(f32[16,8,512]{2,1,0:T(8,128)} %zonal.3) | copy-start | bytes 786436
  11.5 8.4 %copy-start.1 = (f32[16,8,512]{2,1,0:T(8,128)S(1)}, f32[16,8,512]{2,1,0:T(8,128)}, u32[]{:S(2)}) copy-start(f32[16,8,512]{2,1,0:T(8,128)} %meridional.3) | copy-start | bytes 786436
  14.4 5.5 %copy-start.3 = (s32[8,512]{1,0:T(8,128)S(1)}, s32[8,512]{1,0:T(8,128)}, u32[]{:S(2)}) copy-start(s32[8,512]{1,0:T(8,128)} %count.3) | copy-start | bytes 49156
  14.4 5.5 %copy-start.4 = (f32[8,512]{1,0:T(8,128)S(1)}, f32[8,512]{1,0:T(8,128)}, u32[]{:S(2)}) copy-start(f32[8,512]{1,0:T(8,128)} %diffusivity.3) | copy-start | bytes 49156
  15.5 1.3 %collective-permute-start.4 = (f32[1,128]{1,0:T(1,128)S(1)}, f32[1,128]{1,0:T(1,128)S(1)}, u32[]{:S(2)}, u32[]{:S(2)}) collective-permute-start(f32[1,128]{1,0:T(1,128)S(1)} %get-tuple-element.35), channel_id=1, source_target_pairs={{0,1},{1,0},{2,3},{3,2},{4,5},{5,4},{6,7},{7,6},{8,9},{9,8},{10,11... | collective-permute-start | bytes 1544 | tf_op jit(solution)/shard_map/ppermute | solution.py:611
  16.8 3.0 %collective-permute-start.5 = (f32[2,128]{1,0:T(2,128)S(1)}, f32[2,128]{1,0:T(2,128)S(1)}, u32[]{:S(2)}, u32[]{:S(2)}) collective-permute-start(f32[2,128]{1,0:T(2,128)S(1)} %pad_maximum_fusion.3.after), channel_id=1, source_target_pairs={{0,3},{1,2},{2,1},{3,0},{4,7},{5,6},{6,5},{7,4},{8,11},{9,10},{10,... | collective-permute-start | bytes 3080 | tf_op jit(solution)/shard_map/ppermute | solution.py:611
  19.8 3.1 %collective-permute-start.6 = (f32[4,128]{1,0:T(4,128)S(1)}, f32[4,128]{1,0:T(4,128)S(1)}, u32[]{:S(2)}, u32[]{:S(2)}) collective-permute-start(f32[4,128]{1,0:T(4,128)S(1)} %pad_maximum_fusion.2), channel_id=1, source_target_pairs={{0,5},{1,4},{2,7},{3,6},{4,1},{5,0},{6,3},{7,2},{8,13},{9,12},{10,... | collective-permute-start | bytes 6152 | tf_op jit(solution)/shard_map/ppermute | solution.py:611
  22.9 4.0 %collective-permute-start.7 = (f32[8,128]{1,0:T(8,128)S(1)}, f32[8,128]{1,0:T(8,128)S(1)}, u32[]{:S(2)}, u32[]{:S(2)}) collective-permute-start(f32[8,128]{1,0:T(8,128)S(1)} %pad_maximum_fusion.1.after), channel_id=1, source_target_pairs={{0,9},{1,8},{2,11},{3,10},{4,13},{5,12},{6,15},{7,14},{8,1},{9,0},... | collective-permute-start | bytes 12296 | tf_op jit(solution)/shard_map/ppermute | solution.py:611

commit v7 on v6

--- a/solution.py
+++ b/solution.py
@@ -412,7 +412,7 @@
     terms = [turned[i * COLS:(i + 1) * COLS] for i in range(LANES // COLS)]
     high, low = pair_norm(pair_rows(pair_tree([(t, roll(t, -size, 1)) for t in terms])))
     row = jnp.where(iota((COLS, LANES), 1) < size, high, roll(low, size, 1))
-    gram[...] = row[:1]
+    gram[...] = jnp.broadcast_to(row[:1], gram.shape)
 
 
 def coefficients(gram):
@@ -533,7 +533,7 @@
 
 
 def tracer_kernel(
-    tracer, zonal, meridional, count, diffusivity, sibling, beyond, mirror, after, tracer_next
+    tracer, zonal, meridional, count, diffusivity, sibling, beyond, mirror, tracer_next
 ):
     lc, padded, mask_sum = neighbours(count, sibling, beyond, mirror)
     diff = diffusivity[...]
@@ -561,7 +561,7 @@
 
 
 def flow_kernel(
-    zonal, meridional, count, diffusivity, sibling, beyond, mirror, after,
+    zonal, meridional, count, diffusivity, sibling, beyond, mirror,
     zonal_step, meridional_step, levels,
 ):
     lc, padded, mask_sum = neighbours(count, sibling, beyond, mirror)
@@ -578,20 +578,16 @@
         meridional_step[k] = mask * (v + diff * (meridional_sum - sides * v) - turn * u)
 
 
-def call(kernel, shapes, *args, flops=0, after=None, scratch=(), stay=0):
+def call(kernel, shapes, *args, flops=0, scratch=(), stay=0):
     moved = 4 * sum(a.size for a in args) + 4 * sum(
         functools.reduce(lambda x, y: x * y, s, 1) for s in shapes
     )
     space = pl.BlockSpec(memory_space=pltpu.VMEM)
-    anywhere = pl.BlockSpec(memory_space=pl.ANY)
     in_specs = [space] * (len(args) - stay) + [pl.BlockSpec(memory_space=pltpu.HBM)] * stay
     here = len(args) - stay
     args = args[:here] + tuple(
         pltpu.with_memory_space_constraint(a, pltpu.HBM) for a in args[here:]
     )
-    if after is not None:
-        in_specs.append(anywhere)
-        args = args + (after,)
     return pl.pallas_call(
         kernel,
         out_shape=[jax.ShapeDtypeStruct(s, f32) for s in shapes],
@@ -637,29 +633,22 @@
     )
     vectors_last, gram = call(
         fold_kernel,
-        [(ITERS * EXT, NY - NEAR + LANES), (1, LANES)],
+        [(ITERS * EXT, NY - NEAR + LANES), (size, LANES)],
         last, last_code, beyond, tile, mirror, mirror_far, partial,
     )
     halos = (sibling, beyond, mirror)
-    reach = 1
-    tracer_next = None
-    while reach < size:
-        if 8 * reach >= size and tracer_next is None and reach > 1:
-            tracer_next, = call(
-                tracer_kernel, [block],
-                tracer, zonal, meridional, count, diffusivity, *halos,
-                flops=65536 * 40, after=gram,
-            )
-        other = permute(gram, [(i, i ^ (reach ^ 1 if reach > 1 else 1)) for i in range(size)])
-        gram = jnp.concatenate([gram, other], axis=0)
-        reach *= 2
-        if 2 * reach == size:
-            gram, tracer_next = lax.optimization_barrier((gram, tracer_next))
-            zonal_step, meridional_step, levels = call(
-                flow_kernel, [block, block, (COLS, NY)],
-                zonal, meridional, count, diffusivity, *halos,
-                flops=65536 * 40, after=gram,
-            )
+    tracer_next, = call(
+        tracer_kernel, [block],
+        tracer, zonal, meridional, count, diffusivity, *halos,
+        flops=65536 * 40,
+    )
+    zonal_step, meridional_step, levels = call(
+        flow_kernel, [block, block, (COLS, NY)],
+        zonal, meridional, count, diffusivity, *halos,
+        flops=65536 * 40,
+    )
+    group = [(i + size // 2 + 1) % size for i in range(size)]
+    gram = lax.all_to_all(gram, "lon", 0, 0, tiled=True, axis_index_groups=[group])
     zonal_next, meridional_next, height = call(
         finish_kernel, [block, block, (COLS, NY)],
         gram, vectors, vectors_last, zonal_step, meridional_step, levels,

time: 28.7 us -> 26.3 us (0.916)
  waiting for transfers between devices: 12.3 us -> 6.07 us
  starting transfers between devices: 8.54 us -> 11.8 us
  Pallas kernels: 6.93 us -> 7.49 us
    ppermute x8 -> x4, waiting for transfers between devices: 12.3 us -> 3.8 us  [permute(): return lax.ppermute(value, 'lon', pairs)]
    all_to_all x0 -> x1, starting transfers between devices: none -> 4.31 us  [body(): lax.all_to_all(gram, 'lon', 0, 0, tiled=True, axis_index_groups=[group])]
    all_to_all x0 -> x1, waiting for transfers between devices: none -> 2.26 us  [body(): lax.all_to_all(gram, 'lon', 0, 0, tiled=True, axis_index_groups=[group])]
    ppermute x8 -> x4, starting transfers between devices: 8.54 us -> 7.47 us  [permute(): return lax.ppermute(value, 'lon', pairs)]
    pallas_call x7, Pallas kernels: 6.93 us -> 7.49 us  [call(): pl.pallas_call(kernel, out_shape=[jax.ShapeDtypeStruct(s, f32) for s in s...]
  transfers between devices with their start and end apart: 8 -> 5, of which waited for: 6 -> 3; matrix products, arithmetic and copies ran while one was open for 0% -> 0% of each run, Pallas kernels for 9% -> 10%
where the time goes in v7:
time: 26.3 us; the launch traced here: 26.1 us
  starting transfers between devices  11.8 us (45%)
  Pallas kernels  7.49 us (28%)
  waiting for transfers between devices  6.07 us (23%)
  between operations  0.7 us (3%)
    pallas_call x7, Pallas kernels, call(): pl.pallas_call(kernel, out_shape=[jax.ShapeDtypeStruct(s, f32) for s in s...  7.49 us
    ppermute x4, starting transfers between devices, permute(): return lax.ppermute(value, 'lon', pairs)  7.47 us
    all_to_all x1, starting transfers between devices, body(): lax.all_to_all(gram, 'lon', 0, 0, tiled=True, axis_index_groups=[group])  4.31 us
    ppermute x4, waiting for transfers between devices, permute(): return lax.ppermute(value, 'lon', pairs)  3.8 us
    all_to_all x1, waiting for transfers between devices, body(): lax.all_to_all(gram, 'lon', 0, 0, tiled=True, axis_index_groups=[group])  2.26 us
  transfers between devices with their start and end apart: 5, of which 3 were waited for; matrix products, arithmetic and copies ran while one was open for 0% of the time, Pallas kernels for 10%

profile of v7, /device:TPU:0, one launch (start us, length us, event | category | flops | bytes accessed | tf_op | source)
XLA Modules:
  0.0 26.1 jit_solution(5933139937760349354)
XLA Ops:
  0.6 1.6 %shard_map.93 = (f32[80,512]{1,0:T(8,128)S(1)}, f32[80,512]{1,0:T(8,128)S(1)}) custom-call(f32[16,8,512]{2,1,0:T(8,128)} %tracer.1, f32[16,8,512]{2,1,0:T(8,128)} %zonal.3, f32[16,8,512]{2,1,0:T(8,128)} %meridional.3, s32[8,512]{1,0:T(8,128)} %count.3, f32[8,512]{1,0:T(8,128)} %diffusivity.3, f32[8,512]{1,0:T(8,128)} %surface_in.1), custom_call_target="tpu_custom_call" | custom-call | bytes 1163264 | tf_op jit(solution)/shard_map/pallas_call | solution.py:591
  2.2 0.5 %collective-permute-start = (f32[80,512]{1,0:T(8,128)S(1)}, f32[80,512]{1,0:T(8,128)S(1)}, u32[]{:S(2)}, u32[]{:S(2)}) collective-permute-start(f32[80,512]{1,0:T(8,128)S(1)} %get-tuple-element.23.inner), channel_id=1, source_target_pairs={{0,1},{1,0},{2,3},{3,2},{4,5},{5,4},{6,7},{7,6},{8,9},{9,8},{10,11... | collective-permute-start | bytes 491528 | tf_op jit(solution)/shard_map/ppermute | solution.py:607
  2.8 5.7 %collective-permute-start.1 = (f32[80,512]{1,0:T(8,128)S(1)}, f32[80,512]{1,0:T(8,128)S(1)}, u32[]{:S(2)}, u32[]{:S(2)}) collective-permute-start(f32[80,512]{1,0:T(8,128)S(1)} %get-tuple-element.24.outer), channel_id=1, source_target_pairs={{0,15},{1,2},{2,1},{3,4},{4,3},{5,6},{6,5},{7,8},{8,7},{9,10},{10,... | collective-permute-start | bytes 491528 | tf_op jit(solution)/shard_map/ppermute | solution.py:607
  8.4 0.0 collective-permute-done.sibling
  8.4 0.0 copy-start.2
  8.4 0.1 shard_map.94
  8.6 1.1 %collective-permute-start.2 = (f32[16,128]{1,0:T(8,128)S(1)}, f32[16,128]{1,0:T(8,128)S(1)}, u32[]{:S(2)}, u32[]{:S(2)}) collective-permute-start(f32[16,128]{1,0:T(8,128)S(1)} %get-tuple-element.25), channel_id=1, source_target_pairs={{0,15},{1,14},{2,13},{3,12},{4,11},{5,10},{6,9},{7,8},{8,7},{9,6},... | collective-permute-start | bytes 24584 | tf_op jit(solution)/shard_map/ppermute | solution.py:607
  9.7 0.2 collective-permute-start.3
  9.9 1.7 %collective-permute-done.1.beyond = f32[80,512]{1,0:T(8,128)S(1)} collective-permute-done((f32[80,512]{1,0:T(8,128)S(1)}, f32[80,512]{1,0:T(8,128)S(1)}, u32[]{:S(2)}, u32[]{:S(2)}) %collective-permute-start.1) | collective-permute-done | bytes 163872 | tf_op jit(solution)/shard_map/ppermute | solution.py:607
  11.5 0.0 copy-start
  11.5 0.0 copy-start.1
  11.5 0.7 %shard_map.96 = (f32[24,256]{1,0:T(8,128)S(1)}, f32[24,256]{1,0:T(8,128)S(1)}, f32[144,384]{1,0:T(8,128)S(1)}, f32[64,128]{1,0:T(8,128)S(1)}) custom-call(f32[80,512]{1,0:T(8,128)S(1)} %get-tuple-element.24.outer, f32[80,512]{1,0:T(8,128)S(1)} %collective-permute-done.1.beyond, f32[16,512]{1,0:T(8,128)S(1)} %get-tuple-element.26.forcing, ...), custom_call_target="tpu_custom_call" | custom-call | flops 819200 | bytes 696320 | tf_op jit(solution)/shard_map/pallas_call | solution.py:591
  12.3 2.1 %collective-permute-done.2.mirror = f32[16,128]{1,0:T(8,128)S(1)} collective-permute-done((f32[16,128]{1,0:T(8,128)S(1)}, f32[16,128]{1,0:T(8,128)S(1)}, u32[]{:S(2)}, u32[]{:S(2)}) %collective-permute-start.2) | collective-permute-done | bytes 8224 | tf_op jit(solution)/shard_map/ppermute | solution.py:607
  14.4 0.0 collective-permute-done.3.mirror_far
  14.4 0.0 copy-start.4
  14.4 1.7 %shard_map.97 = (f32[144,256]{1,0:T(8,128)S(1)}, f32[16,128]{1,0:T(8,128)}) custom-call(f32[24,256]{1,0:T(8,128)S(1)} %get-tuple-element.28.last, f32[24,256]{1,0:T(8,128)S(1)} %get-tuple-element.29.last_code, f32[80,512]{1,0:T(8,128)S(1)} %collective-permute-done.1.beyond, f32[16,128]{1,0:T(8,128)S(1)} %get-tuple-element.30.tile, ...), custom_call_target="tpu_custom_call" | custom-call | bytes 425984 | tf_op jit(solution)/shard_map/pallas_call | solution.py:591
  16.1 0.0 copy-start.3
  16.1 4.3 %all-to-all-start = ((f32[16,1,128]{2,1,0:T(1,128)}), f32[16,1,128]{2,1,0:T(1,128)S(1)}, u32[]{:S(2)}, u32[]{:S(2)}) async-start(f32[16,1,128]{2,1,0:T(1,128)} %bitcast.1), calls=%async_computation | async-start | bytes 16384 | tf_op jit(solution)/shard_map/all_to_all | solution.py:651
  20.4 0.0 copy-done.2
  20.4 0.0 copy-done
  20.4 0.0 copy-done.1
  20.5 0.0 copy-done.4
  20.5 0.0 copy-done.3
  20.5 1.2 %shard_map.95 = f32[16,8,512]{2,1,0:T(8,128)} custom-call(f32[16,8,512]{2,1,0:T(8,128)S(1)} %copy-done.2, f32[16,8,512]{2,1,0:T(8,128)S(1)} %copy-done, f32[16,8,512]{2,1,0:T(8,128)S(1)} %copy-done.1, s32[8,512]{1,0:T(8,128)S(1)} %copy-done.3, f32[8,512]{1,0:T(8,128)S(1)} %copy-done.4, f32[80,512]{1,0:T(8,128)S(1)} %collective-permute-done.sibling, ...), custom_call_target="tpu_custom_call" | custom-call | flops 2621440 | bytes 1417216 | tf_op jit(solution)/shard_map/pallas_call | solution.py:591
  21.6 0.6 %shard_map.98 = (f32[16,8,512]{2,1,0:T(8,128)S(1)}, f32[16,8,512]{2,1,0:T(8,128)S(1)}, f32[8,512]{1,0:T(8,128)S(1)}) custom-call(f32[16,8,512]{2,1,0:T(8,128)S(1)} %copy-done, f32[16,8,512]{2,1,0:T(8,128)S(1)} %copy-done.1, s32[8,512]{1,0:T(8,128)S(1)} %copy-done.3, f32[8,512]{1,0:T(8,128)S(1)} %copy-done.4, f32[80,512]{1,0:T(8,128)S(1)} %collective-permute-done.sibling, ...), custom_call_target="tpu_custom_call" | custom-call | flops 2621440 | bytes 1433600 | tf_op jit(solution)/shard_map/pallas_call | solution.py:591
  22.2 2.3 %all-to-all-done = f32[16,1,128]{2,1,0:T(1,128)S(1)} async-done(((f32[16,1,128]{2,1,0:T(1,128)}), f32[16,1,128]{2,1,0:T(1,128)S(1)}, u32[]{:S(2)}, u32[]{:S(2)}) %all-to-all-start) | async-done | bytes 8224 | tf_op jit(solution)/shard_map/all_to_all | solution.py:651
  24.5 1.6 %shard_map.99 = (f32[16,8,512]{2,1,0:T(8,128)}, f32[16,8,512]{2,1,0:T(8,128)}, f32[8,512]{1,0:T(8,128)}) custom-call(f32[16,128]{1,0:T(8,128)S(1)} %bitcast.4, f32[144,384]{1,0:T(8,128)S(1)} %get-tuple-element.34.vectors, f32[144,256]{1,0:T(8,128)S(1)} %get-tuple-element.35.vectors_last, f32[16,8,512]{2,1,0:T(8,128)S(1)} %get-tuple-element.36.zonal, ...), custom_call_target="tpu_custom_call" | custom-call | bytes 1458176 | tf_op jit(solution)/shard_map/pallas_call | solution.py:591
Async XLA Ops:
  2.2 6.2 %collective-permute-start = (f32[80,512]{1,0:T(8,128)S(1)}, f32[80,512]{1,0:T(8,128)S(1)}, u32[]{:S(2)}, u32[]{:S(2)}) collective-permute-start(f32[80,512]{1,0:T(8,128)S(1)} %get-tuple-element.23.inner), channel_id=1, source_target_pairs={{0,1},{1,0},{2,3},{3,2},{4,5},{5,4},{6,7},{7,6},{8,9},{9,8},{10,11... | collective-permute-start | bytes 491528 | tf_op jit(solution)/shard_map/ppermute | solution.py:607
  2.8 8.8 %collective-permute-start.1 = (f32[80,512]{1,0:T(8,128)S(1)}, f32[80,512]{1,0:T(8,128)S(1)}, u32[]{:S(2)}, u32[]{:S(2)}) collective-permute-start(f32[80,512]{1,0:T(8,128)S(1)} %get-tuple-element.24.outer), channel_id=1, source_target_pairs={{0,15},{1,2},{2,1},{3,4},{4,3},{5,6},{6,5},{7,8},{8,7},{9,10},{10,... | collective-permute-start | bytes 491528 | tf_op jit(solution)/shard_map/ppermute | solution.py:607
  8.4 12.0 %copy-start.2 = (f32[16,8,512]{2,1,0:T(8,128)S(1)}, f32[16,8,512]{2,1,0:T(8,128)}, u32[]{:S(2)}) copy-start(f32[16,8,512]{2,1,0:T(8,128)} %tracer.1) | copy-start | bytes 786436
  8.6 5.8 %collective-permute-start.2 = (f32[16,128]{1,0:T(8,128)S(1)}, f32[16,128]{1,0:T(8,128)S(1)}, u32[]{:S(2)}, u32[]{:S(2)}) collective-permute-start(f32[16,128]{1,0:T(8,128)S(1)} %get-tuple-element.25), channel_id=1, source_target_pairs={{0,15},{1,14},{2,13},{3,12},{4,11},{5,10},{6,9},{7,8},{8,7},{9,6},... | collective-permute-start | bytes 24584 | tf_op jit(solution)/shard_map/ppermute | solution.py:607
  9.7 4.8 %collective-permute-start.3 = (f32[16,128]{1,0:T(8,128)S(1)}, f32[16,128]{1,0:T(8,128)S(1)}, u32[]{:S(2)}, u32[]{:S(2)}) collective-permute-start(f32[16,128]{1,0:T(8,128)S(1)} %get-tuple-element.31), channel_id=1, source_target_pairs={{1,0},{12,1},{15,2},{10,3},{13,4},{8,5},{11,6},{6,7},{9,8},{4,9},{... | collective-permute-start | bytes 24584 | tf_op jit(solution)/shard_map/ppermute | solution.py:607
  11.5 8.9 %copy-start = (f32[16,8,512]{2,1,0:T(8,128)S(1)}, f32[16,8,512]{2,1,0:T(8,128)}, u32[]{:S(2)}) copy-start(f32[16,8,512]{2,1,0:T(8,128)} %zonal.3) | copy-start | bytes 786436
  11.5 8.9 %copy-start.1 = (f32[16,8,512]{2,1,0:T(8,128)S(1)}, f32[16,8,512]{2,1,0:T(8,128)}, u32[]{:S(2)}) copy-start(f32[16,8,512]{2,1,0:T(8,128)} %meridional.3) | copy-start | bytes 786436
  14.4 6.0 %copy-start.4 = (f32[8,512]{1,0:T(8,128)S(1)}, f32[8,512]{1,0:T(8,128)}, u32[]{:S(2)}) copy-start(f32[8,512]{1,0:T(8,128)} %diffusivity.3) | copy-start | bytes 49156
  16.1 4.4 %copy-start.3 = (s32[8,512]{1,0:T(8,128)S(1)}, s32[8,512]{1,0:T(8,128)}, u32[]{:S(2)}) copy-start(s32[8,512]{1,0:T(8,128)} %count.3) | copy-start | bytes 49156
  16.1 8.4 %all-to-all-start = ((f32[16,1,128]{2,1,0:T(1,128)}), f32[16,1,128]{2,1,0:T(1,128)S(1)}, u32[]{:S(2)}, u32[]{:S(2)}) async-start(f32[16,1,128]{2,1,0:T(1,128)} %bitcast.1), calls=%async_computation | async-start | bytes 16384 | tf_op jit(solution)/shard_map/all_to_all | solution.py:651

commit v8 on v7

--- a/solution.py
+++ b/solution.py
@@ -15,7 +15,7 @@
 LANES = 128
 PACK = 80
 BASIS = ITERS + 1
-NEAR = 384
+CUT = NY - COLS
 GROUPS = (BASIS * (BASIS + 1) // 2 + COLS - 1) // COLS
 CHUNKS = 2
 
@@ -33,6 +33,8 @@
 LANE_MU = 56
 LANE_MV = 72
 LANE_EDGE = 88
+LANE_CODE = LANES - 2 * COLS
+LANE_F = LANES - COLS
 
 f32 = jnp.float32
 
@@ -281,8 +283,8 @@
     lane = iota((2 * COLS, LANES), 1)
     for j in range(COLS):
         at = NY - 1 - j
-        fold = jnp.where(lane == j, full[:, at:at + 1], fold)
-        fold = jnp.where(lane == COLS + j, code[:, at:at + 1], fold)
+        fold = jnp.where(lane == LANE_F + j, full[:, at:at + 1], fold)
+        fold = jnp.where(lane == LANE_CODE + j, code[:, at:at + 1], fold)
     fold = jnp.concatenate(
         [fold[i:i + 1] for i in range(2 * COLS - 1, -1, -1)], axis=0
     )
@@ -290,7 +292,7 @@
         edge = jnp.concatenate(
             [source[72:80, LANES:2 * LANES], source[72:80, 2 * LANES:3 * LANES]], axis=0
         )
-        out[...] = jnp.where(lane >= LANE_EDGE, edge, fold)
+        out[...] = jnp.where((lane >= LANE_EDGE) & (lane < LANE_CODE), edge, fold)
 
 
 def across_fold(even, chip, far):
@@ -303,7 +305,8 @@
     )
 
     def change(tile):
-        return jnp.where(lane < COLS, roll(roll(tile[:1], -2 * COLS, 1) * flux, -LANE_EDGE, 1), 0.0)
+        product = roll(tile[:1], -2 * COLS, 1) * flux
+        return jnp.where(lane >= LANE_F, roll(product, LANE_F - LANE_EDGE, 1), 0.0)
 
     chip_change, far_change = change(chip), -change(far)
     tile = extend(even, far[COLS:], chip, far[:COLS])
@@ -343,15 +346,14 @@
     return v
 
 
-def gram_rows(v, blocks):
-    own = [[q[COLS:2 * COLS, c * LANES:(c + 1) * LANES] for c in blocks] for q in v]
-    parts = [[split(q) for q in row] for row in own]
+def gram_rows(blocks):
+    parts = [[split(q) for q in row] for row in blocks]
     entries = []
     for i in range(BASIS):
         for j in range(i, BASIS):
             terms = [
-                two_prod(own[i][c], own[j][c], parts[i][c], parts[j][c])
-                for c in range(len(blocks))
+                two_prod(a, b, a_parts, b_parts)
+                for a, b, a_parts, b_parts in zip(blocks[i], blocks[j], parts[i], parts[j])
             ]
             entries.append(pair_tree(terms))
     return [pair_pack(entries[g:g + COLS]) for g in range(0, len(entries), COLS)]
@@ -367,12 +369,18 @@
     far_forcing, far_code = beyond[:COLS], beyond[COLS:2 * COLS]
     south = extend(even, far_forcing, forcing[...], far_forcing) + jnp.where(even, west, east)
     code = extend(even, far_code, coded[...], far_code)
-    last[...] = south[:, NEAR - LANES:]
-    last_code[...] = code[:, NEAR - LANES:]
+    last[...] = roll(south[:, NY - LANES:], -COLS, 1)
+    last_code[...] = roll(code[:, NY - LANES:], -COLS, 1)
     v = basis(south, code)
-    for j in range(ITERS):
-        vectors[j * EXT:(j + 1) * EXT] = v[j][:, :NEAR]
-    for g, pair in enumerate(gram_rows(v, range(NEAR // LANES))):
+    lane = iota((COLS, LANES), 1)
+    blocks = []
+    for j, q in enumerate(v):
+        if j < ITERS:
+            vectors[j * EXT:(j + 1) * EXT] = q
+        cut = [q[COLS:2 * COLS, c:c + LANES] for c in range(0, NY, LANES)]
+        cut[-1] = jnp.where(lane < LANES - COLS, cut[-1], 0.0)
+        blocks.append(cut)
+    for g, pair in enumerate(gram_rows(blocks)):
         for at, part in zip((0, GROUPS * COLS), pair):
             partial[at + g * COLS:at + (g + 1) * COLS] = part
 
@@ -390,20 +398,21 @@
     flux = -jnp.sum(weight * (mask_mine * theirs + mask_theirs * mine), axis=1, keepdims=True)
     own_change = mine[:, LANE_DIFF:LANE_DIFF + 1] * flux
     far_change = theirs[:, LANE_DIFF:LANE_DIFF + 1] * flux
-    north = jnp.where(lane < COLS, theirs, 0.0) + between
-    north = north + jnp.where(lane == 0, far_change, 0.0)
-    width = NY - NEAR + LANES
-    south = last[...] + jnp.where(iota((EXT, width), 1) == width - 1, own_change, 0.0)
-    north_code = jnp.where(lane < COLS, roll(theirs, -COLS, 1), -1.0)
-    v = basis(
-        jnp.concatenate([south, north], axis=1),
-        jnp.concatenate([last_code[...], north_code], axis=1),
-    )
+    beyond_fold = lane >= LANE_F
+    start = jnp.where(beyond_fold, theirs, last[...]) + between
+    start = start + jnp.where(
+        lane == LANE_F, far_change, jnp.where(lane == LANE_F - 1, own_change, 0.0)
+    )
+    code = jnp.where(beyond_fold, roll(theirs, LANE_F - LANE_CODE, 1), last_code[...])
+    v = basis(start, code)
     for j in range(ITERS):
-        vectors[j * EXT:(j + 1) * EXT] = v[j][:, LANES:]
+        vectors[j * EXT:(j + 1) * EXT] = v[j]
+    own_lane = lane[:COLS]
+    summed = (own_lane >= LANE_F - COLS) & (own_lane < LANE_F)
+    blocks = [[jnp.where(summed, q[COLS:2 * COLS], 0.0)] for q in v]
     size = GROUPS * COLS
     high, low = [], []
-    for g, pair in enumerate(gram_rows(v, range(1, width // LANES))):
+    for g, pair in enumerate(gram_rows(blocks)):
         at = g * COLS
         pair = pair_add(pair, (partial[at:at + COLS], partial[size + at:size + at + COLS]))
         high.append(pair[0])
@@ -484,15 +493,25 @@
     gram, vectors, vectors_last, zonal, meridional, levels, zonal_next, meridional_next, height
 ):
     x = coefficients(gram)
-    total = []
-    for part in (vectors, vectors_last):
-        at = [x[j:j + 1, :1] * part[j * EXT:(j + 1) * EXT] for j in range(ITERS)]
-        total.append(sum(at[1:], at[0]))
-    total = jnp.concatenate(total, axis=1)
-    own = total[COLS:2 * COLS, :NY]
-    height[...] = own
-    east = gravity * (roll(total, -1, 0)[COLS:2 * COLS, :NY] - own)
-    north = gravity * (roll(total, -1, 1)[COLS:2 * COLS, :NY] - own)
+
+    def combine(part):
+        terms = [x[j:j + 1, :1] * part[j * EXT:(j + 1) * EXT] for j in range(ITERS)]
+        return sum(terms[1:], terms[0])
+
+    total, window = combine(vectors), combine(vectors_last)
+    near = iota((COLS, LANES), 1) >= CUT - (NY - LANES)
+
+    def finished(value, from_window):
+        value = value[COLS:2 * COLS]
+        moved = roll(from_window[COLS:2 * COLS], COLS, 1)
+        last = jnp.where(near, moved, value[:, NY - LANES:])
+        return jnp.concatenate([value[:, :NY - LANES], last], axis=1)
+
+    def step(axis):
+        return gravity * finished(roll(total, -1, axis) - total, roll(window, -1, axis) - window)
+
+    height[...] = finished(total, window)
+    east, north = step(0), step(1)
     lc = levels[...]
     for k in range(K):
         zonal_next[k] = zonal[k] - jnp.where(lc > k, east, 0.0)
@@ -625,15 +644,15 @@
     )
     mirror = permute(near, mirrored)
     mirror_far = permute(far, mirrored_far)
-    last_rows = (EXT, NY - NEAR + LANES)
+    window = (EXT, LANES)
     last, last_code, vectors, partial = call(
         inner_kernel,
-        [last_rows, last_rows, (ITERS * EXT, NEAR), (2 * GROUPS * COLS, LANES)],
+        [window, window, (ITERS * EXT, NY), (2 * GROUPS * COLS, LANES)],
         outer, beyond, forcing, coded, flops=8192 * 100,
     )
     vectors_last, gram = call(
         fold_kernel,
-        [(ITERS * EXT, NY - NEAR + LANES), (size, LANES)],
+        [(ITERS * EXT, LANES), (size, LANES)],
         last, last_code, beyond, tile, mirror, mirror_far, partial,
     )
     halos = (sibling, beyond, mirror)

time: 26.3 us -> 26.3 us (level)
  no operation moved by 1% of the time
where the time goes in v8:
time: 26.3 us; the launch traced here: 26.1 us
  starting transfers between devices  11.8 us (45%)
  Pallas kernels  7.51 us (29%)
  waiting for transfers between devices  6.05 us (23%)
  between operations  0.7 us (3%)
    pallas_call x7, Pallas kernels, call(): pl.pallas_call(kernel, out_shape=[jax.ShapeDtypeStruct(s, f32) for s in s...  7.51 us
    ppermute x4, starting transfers between devices, permute(): return lax.ppermute(value, 'lon', pairs)  7.47 us
    all_to_all x1, starting transfers between devices, body(): lax.all_to_all(gram, 'lon', 0, 0, tiled=True, axis_index_groups=[group])  4.31 us
    ppermute x4, waiting for transfers between devices, permute(): return lax.ppermute(value, 'lon', pairs)  3.78 us
    all_to_all x1, waiting for transfers between devices, body(): lax.all_to_all(gram, 'lon', 0, 0, tiled=True, axis_index_groups=[group])  2.27 us
  transfers between devices with their start and end apart: 5, of which 3 were waited for; matrix products, arithmetic and copies ran while one was open for 0% of the time, Pallas kernels for 10%

profile of v8, /device:TPU:0, one launch (start us, length us, event | category | flops | bytes accessed | tf_op | source)
XLA Modules:
  0.0 26.1 jit_solution(8770149783384891356)
XLA Ops:
  0.6 1.6 %shard_map.93 = (f32[80,512]{1,0:T(8,128)S(1)}, f32[80,512]{1,0:T(8,128)S(1)}) custom-call(f32[16,8,512]{2,1,0:T(8,128)} %tracer.1, f32[16,8,512]{2,1,0:T(8,128)} %zonal.3, f32[16,8,512]{2,1,0:T(8,128)} %meridional.3, s32[8,512]{1,0:T(8,128)} %count.3, f32[8,512]{1,0:T(8,128)} %diffusivity.3, f32[8,512]{1,0:T(8,128)} %surface_in.1), custom_call_target="tpu_custom_call" | custom-call | bytes 1163264 | tf_op jit(solution)/shard_map/pallas_call | solution.py:610
  2.2 0.5 %collective-permute-start = (f32[80,512]{1,0:T(8,128)S(1)}, f32[80,512]{1,0:T(8,128)S(1)}, u32[]{:S(2)}, u32[]{:S(2)}) collective-permute-start(f32[80,512]{1,0:T(8,128)S(1)} %get-tuple-element.23.inner), channel_id=1, source_target_pairs={{0,1},{1,0},{2,3},{3,2},{4,5},{5,4},{6,7},{7,6},{8,9},{9,8},{10,11... | collective-permute-start | bytes 491528 | tf_op jit(solution)/shard_map/ppermute | solution.py:626
  2.8 5.7 %collective-permute-start.1 = (f32[80,512]{1,0:T(8,128)S(1)}, f32[80,512]{1,0:T(8,128)S(1)}, u32[]{:S(2)}, u32[]{:S(2)}) collective-permute-start(f32[80,512]{1,0:T(8,128)S(1)} %get-tuple-element.24.outer), channel_id=1, source_target_pairs={{0,15},{1,2},{2,1},{3,4},{4,3},{5,6},{6,5},{7,8},{8,7},{9,10},{10,... | collective-permute-start | bytes 491528 | tf_op jit(solution)/shard_map/ppermute | solution.py:626
  8.4 0.0 collective-permute-done.sibling
  8.4 0.0 copy-start.2
  8.4 0.1 shard_map.94
  8.6 1.1 %collective-permute-start.2 = (f32[16,128]{1,0:T(8,128)S(1)}, f32[16,128]{1,0:T(8,128)S(1)}, u32[]{:S(2)}, u32[]{:S(2)}) collective-permute-start(f32[16,128]{1,0:T(8,128)S(1)} %get-tuple-element.25), channel_id=1, source_target_pairs={{0,15},{1,14},{2,13},{3,12},{4,11},{5,10},{6,9},{7,8},{8,7},{9,6},... | collective-permute-start | bytes 24584 | tf_op jit(solution)/shard_map/ppermute | solution.py:626
  9.7 0.2 collective-permute-start.3
  9.9 1.7 %collective-permute-done.1.beyond = f32[80,512]{1,0:T(8,128)S(1)} collective-permute-done((f32[80,512]{1,0:T(8,128)S(1)}, f32[80,512]{1,0:T(8,128)S(1)}, u32[]{:S(2)}, u32[]{:S(2)}) %collective-permute-start.1) | collective-permute-done | bytes 163872 | tf_op jit(solution)/shard_map/ppermute | solution.py:626
  11.5 0.0 copy-start
  11.5 0.0 copy-start.1
  11.5 0.8 %shard_map.96 = (f32[24,128]{1,0:T(8,128)S(1)}, f32[24,128]{1,0:T(8,128)S(1)}, f32[144,512]{1,0:T(8,128)S(1)}, f32[64,128]{1,0:T(8,128)S(1)}) custom-call(f32[80,512]{1,0:T(8,128)S(1)} %get-tuple-element.24.outer, f32[80,512]{1,0:T(8,128)S(1)} %collective-permute-done.1.beyond, f32[16,512]{1,0:T(8,128)S(1)} %get-tuple-element.26.forcing, ...), custom_call_target="tpu_custom_call" | custom-call | flops 819200 | bytes 745472 | tf_op jit(solution)/shard_map/pallas_call | solution.py:610
  12.3 2.1 %collective-permute-done.2.mirror = f32[16,128]{1,0:T(8,128)S(1)} collective-permute-done((f32[16,128]{1,0:T(8,128)S(1)}, f32[16,128]{1,0:T(8,128)S(1)}, u32[]{:S(2)}, u32[]{:S(2)}) %collective-permute-start.2) | collective-permute-done | bytes 8224 | tf_op jit(solution)/shard_map/ppermute | solution.py:626
  14.4 0.0 collective-permute-done.3.mirror_far
  14.4 0.0 copy-start.4
  14.4 1.6 %shard_map.97 = (f32[144,128]{1,0:T(8,128)S(1)}, f32[16,128]{1,0:T(8,128)}) custom-call(f32[24,128]{1,0:T(8,128)S(1)} %get-tuple-element.28.last, f32[24,128]{1,0:T(8,128)S(1)} %get-tuple-element.29.last_code, f32[80,512]{1,0:T(8,128)S(1)} %collective-permute-done.1.beyond, f32[16,128]{1,0:T(8,128)S(1)} %get-tuple-element.30.tile, ...), custom_call_target="tpu_custom_call" | custom-call | bytes 327680 | tf_op jit(solution)/shard_map/pallas_call | solution.py:610
  16.0 0.0 copy-start.3
  16.0 4.3 %all-to-all-start = ((f32[16,1,128]{2,1,0:T(1,128)}), f32[16,1,128]{2,1,0:T(1,128)S(1)}, u32[]{:S(2)}, u32[]{:S(2)}) async-start(f32[16,1,128]{2,1,0:T(1,128)} %bitcast.1), calls=%async_computation | async-start | bytes 16384 | tf_op jit(solution)/shard_map/all_to_all | solution.py:670
  20.4 0.0 copy-done.2
  20.4 0.0 copy-done
  20.4 0.0 copy-done.1
  20.4 0.0 copy-done.4
  20.4 0.0 copy-done.3
  20.4 1.2 %shard_map.95 = f32[16,8,512]{2,1,0:T(8,128)} custom-call(f32[16,8,512]{2,1,0:T(8,128)S(1)} %copy-done.2, f32[16,8,512]{2,1,0:T(8,128)S(1)} %copy-done, f32[16,8,512]{2,1,0:T(8,128)S(1)} %copy-done.1, s32[8,512]{1,0:T(8,128)S(1)} %copy-done.3, f32[8,512]{1,0:T(8,128)S(1)} %copy-done.4, f32[80,512]{1,0:T(8,128)S(1)} %collective-permute-done.sibling, ...), custom_call_target="tpu_custom_call" | custom-call | flops 2621440 | bytes 1417216 | tf_op jit(solution)/shard_map/pallas_call | solution.py:610
  21.6 0.6 %shard_map.98 = (f32[16,8,512]{2,1,0:T(8,128)S(1)}, f32[16,8,512]{2,1,0:T(8,128)S(1)}, f32[8,512]{1,0:T(8,128)S(1)}) custom-call(f32[16,8,512]{2,1,0:T(8,128)S(1)} %copy-done, f32[16,8,512]{2,1,0:T(8,128)S(1)} %copy-done.1, s32[8,512]{1,0:T(8,128)S(1)} %copy-done.3, f32[8,512]{1,0:T(8,128)S(1)} %copy-done.4, f32[80,512]{1,0:T(8,128)S(1)} %collective-permute-done.sibling, ...), custom_call_target="tpu_custom_call" | custom-call | flops 2621440 | bytes 1433600 | tf_op jit(solution)/shard_map/pallas_call | solution.py:610
  22.2 2.3 %all-to-all-done = f32[16,1,128]{2,1,0:T(1,128)S(1)} async-done(((f32[16,1,128]{2,1,0:T(1,128)}), f32[16,1,128]{2,1,0:T(1,128)S(1)}, u32[]{:S(2)}, u32[]{:S(2)}) %all-to-all-start) | async-done | bytes 8224 | tf_op jit(solution)/shard_map/all_to_all | solution.py:670
  24.4 1.6 %shard_map.99 = (f32[16,8,512]{2,1,0:T(8,128)}, f32[16,8,512]{2,1,0:T(8,128)}, f32[8,512]{1,0:T(8,128)}) custom-call(f32[16,128]{1,0:T(8,128)S(1)} %bitcast.4, f32[144,512]{1,0:T(8,128)S(1)} %get-tuple-element.34.vectors, f32[144,128]{1,0:T(8,128)S(1)} %get-tuple-element.35.vectors_last, f32[16,8,512]{2,1,0:T(8,128)S(1)} %get-tuple-element.36.zonal, ...), custom_call_target="tpu_custom_call" | custom-call | bytes 1458176 | tf_op jit(solution)/shard_map/pallas_call | solution.py:610
Async XLA Ops:
  2.2 6.2 %collective-permute-start = (f32[80,512]{1,0:T(8,128)S(1)}, f32[80,512]{1,0:T(8,128)S(1)}, u32[]{:S(2)}, u32[]{:S(2)}) collective-permute-start(f32[80,512]{1,0:T(8,128)S(1)} %get-tuple-element.23.inner), channel_id=1, source_target_pairs={{0,1},{1,0},{2,3},{3,2},{4,5},{5,4},{6,7},{7,6},{8,9},{9,8},{10,11... | collective-permute-start | bytes 491528 | tf_op jit(solution)/shard_map/ppermute | solution.py:626
  2.8 8.8 %collective-permute-start.1 = (f32[80,512]{1,0:T(8,128)S(1)}, f32[80,512]{1,0:T(8,128)S(1)}, u32[]{:S(2)}, u32[]{:S(2)}) collective-permute-start(f32[80,512]{1,0:T(8,128)S(1)} %get-tuple-element.24.outer), channel_id=1, source_target_pairs={{0,15},{1,2},{2,1},{3,4},{4,3},{5,6},{6,5},{7,8},{8,7},{9,10},{10,... | collective-permute-start | bytes 491528 | tf_op jit(solution)/shard_map/ppermute | solution.py:626
  8.4 11.9 %copy-start.2 = (f32[16,8,512]{2,1,0:T(8,128)S(1)}, f32[16,8,512]{2,1,0:T(8,128)}, u32[]{:S(2)}) copy-start(f32[16,8,512]{2,1,0:T(8,128)} %tracer.1) | copy-start | bytes 786436
  8.6 5.8 %collective-permute-start.2 = (f32[16,128]{1,0:T(8,128)S(1)}, f32[16,128]{1,0:T(8,128)S(1)}, u32[]{:S(2)}, u32[]{:S(2)}) collective-permute-start(f32[16,128]{1,0:T(8,128)S(1)} %get-tuple-element.25), channel_id=1, source_target_pairs={{0,15},{1,14},{2,13},{3,12},{4,11},{5,10},{6,9},{7,8},{8,7},{9,6},... | collective-permute-start | bytes 24584 | tf_op jit(solution)/shard_map/ppermute | solution.py:626
  9.7 4.8 %collective-permute-start.3 = (f32[16,128]{1,0:T(8,128)S(1)}, f32[16,128]{1,0:T(8,128)S(1)}, u32[]{:S(2)}, u32[]{:S(2)}) collective-permute-start(f32[16,128]{1,0:T(8,128)S(1)} %get-tuple-element.31), channel_id=1, source_target_pairs={{1,0},{12,1},{15,2},{10,3},{13,4},{8,5},{11,6},{6,7},{9,8},{4,9},{... | collective-permute-start | bytes 24584 | tf_op jit(solution)/shard_map/ppermute | solution.py:626
  11.5 8.8 %copy-start = (f32[16,8,512]{2,1,0:T(8,128)S(1)}, f32[16,8,512]{2,1,0:T(8,128)}, u32[]{:S(2)}) copy-start(f32[16,8,512]{2,1,0:T(8,128)} %zonal.3) | copy-start | bytes 786436
  11.5 8.8 %copy-start.1 = (f32[16,8,512]{2,1,0:T(8,128)S(1)}, f32[16,8,512]{2,1,0:T(8,128)}, u32[]{:S(2)}) copy-start(f32[16,8,512]{2,1,0:T(8,128)} %meridional.3) | copy-start | bytes 786436
  14.4 6.0 %copy-start.4 = (f32[8,512]{1,0:T(8,128)S(1)}, f32[8,512]{1,0:T(8,128)}, u32[]{:S(2)}) copy-start(f32[8,512]{1,0:T(8,128)} %diffusivity.3) | copy-start | bytes 49156
  16.0 4.4 %copy-start.3 = (s32[8,512]{1,0:T(8,128)S(1)}, s32[8,512]{1,0:T(8,128)}, u32[]{:S(2)}) copy-start(s32[8,512]{1,0:T(8,128)} %count.3) | copy-start | bytes 49156
  16.0 8.4 %all-to-all-start = ((f32[16,1,128]{2,1,0:T(1,128)}), f32[16,1,128]{2,1,0:T(1,128)S(1)}, u32[]{:S(2)}, u32[]{:S(2)}) async-start(f32[16,1,128]{2,1,0:T(1,128)} %bitcast.1), calls=%async_computation | async-start | bytes 16384 | tf_op jit(solution)/shard_map/all_to_all | solution.py:670

commit v9 on v8

--- a/solution.py
+++ b/solution.py
@@ -13,7 +13,6 @@
 COLS = 8
 EXT = 3 * COLS
 LANES = 128
-PACK = 80
 BASIS = ITERS + 1
 CUT = NY - COLS
 GROUPS = (BASIS * (BASIS + 1) // 2 + COLS - 1) // COLS
@@ -33,6 +32,7 @@
 LANE_MU = 56
 LANE_MV = 72
 LANE_EDGE = 88
+WIDE = 32
 LANE_CODE = LANES - 2 * COLS
 LANE_F = LANES - COLS
 
@@ -136,7 +136,8 @@
 
 
 def pack_kernel(
-    tracer_in, zonal_in, meridional_in, count_in, diffusivity_in, surface_in, inner, outer,
+    tracer_in, zonal_in, meridional_in, count_in, diffusivity_in, surface_in,
+    inner, outer,
     tracer, zonal, meridional, count, diffusivity, surface, edges, sems,
 ):
     shape = (COLS, NY)
@@ -207,6 +208,7 @@
     fold = jnp.where(tile_lane == LANE_LC, lc_fold, fold)
     fold = jnp.where(tile_lane == LANE_DIFF, diff[:, NY - 1:], fold)
     edge_level = iota((K, NY), 0).astype(f32)
+
     for copy in rows:
         copy.wait()
     for base in range(3):
@@ -227,6 +229,7 @@
     edge = jnp.zeros((K, LANES), f32)
     edge_lane = iota((K, LANES), 1)
     p = outer[32:48, NY - LANES:] + outer[48:64, NY - LANES:]
+    sub = iota((COLS, LANES), 0)
     edge_lc = jnp.where(even, lc[:1], lc[COLS - 1:])
     edge_diff = jnp.where(even, diff[:1], diff[COLS - 1:])
     for j in range(COLS):
@@ -235,54 +238,84 @@
         edge = jnp.where(edge_lane == here, p[:, LANES - 1 - j:LANES - j], edge)
         edge = jnp.where(edge_lane == here + COLS, edge_lc[:, at:at + 1], edge)
         edge = jnp.where(edge_lane == here + 2 * COLS, edge_diff[:, at:at + 1], edge)
-    edge = [edge[:COLS], edge[COLS:]]
-    zeros = jnp.zeros((COLS, NY - 3 * LANES), f32)
-    for pack, mine, other in ((inner, COLS - 1, 0), (outer, 0, COLS - 1)):
-        pack[0:COLS] = forcing
-        pack[COLS:2 * COLS] = coded
-        edge_lc = jnp.where(even, lc[mine:mine + 1], lc[other:other + 1])
-        edge_diff = jnp.where(even, diff[mine:mine + 1], diff[other:other + 1])
-        pack[64:72] = jnp.where(row == 0, edge_lc, jnp.where(row == 1, edge_diff, 0.0))
-        pack[72:80] = jnp.concatenate([fold, *edge, zeros], axis=1)
-
-
-def interface_flux(mine, theirs):
-    level = iota((K, NY), 0).astype(f32)
+    blank = jnp.zeros((COLS, NY - 3 * LANES), f32)
+    inner[72:80] = jnp.concatenate([fold, edge[:COLS], edge[COLS:], blank], axis=1)
+    inner[0:COLS] = forcing
+    inner[COLS:2 * COLS] = coded
+    mine_lc = jnp.where(even, lc[COLS - 1:], lc[:1])
+    mine_diff = jnp.where(even, diff[COLS - 1:], diff[:1])
+    inner[64:72] = jnp.where(row == 0, mine_lc, jnp.where(row == 1, mine_diff, 0.0))
+    far, next_far = jnp.where(even, COLS - 1, 0), jnp.where(even, COLS - 2, 1)
+    used = jnp.where((tile_lane >= LANE_P) & (tile_lane < LANE_P + WIDE), fold, 0.0)
+    moved = [
+        jnp.sum(
+            sum(
+                jnp.where(sub == x, roll(used, (x - first) * WIDE - LANE_P, 1), 0.0)
+                for x in range(first, first + LANES // WIDE)
+            ),
+            axis=0, keepdims=True,
+        )
+        for first in range(0, COLS, LANES // WIDE)
+    ]
+    tile_row = jnp.concatenate(moved + [jnp.zeros((1, NY - len(moved) * LANES), f32)], axis=1)
+    outer[0:COLS] = jnp.where(row == far, edge_lc, jnp.where(row == next_far, tile_row, forcing))
+    outer[COLS:2 * COLS] = jnp.where(row == far, edge_diff, coded)
+
+
+def far_rows(pack, far, next_far):
+    tile_row = jnp.where(next_far == 1, pack[1:2], pack[COLS - 2:COLS - 1])
+    sub = iota((COLS, LANES), 0)
+    tile = jnp.zeros((COLS, LANES), f32)
+    for x in range(COLS):
+        block, place = divmod(x * WIDE, LANES)
+        piece = tile_row[:, block * LANES:(block + 1) * LANES]
+        tile = jnp.where(sub == x, roll(piece, LANE_P - place, 1), tile)
+    return (
+        jnp.where(far == 0, pack[0:1], pack[COLS - 1:COLS]),
+        jnp.where(far == 0, pack[COLS:COLS + 1], pack[2 * COLS - 1:2 * COLS]),
+        tile,
+    )
+
+
+def interface_flux(mine, theirs, lc_mine, lc_theirs):
     p_mine = mine[32:48] + mine[48:64]
     p_theirs = theirs[32:48] + theirs[48:64]
+    level = iota(p_mine.shape, 0).astype(f32)
     return level_sum(
-        jnp.where(level < mine[64:65], p_theirs, 0.0)
-        - jnp.where(level < theirs[64:65], p_mine, 0.0)
-    )
-
-
-def is_even():
-    return lax.axis_index("lon") % 2 == 0
-
-
-def beside(even, west, east):
-    return jnp.concatenate([jnp.where(even, west, east), jnp.where(even, east, west)], axis=0)
-
-
-def chip_kernel(inner, sibling, forcing, coded, tile, near, far):
-    even = is_even()
-    flux = interface_flux(inner, sibling)
+        jnp.where(level < lc_mine, p_theirs, 0.0) - jnp.where(level < lc_theirs, p_mine, 0.0)
+    )
+
+
+def chip_forcing(even, inner, sibling):
+    flux = interface_flux(inner, sibling, inner[64:65], sibling[64:65])
     own, other = inner[65:66] * flux, -sibling[65:66] * flux
-    row = iota((2 * COLS, NY), 0)
+    row = iota((2 * COLS, flux.shape[1]), 0)
     change = jnp.where(
         row == COLS - 1,
         jnp.where(even, own, other),
         jnp.where(row == COLS, jnp.where(even, other, own), 0.0),
     )
-    full = beside(even, inner[:COLS], sibling[:COLS]) + change
-    code = beside(even, inner[COLS:2 * COLS], sibling[COLS:2 * COLS])
+    return beside(even, inner[:COLS], sibling[:COLS]) + change
+
+
+def is_even():
+    return lax.axis_index("lon") % 2 == 0
+
+
+def beside(even, west, east):
+    return jnp.concatenate([jnp.where(even, west, east), jnp.where(even, east, west)], axis=0)
+
+
+def chip_kernel(inner, sibling, tile, near, far):
+    even = is_even()
+    ours, theirs = (pack[:72, NY - LANES:] for pack in (inner, sibling))
+    full = chip_forcing(even, ours, theirs)
+    code = beside(even, ours[COLS:2 * COLS], theirs[COLS:2 * COLS])
     fold = beside(even, inner[72:80, :LANES], sibling[72:80, :LANES])
-    forcing[...] = full
-    coded[...] = code
     tile[...] = fold
     lane = iota((2 * COLS, LANES), 1)
     for j in range(COLS):
-        at = NY - 1 - j
+        at = LANES - 1 - j
         fold = jnp.where(lane == LANE_F + j, full[:, at:at + 1], fold)
         fold = jnp.where(lane == LANE_CODE + j, code[:, at:at + 1], fold)
     fold = jnp.concatenate(
@@ -359,16 +392,23 @@
     return [pair_pack(entries[g:g + COLS]) for g in range(0, len(entries), COLS)]
 
 
-def inner_kernel(outer, beyond, forcing, coded, last, last_code, vectors, partial):
+def inner_kernel(
+    inner, outer, sibling, beyond, last, last_code, vectors, partial, far_tile,
+):
     even = is_even()
-    flux_out = interface_flux(outer, beyond)
-    own, far = outer[65:66] * flux_out, -beyond[65:66] * flux_out
+    forcing = chip_forcing(even, inner, sibling)
+    coded = beside(even, inner[COLS:2 * COLS], sibling[COLS:2 * COLS])
+    at_east, at_west = jnp.where(even, 0, COLS - 1), jnp.where(even, COLS - 1, 0)
+    lc_out, diff_out, _ = far_rows(outer, at_west, jnp.where(even, COLS - 2, 1))
+    lc_far, diff_far, far_tile[...] = far_rows(beyond, at_east, jnp.where(even, 1, COLS - 2))
+    flux_out = interface_flux(outer, beyond, lc_out, lc_far)
+    own, far = diff_out * flux_out, -diff_far * flux_out
     row = iota((EXT, NY), 0)
     west = jnp.where(row == COLS - 1, far, jnp.where(row == COLS, own, 0.0))
     east = jnp.where(row == 2 * COLS - 1, own, jnp.where(row == 2 * COLS, far, 0.0))
     far_forcing, far_code = beyond[:COLS], beyond[COLS:2 * COLS]
-    south = extend(even, far_forcing, forcing[...], far_forcing) + jnp.where(even, west, east)
-    code = extend(even, far_code, coded[...], far_code)
+    south = extend(even, far_forcing, forcing, far_forcing) + jnp.where(even, west, east)
+    code = extend(even, far_code, coded, far_code)
     last[...] = roll(south[:, NY - LANES:], -COLS, 1)
     last_code[...] = roll(code[:, NY - LANES:], -COLS, 1)
     v = basis(south, code)
@@ -385,11 +425,10 @@
             partial[at + g * COLS:at + (g + 1) * COLS] = part
 
 
-def fold_kernel(last, last_code, beyond, tile, mirror, mirror_far, partial, vectors, gram):
+def fold_kernel(last, last_code, far_tile, tile, mirror, mirror_far, partial, vectors, gram):
     even = is_even()
     lane = iota((EXT, LANES), 1)
-    mine = beyond[72:80, :LANES]
-    mine = extend(even, mine, tile[...], mine)
+    mine = extend(even, far_tile[...], tile[...], far_tile[...])
     theirs, between = across_fold(even, mirror[...], mirror_far[...])
     level = (lane - LANE_P).astype(f32)
     weight = jnp.where((lane >= LANE_P) & (lane < LANE_P + K), 0.5 * (0.5 + level / K), 0.0)
@@ -441,51 +480,66 @@
         )
 
     matrix = [column(j) for j in range(BASIS)]
-    first = (sub == 0).astype(f32)
     zero = jnp.zeros(shape, f32)
+    half = scale / 2
+
+    def times_power(pair, factor):
+        return tuple(factor * part for part in pair)
+
+    def shifted(pair):
+        return pair_add(times_power(pair, shift - 1.0), pair)
 
     def apply(b):
-        half = scale / 2
         up = [half * jnp.where(sub == 0, 0.0, roll(part, 1, 0)) for part in b]
-        up = [jnp.where(sub == 1, 2.0 * part, part) for part in up]
-        down = [half * jnp.where(sub == COLS - 1, 0.0, roll(part, -1, 0)) for part in b]
-        four = tuple(4.0 * part for part in b)
-        return pair_add(pair_add(four, b), pair_add(tuple(up), tuple(down)))
-
-    def times(vector, count):
+        up = tuple(jnp.where(sub == 1, 2.0 * part, part) for part in up)
+        down = tuple(half * jnp.where(sub == COLS - 1, 0.0, roll(part, -1, 0)) for part in b)
+        return pair_add(shifted(b), pair_add(up, down))
+
+    images = [pair_add(shifted(matrix[0]), times_power(matrix[1], scale))]
+    for j in range(1, ITERS):
+        sides = pair_add(matrix[j - 1], matrix[j + 1])
+        images.append(pair_add(shifted(matrix[j]), times_power(sides, half)))
+
+    def image_of(vector, count):
         terms = []
         for j in range(count):
             at = tuple(wide(part[j:j + 1]) for part in vector)
-            terms.append(pair_mul(matrix[j], at))
+            terms.append(pair_mul(images[j], at))
         return pair_tree(terms)
 
     def dot(a, b):
-        s = pair_rows(pair_mul(a, b))
-        return s[0] + s[1]
-
-    residual = (first, zero)
-    image = matrix[0]
+        return pair_rows(pair_mul(a, b))
+
+    residual = ((sub == 0).astype(f32), zero)
     direction = residual
     solution = zero
-    norm_now = wide(matrix[0][0][:1])
-    floor = 1e-13 * norm_now
-    alive = norm_now > 0
+    norm_now = tuple(wide(part[:1]) for part in matrix[0])
+    floor = 1e-13 * norm_now[0]
+    alive = norm_now[0] > 0
     for iteration in range(ITERS):
         applied = apply(direction)
-        applied_image = times(applied, iteration + 2)
-        curvature = dot(direction, applied_image)
-        alive = alive & (curvature > 0)
-        step = jnp.where(alive, norm_now / jnp.where(alive, curvature, 1.0), 0.0)
+        if iteration == 0:
+            image = images[0]
+            curvature = tuple(wide(part[:1]) for part in image)
+        else:
+            image = image_of(direction, iteration + 1)
+            curvature = dot(direction, image)
+        size = curvature[0] + curvature[1]
+        alive = alive & (size > 0)
+        step = jnp.where(alive, (norm_now[0] + norm_now[1]) / jnp.where(alive, size, 1.0), 0.0)
         solution = solution + step * direction[0]
         if iteration + 1 < ITERS:
-            back = -step
-            residual = pair_norm(pair_add(residual, pair_scale(applied, back)))
-            image = pair_norm(pair_add(image, pair_scale(applied_image, back)))
-            norm_next = dot(residual, image)
-            ratio = jnp.where(alive, norm_next / jnp.where(alive, norm_now, 1.0), 0.0)
+            crossed = curvature if iteration == 0 else dot(residual, image)
+            squared = dot(applied, image)
+            change = pair_add(
+                pair_scale(squared, step), times_power(crossed, -2.0)
+            )
+            norm_next = pair_norm(pair_add(norm_now, pair_scale(pair_norm(change), step)))
+            residual = pair_norm(pair_add(residual, pair_scale(applied, -step)))
+            ratio = jnp.where(alive, norm_next[0] / jnp.where(alive, norm_now[0], 1.0), 0.0)
             direction = pair_norm(pair_add(residual, pair_scale(direction, ratio)))
             norm_now = norm_next
-            alive = alive & (norm_now > floor)
+            alive = alive & (norm_now[0] > floor)
     return solution
 
 
@@ -533,15 +587,18 @@
             jnp.where(lane == 0, 0.0, roll(field, 1, 1)),
         )
 
+    def sides(a, b):
+        return jnp.where(even, b, a), jnp.where(even, a, b)
+
     def edges(at):
-        a, b = sibling[at:at + 1], beyond[at:at + 1]
-        return jnp.where(even, b, a), jnp.where(even, a, b)
+        return sides(sibling[at:at + 1], beyond[at:at + 1])
 
     def padded(field, base, k, sign):
         at = LANE_MT + base * K + k
         return around(field, *edges(2 * COLS + base * K + k), sign * north_tile[:, at:at + 1])
 
-    west_lc, east_lc = edges(64)
+    beyond_lc = jnp.where(even, beyond[0:1], beyond[COLS - 1:COLS])
+    west_lc, east_lc = sides(sibling[64:65], beyond_lc)
     north_lc = north_tile[:, LANE_LC:LANE_LC + 1]
 
     def mask_sum(mask, k):
@@ -631,29 +688,29 @@
     mirrored_far = [((size + 1 - 4 * (i % 2) - i) % size, i) for i in range(size)]
     arguments = (tracer, zonal, meridional, count, diffusivity, surface)
     inner, outer = call(
-        pack_kernel, [(PACK, NY)] * 2, *arguments,
+        pack_kernel, [(80, NY), (64, NY)], *arguments,
         scratch=[pltpu.VMEM((K, COLS, LANES), f32)]
         + [pltpu.VMEM(a.shape, a.dtype) for a in arguments[1:]]
         + [pltpu.VMEM((6, K, NY), f32), pltpu.SemaphoreType.DMA((9 + 3 * CHUNKS,))], stay=len(arguments),
     )
     beyond = permute(outer, outward)
     sibling = permute(inner, siblings)
-    chip = (2 * COLS, NY)
-    forcing, coded, tile, near, far = call(
-        chip_kernel, [chip, chip] + [(2 * COLS, LANES)] * 3, inner, sibling
-    )
+    patch = (2 * COLS, LANES)
+    tile, near, far = call(chip_kernel, [patch] * 3, inner, sibling)
     mirror = permute(near, mirrored)
     mirror_far = permute(far, mirrored_far)
     window = (EXT, LANES)
-    last, last_code, vectors, partial = call(
+    last, last_code, vectors, partial, far_tile = call(
         inner_kernel,
-        [window, window, (ITERS * EXT, NY), (2 * GROUPS * COLS, LANES)],
-        outer, beyond, forcing, coded, flops=8192 * 100,
+        [
+            window, window, (ITERS * EXT, NY), (2 * GROUPS * COLS, LANES), (COLS, LANES),
+        ],
+        inner, outer, sibling, beyond, flops=8192 * 100,
     )
     vectors_last, gram = call(
         fold_kernel,
         [(ITERS * EXT, LANES), (size, LANES)],
-        last, last_code, beyond, tile, mirror, mirror_far, partial,
+        last, last_code, far_tile, tile, mirror, mirror_far, partial,
     )
     halos = (sibling, beyond, mirror)
     tracer_next, = call(

time: 26.3 us -> 26.2 us (level)
  no operation moved by 1% of the time
where the time goes in v9:
time: 26.2 us; the launch traced here: 26 us
  starting transfers between devices  11.8 us (45%)
  Pallas kernels  7.42 us (28%)
  waiting for transfers between devices  6.03 us (23%)
  between operations  0.7 us (3%)
    ppermute x4, starting transfers between devices, permute(): return lax.ppermute(value, 'lon', pairs)  7.47 us
    pallas_call x7, Pallas kernels, call(): pl.pallas_call(kernel, out_shape=[jax.ShapeDtypeStruct(s, f32) for s in s...  7.42 us
    all_to_all x1, starting transfers between devices, body(): lax.all_to_all(gram, 'lon', 0, 0, tiled=True, axis_index_groups=[group])  4.32 us
    ppermute x4, waiting for transfers between devices, permute(): return lax.ppermute(value, 'lon', pairs)  3.77 us
    all_to_all x1, waiting for transfers between devices, body(): lax.all_to_all(gram, 'lon', 0, 0, tiled=True, axis_index_groups=[group])  2.27 us
  transfers between devices with their start and end apart: 5, of which 3 were waited for; matrix products, arithmetic and copies ran while one was open for 0% of the time, Pallas kernels for 10%

profile of v9, /device:TPU:0, one launch (start us, length us, event | category | flops | bytes accessed | tf_op | source)
XLA Modules:
  0.0 26.0 jit_solution(2993053878904297383)
XLA Ops:
  0.6 1.6 %shard_map.93 = (f32[80,512]{1,0:T(8,128)S(1)}, f32[64,512]{1,0:T(8,128)S(1)}) custom-call(f32[16,8,512]{2,1,0:T(8,128)} %tracer.1, f32[16,8,512]{2,1,0:T(8,128)} %zonal.3, f32[16,8,512]{2,1,0:T(8,128)} %meridional.3, s32[8,512]{1,0:T(8,128)} %count.3, f32[8,512]{1,0:T(8,128)} %diffusivity.3, f32[8,512]{1,0:T(8,128)} %surface_in.1), custom_call_target="tpu_custom_call" | custom-call | bytes 1130496 | tf_op jit(solution)/shard_map/pallas_call | solution.py:667
  2.2 0.5 %collective-permute-start = (f32[80,512]{1,0:T(8,128)S(1)}, f32[80,512]{1,0:T(8,128)S(1)}, u32[]{:S(2)}, u32[]{:S(2)}) collective-permute-start(f32[80,512]{1,0:T(8,128)S(1)} %get-tuple-element.22.inner), channel_id=1, source_target_pairs={{0,1},{1,0},{2,3},{3,2},{4,5},{5,4},{6,7},{7,6},{8,9},{9,8},{10,11... | collective-permute-start | bytes 491528 | tf_op jit(solution)/shard_map/ppermute | solution.py:683
  2.8 5.7 %collective-permute-start.1 = (f32[64,512]{1,0:T(8,128)S(1)}, f32[64,512]{1,0:T(8,128)S(1)}, u32[]{:S(2)}, u32[]{:S(2)}) collective-permute-start(f32[64,512]{1,0:T(8,128)S(1)} %get-tuple-element.23.outer), channel_id=1, source_target_pairs={{0,15},{1,2},{2,1},{3,4},{4,3},{5,6},{6,5},{7,8},{8,7},{9,10},{10,... | collective-permute-start | bytes 393224 | tf_op jit(solution)/shard_map/ppermute | solution.py:683
  8.4 0.0 collective-permute-done.sibling
  8.4 0.0 copy-start.2
  8.4 0.1 shard_map.94
  8.6 1.1 %collective-permute-start.2 = (f32[16,128]{1,0:T(8,128)S(1)}, f32[16,128]{1,0:T(8,128)S(1)}, u32[]{:S(2)}, u32[]{:S(2)}) collective-permute-start(f32[16,128]{1,0:T(8,128)S(1)} %get-tuple-element.24), channel_id=1, source_target_pairs={{0,15},{1,14},{2,13},{3,12},{4,11},{5,10},{6,9},{7,8},{8,7},{9,6},... | collective-permute-start | bytes 24584 | tf_op jit(solution)/shard_map/ppermute | solution.py:683
  9.7 0.0 copy-start
  9.7 0.0 copy-start.1
  9.7 0.2 collective-permute-start.3
  9.9 1.3 %collective-permute-done.1.beyond = f32[64,512]{1,0:T(8,128)S(1)} collective-permute-done((f32[64,512]{1,0:T(8,128)S(1)}, f32[64,512]{1,0:T(8,128)S(1)}, u32[]{:S(2)}, u32[]{:S(2)}) %collective-permute-start.1) | collective-permute-done | bytes 131104 | tf_op jit(solution)/shard_map/ppermute | solution.py:683
  11.2 0.8 %shard_map.96 = (f32[24,128]{1,0:T(8,128)S(1)}, f32[24,128]{1,0:T(8,128)S(1)}, f32[144,512]{1,0:T(8,128)S(1)}, f32[64,128]{1,0:T(8,128)S(1)}, f32[8,128]{1,0:T(8,128)S(1)}) custom-call(f32[80,512]{1,0:T(8,128)S(1)} %get-tuple-element.22.inner, f32[64,512]{1,0:T(8,128)S(1)} %get-tuple-element.23.outer, f32[80,512]{1,0:T(8,128)S(1)} %collective-permute-done.sibling, ...), custom_call_target="tpu_custom_call" | custom-call | flops 819200 | bytes 946176 | tf_op jit(solution)/shard_map/pallas_call | solution.py:667
  11.9 2.5 %collective-permute-done.2.mirror = f32[16,128]{1,0:T(8,128)S(1)} collective-permute-done((f32[16,128]{1,0:T(8,128)S(1)}, f32[16,128]{1,0:T(8,128)S(1)}, u32[]{:S(2)}, u32[]{:S(2)}) %collective-permute-start.2) | collective-permute-done | bytes 8224 | tf_op jit(solution)/shard_map/ppermute | solution.py:683
  14.4 0.0 collective-permute-done.3.mirror_far
  14.4 0.0 copy-start.4
  14.4 1.6 %shard_map.97 = (f32[144,128]{1,0:T(8,128)S(1)}, f32[16,128]{1,0:T(8,128)}) custom-call(f32[24,128]{1,0:T(8,128)S(1)} %get-tuple-element.25.last, f32[24,128]{1,0:T(8,128)S(1)} %get-tuple-element.26.last_code, f32[8,128]{1,0:T(8,128)S(1)} %get-tuple-element.27.far_tile, f32[16,128]{1,0:T(8,128)S(1)} %get-tuple-element.28.tile, ...), custom_call_target="tpu_custom_call" | custom-call | bytes 167936 | tf_op jit(solution)/shard_map/pallas_call | solution.py:667
  16.0 0.0 copy-start.3
  16.0 4.3 %all-to-all-start = ((f32[16,1,128]{2,1,0:T(1,128)}), f32[16,1,128]{2,1,0:T(1,128)S(1)}, u32[]{:S(2)}, u32[]{:S(2)}) async-start(f32[16,1,128]{2,1,0:T(1,128)} %bitcast.1), calls=%async_computation | async-start | bytes 16384 | tf_op jit(solution)/shard_map/all_to_all | solution.py:727
  20.4 0.0 copy-done.2
  20.4 0.0 copy-done
  20.4 0.0 copy-done.1
  20.4 0.0 copy-done.4
  20.4 0.0 copy-done.3
  20.4 1.2 %shard_map.95 = f32[16,8,512]{2,1,0:T(8,128)} custom-call(f32[16,8,512]{2,1,0:T(8,128)S(1)} %copy-done.2, f32[16,8,512]{2,1,0:T(8,128)S(1)} %copy-done, f32[16,8,512]{2,1,0:T(8,128)S(1)} %copy-done.1, s32[8,512]{1,0:T(8,128)S(1)} %copy-done.3, f32[8,512]{1,0:T(8,128)S(1)} %copy-done.4, f32[80,512]{1,0:T(8,128)S(1)} %collective-permute-done.sibling, ...), custom_call_target="tpu_custom_call" | custom-call | flops 2621440 | bytes 1384448 | tf_op jit(solution)/shard_map/pallas_call | solution.py:667
  21.6 0.6 %shard_map.98 = (f32[16,8,512]{2,1,0:T(8,128)S(1)}, f32[16,8,512]{2,1,0:T(8,128)S(1)}, f32[8,512]{1,0:T(8,128)S(1)}) custom-call(f32[16,8,512]{2,1,0:T(8,128)S(1)} %copy-done, f32[16,8,512]{2,1,0:T(8,128)S(1)} %copy-done.1, s32[8,512]{1,0:T(8,128)S(1)} %copy-done.3, f32[8,512]{1,0:T(8,128)S(1)} %copy-done.4, f32[80,512]{1,0:T(8,128)S(1)} %collective-permute-done.sibling, ...), custom_call_target="tpu_custom_call" | custom-call | flops 2621440 | bytes 1400832 | tf_op jit(solution)/shard_map/pallas_call | solution.py:667
  22.2 2.3 %all-to-all-done = f32[16,1,128]{2,1,0:T(1,128)S(1)} async-done(((f32[16,1,128]{2,1,0:T(1,128)}), f32[16,1,128]{2,1,0:T(1,128)S(1)}, u32[]{:S(2)}, u32[]{:S(2)}) %all-to-all-start) | async-done | bytes 8224 | tf_op jit(solution)/shard_map/all_to_all | solution.py:727
  24.4 1.5 %shard_map.99 = (f32[16,8,512]{2,1,0:T(8,128)}, f32[16,8,512]{2,1,0:T(8,128)}, f32[8,512]{1,0:T(8,128)}) custom-call(f32[16,128]{1,0:T(8,128)S(1)} %bitcast.4, f32[144,512]{1,0:T(8,128)S(1)} %get-tuple-element.32.vectors, f32[144,128]{1,0:T(8,128)S(1)} %get-tuple-element.33.vectors_last, f32[16,8,512]{2,1,0:T(8,128)S(1)} %get-tuple-element.34.zonal, ...), custom_call_target="tpu_custom_call" | custom-call | bytes 1458176 | tf_op jit(solution)/shard_map/pallas_call | solution.py:667
Async XLA Ops:
  2.2 6.2 %collective-permute-start = (f32[80,512]{1,0:T(8,128)S(1)}, f32[80,512]{1,0:T(8,128)S(1)}, u32[]{:S(2)}, u32[]{:S(2)}) collective-permute-start(f32[80,512]{1,0:T(8,128)S(1)} %get-tuple-element.22.inner), channel_id=1, source_target_pairs={{0,1},{1,0},{2,3},{3,2},{4,5},{5,4},{6,7},{7,6},{8,9},{9,8},{10,11... | collective-permute-start | bytes 491528 | tf_op jit(solution)/shard_map/ppermute | solution.py:683
  2.8 8.4 %collective-permute-start.1 = (f32[64,512]{1,0:T(8,128)S(1)}, f32[64,512]{1,0:T(8,128)S(1)}, u32[]{:S(2)}, u32[]{:S(2)}) collective-permute-start(f32[64,512]{1,0:T(8,128)S(1)} %get-tuple-element.23.outer), channel_id=1, source_target_pairs={{0,15},{1,2},{2,1},{3,4},{4,3},{5,6},{6,5},{7,8},{8,7},{9,10},{10,... | collective-permute-start | bytes 393224 | tf_op jit(solution)/shard_map/ppermute | solution.py:683
  8.4 11.9 %copy-start.2 = (f32[16,8,512]{2,1,0:T(8,128)S(1)}, f32[16,8,512]{2,1,0:T(8,128)}, u32[]{:S(2)}) copy-start(f32[16,8,512]{2,1,0:T(8,128)} %tracer.1) | copy-start | bytes 786436
  8.6 5.8 %collective-permute-start.2 = (f32[16,128]{1,0:T(8,128)S(1)}, f32[16,128]{1,0:T(8,128)S(1)}, u32[]{:S(2)}, u32[]{:S(2)}) collective-permute-start(f32[16,128]{1,0:T(8,128)S(1)} %get-tuple-element.24), channel_id=1, source_target_pairs={{0,15},{1,14},{2,13},{3,12},{4,11},{5,10},{6,9},{7,8},{8,7},{9,6},... | collective-permute-start | bytes 24584 | tf_op jit(solution)/shard_map/ppermute | solution.py:683
  9.7 10.7 %copy-start = (f32[16,8,512]{2,1,0:T(8,128)S(1)}, f32[16,8,512]{2,1,0:T(8,128)}, u32[]{:S(2)}) copy-start(f32[16,8,512]{2,1,0:T(8,128)} %zonal.3) | copy-start | bytes 786436
  9.7 10.7 %copy-start.1 = (f32[16,8,512]{2,1,0:T(8,128)S(1)}, f32[16,8,512]{2,1,0:T(8,128)}, u32[]{:S(2)}) copy-start(f32[16,8,512]{2,1,0:T(8,128)} %meridional.3) | copy-start | bytes 786436
  9.7 4.7 %collective-permute-start.3 = (f32[16,128]{1,0:T(8,128)S(1)}, f32[16,128]{1,0:T(8,128)S(1)}, u32[]{:S(2)}, u32[]{:S(2)}) collective-permute-start(f32[16,128]{1,0:T(8,128)S(1)} %get-tuple-element.29), channel_id=1, source_target_pairs={{1,0},{12,1},{15,2},{10,3},{13,4},{8,5},{11,6},{6,7},{9,8},{4,9},{... | collective-permute-start | bytes 24584 | tf_op jit(solution)/shard_map/ppermute | solution.py:683
  14.4 6.0 %copy-start.4 = (f32[8,512]{1,0:T(8,128)S(1)}, f32[8,512]{1,0:T(8,128)}, u32[]{:S(2)}) copy-start(f32[8,512]{1,0:T(8,128)} %diffusivity.3) | copy-start | bytes 49156
  16.0 4.4 %copy-start.3 = (s32[8,512]{1,0:T(8,128)S(1)}, s32[8,512]{1,0:T(8,128)}, u32[]{:S(2)}) copy-start(s32[8,512]{1,0:T(8,128)} %count.3) | copy-start | bytes 49156
  16.0 8.4 %all-to-all-start = ((f32[16,1,128]{2,1,0:T(1,128)}), f32[16,1,128]{2,1,0:T(1,128)S(1)}, u32[]{:S(2)}, u32[]{:S(2)}) async-start(f32[16,1,128]{2,1,0:T(1,128)} %bitcast.1), calls=%async_computation | async-start | bytes 16384 | tf_op jit(solution)/shard_map/all_to_all | solution.py:727

commit v10 on v9

--- a/solution.py
+++ b/solution.py
@@ -306,7 +306,20 @@
     return jnp.concatenate([jnp.where(even, west, east), jnp.where(even, east, west)], axis=0)
 
 
-def chip_kernel(inner, sibling, tile, near, far):
+def far_first():
+    size, index = lax.axis_size("lon"), lax.axis_index("lon")
+    odd = index % 2 == 1
+    return odd & (index < size // 2), ~odd & (index >= size // 2)
+
+
+def patch_order(one, two, near):
+    size, index = lax.axis_size("lon"), lax.axis_index("lon")
+    swapped = far_first()[1]
+    own = (index == 0) | (index == size // 2)
+    return jnp.where(swapped, two, one), jnp.where(own, near, jnp.where(swapped, one, two))
+
+
+def chip_kernel(inner, sibling, tile, near, one, two):
     even = is_even()
     ours, theirs = (pack[:72, NY - LANES:] for pack in (inner, sibling))
     full = chip_forcing(even, ours, theirs)
@@ -321,11 +334,16 @@
     fold = jnp.concatenate(
         [fold[i:i + 1] for i in range(2 * COLS - 1, -1, -1)], axis=0
     )
-    for out, source in ((near, inner), (far, sibling)):
+    patches = []
+    for source in (inner, sibling):
         edge = jnp.concatenate(
             [source[72:80, LANES:2 * LANES], source[72:80, 2 * LANES:3 * LANES]], axis=0
         )
-        out[...] = jnp.where((lane >= LANE_EDGE) & (lane < LANE_CODE), edge, fold)
+        patches.append(jnp.where((lane >= LANE_EDGE) & (lane < LANE_CODE), edge, fold))
+    swapped = far_first()[0]
+    near[...] = patches[0]
+    one[...] = jnp.where(swapped, patches[1], patches[0])
+    two[...] = jnp.where(swapped, patches[0], patches[1])
 
 
 def across_fold(even, chip, far):
@@ -425,11 +443,13 @@
             partial[at + g * COLS:at + (g + 1) * COLS] = part
 
 
-def fold_kernel(last, last_code, far_tile, tile, mirror, mirror_far, partial, vectors, gram):
+def fold_kernel(
+    last, last_code, far_tile, tile, one, two, near, partial, vectors, gram
+):
     even = is_even()
     lane = iota((EXT, LANES), 1)
     mine = extend(even, far_tile[...], tile[...], far_tile[...])
-    theirs, between = across_fold(even, mirror[...], mirror_far[...])
+    theirs, between = across_fold(even, *patch_order(one[...], two[...], near[...]))
     level = (lane - LANE_P).astype(f32)
     weight = jnp.where((lane >= LANE_P) & (lane < LANE_P + K), 0.5 * (0.5 + level / K), 0.0)
     mask_mine = (level < mine[:, LANE_LC:LANE_LC + 1]).astype(f32)
@@ -572,11 +592,12 @@
         meridional_next[k] = meridional[k] - jnp.where(lc > k, north, 0.0)
 
 
-def neighbours(count, sibling, beyond, mirror):
+def neighbours(count, sibling, beyond, one, two):
     shape = (COLS, NY)
     even = is_even()
     row, lane = iota(shape, 0), iota(shape, 1)
     lc = count[...].astype(f32)
+    mirror = patch_order(one[...], two[...], one[...])[0]
     north_tile = jnp.where(even, mirror[:COLS], mirror[COLS:])
 
     def around(field, west, east, north):
@@ -609,9 +630,9 @@
 
 
 def tracer_kernel(
-    tracer, zonal, meridional, count, diffusivity, sibling, beyond, mirror, tracer_next
+    tracer, zonal, meridional, count, diffusivity, sibling, beyond, one, two, tracer_next
 ):
-    lc, padded, mask_sum = neighbours(count, sibling, beyond, mirror)
+    lc, padded, mask_sum = neighbours(count, sibling, beyond, one, two)
     diff = diffusivity[...]
 
     def masked(k):
@@ -637,10 +658,10 @@
 
 
 def flow_kernel(
-    zonal, meridional, count, diffusivity, sibling, beyond, mirror,
+    zonal, meridional, count, diffusivity, sibling, beyond, one, two,
     zonal_step, meridional_step, levels,
 ):
-    lc, padded, mask_sum = neighbours(count, sibling, beyond, mirror)
+    lc, padded, mask_sum = neighbours(count, sibling, beyond, one, two)
     diff = diffusivity[...]
     turn = planetary(lc.shape)
     levels[...] = lc
@@ -684,8 +705,11 @@
 
     siblings = [(i, i ^ 1) for i in range(size)]
     outward = [(i, (i + 1 if i % 2 else i - 1) % size) for i in range(size)]
-    mirrored = [(i, size - 1 - i) for i in range(size)]
-    mirrored_far = [((size + 1 - 4 * (i % 2) - i) % size, i) for i in range(size)]
+    first = {i: size - 1 - i for i in range(size)}
+    second = {(size + 1 - 4 * (i % 2) - i) % size: i for i in range(size)}
+    for i in range(1, size // 2, 2):
+        first[i], second[i] = second[i], first[i]
+    first[1], second[size // 2 + 1] = size // 2, 0
     arguments = (tracer, zonal, meridional, count, diffusivity, surface)
     inner, outer = call(
         pack_kernel, [(80, NY), (64, NY)], *arguments,
@@ -696,9 +720,9 @@
     beyond = permute(outer, outward)
     sibling = permute(inner, siblings)
     patch = (2 * COLS, LANES)
-    tile, near, far = call(chip_kernel, [patch] * 3, inner, sibling)
-    mirror = permute(near, mirrored)
-    mirror_far = permute(far, mirrored_far)
+    tile, near, one, two = call(chip_kernel, [patch] * 4, inner, sibling)
+    one = permute(one, sorted(first.items()))
+    two = permute(two, sorted(second.items()))
     window = (EXT, LANES)
     last, last_code, vectors, partial, far_tile = call(
         inner_kernel,
@@ -710,9 +734,9 @@
     vectors_last, gram = call(
         fold_kernel,
         [(ITERS * EXT, LANES), (size, LANES)],
-        last, last_code, far_tile, tile, mirror, mirror_far, partial,
-    )
-    halos = (sibling, beyond, mirror)
+        last, last_code, far_tile, tile, one, two, near, partial,
+    )
+    halos = (sibling, beyond, one, two)
     tracer_next, = call(
         tracer_kernel, [block],
         tracer, zonal, meridional, count, diffusivity, *halos,
@@ -723,7 +747,7 @@
         zonal, meridional, count, diffusivity, *halos,
         flops=65536 * 40,
     )
-    group = [(i + size // 2 + 1) % size for i in range(size)]
+    group = [(5 * i + size // 2 - 1) % size for i in range(size)]
     gram = lax.all_to_all(gram, "lon", 0, 0, tiled=True, axis_index_groups=[group])
     zonal_next, meridional_next, height = call(
         finish_kernel, [block, block, (COLS, NY)],

time: 26.2 us -> 26 us (level)
  no operation moved by 1% of the time
where the time goes in v10:
time: 26 us; the launch traced here: 25.7 us
  starting transfers between devices  11.6 us (45%)
  Pallas kernels  7.42 us (29%)
  waiting for transfers between devices  5.99 us (23%)
  between operations  0.7 us (3%)
    ppermute x4, starting transfers between devices, permute(): return lax.ppermute(value, 'lon', pairs)  7.45 us
    pallas_call x7, Pallas kernels, call(): pl.pallas_call(kernel, out_shape=[jax.ShapeDtypeStruct(s, f32) for s in s...  7.42 us
    all_to_all x1, starting transfers between devices, body(): lax.all_to_all(gram, 'lon', 0, 0, tiled=True, axis_index_groups=[group])  4.1 us
    ppermute x4, waiting for transfers between devices, permute(): return lax.ppermute(value, 'lon', pairs)  3.77 us
    all_to_all x1, waiting for transfers between devices, body(): lax.all_to_all(gram, 'lon', 0, 0, tiled=True, axis_index_groups=[group])  2.22 us
  transfers between devices with their start and end apart: 5, of which 3 were waited for; matrix products, arithmetic and copies ran while one was open for 0% of the time, Pallas kernels for 10%

profile of v10, /device:TPU:0, one launch (start us, length us, event | category | flops | bytes accessed | tf_op | source)
XLA Modules:
  0.0 25.7 jit_solution(1923858807954170544)
XLA Ops:
  0.6 1.6 %shard_map.93 = (f32[80,512]{1,0:T(8,128)S(1)}, f32[64,512]{1,0:T(8,128)S(1)}) custom-call(f32[16,8,512]{2,1,0:T(8,128)} %tracer.1, f32[16,8,512]{2,1,0:T(8,128)} %zonal.3, f32[16,8,512]{2,1,0:T(8,128)} %meridional.3, s32[8,512]{1,0:T(8,128)} %count.3, f32[8,512]{1,0:T(8,128)} %diffusivity.3, f32[8,512]{1,0:T(8,128)} %surface_in.1), custom_call_target="tpu_custom_call" | custom-call | bytes 1130496 | tf_op jit(solution)/shard_map/pallas_call | solution.py:688
  2.2 0.5 %collective-permute-start = (f32[80,512]{1,0:T(8,128)S(1)}, f32[80,512]{1,0:T(8,128)S(1)}, u32[]{:S(2)}, u32[]{:S(2)}) collective-permute-start(f32[80,512]{1,0:T(8,128)S(1)} %get-tuple-element.23.inner), channel_id=1, source_target_pairs={{0,1},{1,0},{2,3},{3,2},{4,5},{5,4},{6,7},{7,6},{8,9},{9,8},{10,11... | collective-permute-start | bytes 491528 | tf_op jit(solution)/shard_map/ppermute | solution.py:704
  2.8 5.7 %collective-permute-start.1 = (f32[64,512]{1,0:T(8,128)S(1)}, f32[64,512]{1,0:T(8,128)S(1)}, u32[]{:S(2)}, u32[]{:S(2)}) collective-permute-start(f32[64,512]{1,0:T(8,128)S(1)} %get-tuple-element.24.outer), channel_id=1, source_target_pairs={{0,15},{1,2},{2,1},{3,4},{4,3},{5,6},{6,5},{7,8},{8,7},{9,10},{10,... | collective-permute-start | bytes 393224 | tf_op jit(solution)/shard_map/ppermute | solution.py:704
  8.4 0.0 collective-permute-done.sibling
  8.4 0.0 copy-start.2
  8.4 0.1 shard_map.94
  8.6 1.1 %collective-permute-start.2 = (f32[16,128]{1,0:T(8,128)S(1)}, f32[16,128]{1,0:T(8,128)S(1)}, u32[]{:S(2)}, u32[]{:S(2)}) collective-permute-start(f32[16,128]{1,0:T(8,128)S(1)} %get-tuple-element.25), channel_id=1, source_target_pairs={{0,15},{1,8},{2,13},{3,14},{4,11},{5,12},{6,9},{7,10},{8,7},{9,6},... | collective-permute-start | bytes 24584 | tf_op jit(solution)/shard_map/ppermute | solution.py:704
  9.6 0.0 copy-start
  9.7 0.0 copy-start.1
  9.7 0.2 collective-permute-start.3
  9.8 1.3 %collective-permute-done.1.beyond = f32[64,512]{1,0:T(8,128)S(1)} collective-permute-done((f32[64,512]{1,0:T(8,128)S(1)}, f32[64,512]{1,0:T(8,128)S(1)}, u32[]{:S(2)}, u32[]{:S(2)}) %collective-permute-start.1) | collective-permute-done | bytes 131104 | tf_op jit(solution)/shard_map/ppermute | solution.py:704
  11.2 0.8 %shard_map.96 = (f32[24,128]{1,0:T(8,128)S(1)}, f32[24,128]{1,0:T(8,128)S(1)}, f32[144,512]{1,0:T(8,128)S(1)}, f32[64,128]{1,0:T(8,128)S(1)}, f32[8,128]{1,0:T(8,128)S(1)}) custom-call(f32[80,512]{1,0:T(8,128)S(1)} %get-tuple-element.23.inner, f32[64,512]{1,0:T(8,128)S(1)} %get-tuple-element.24.outer, f32[80,512]{1,0:T(8,128)S(1)} %collective-permute-done.sibling, ...), custom_call_target="tpu_custom_call" | custom-call | flops 819200 | bytes 946176 | tf_op jit(solution)/shard_map/pallas_call | solution.py:688
  11.9 2.5 %collective-permute-done.2.one = f32[16,128]{1,0:T(8,128)S(1)} collective-permute-done((f32[16,128]{1,0:T(8,128)S(1)}, f32[16,128]{1,0:T(8,128)S(1)}, u32[]{:S(2)}, u32[]{:S(2)}) %collective-permute-start.2) | collective-permute-done | bytes 8224 | tf_op jit(solution)/shard_map/ppermute | solution.py:704
  14.4 0.0 collective-permute-done.3.two
  14.4 0.0 copy-start.4
  14.4 1.6 %shard_map.97 = (f32[144,128]{1,0:T(8,128)S(1)}, f32[16,128]{1,0:T(8,128)}) custom-call(f32[24,128]{1,0:T(8,128)S(1)} %get-tuple-element.27.last, f32[24,128]{1,0:T(8,128)S(1)} %get-tuple-element.28.last_code, f32[8,128]{1,0:T(8,128)S(1)} %get-tuple-element.29.far_tile, f32[16,128]{1,0:T(8,128)S(1)} %get-tuple-element.30.tile, ...), custom_call_target="tpu_custom_call" | custom-call | bytes 176128 | tf_op jit(solution)/shard_map/pallas_call | solution.py:688
  16.0 0.0 copy-start.3
  16.0 4.1 %all-to-all-start = ((f32[16,1,128]{2,1,0:T(1,128)}), f32[16,1,128]{2,1,0:T(1,128)S(1)}, u32[]{:S(2)}, u32[]{:S(2)}) async-start(f32[16,1,128]{2,1,0:T(1,128)} %bitcast.1), calls=%async_computation | async-start | bytes 16384 | tf_op jit(solution)/shard_map/all_to_all | solution.py:751
  20.1 0.0 copy-done.2
  20.1 0.0 copy-done
  20.1 0.0 copy-done.1
  20.2 0.0 copy-done.4
  20.2 0.0 copy-done.3
  20.2 1.2 %shard_map.95 = f32[16,8,512]{2,1,0:T(8,128)} custom-call(f32[16,8,512]{2,1,0:T(8,128)S(1)} %copy-done.2, f32[16,8,512]{2,1,0:T(8,128)S(1)} %copy-done, f32[16,8,512]{2,1,0:T(8,128)S(1)} %copy-done.1, s32[8,512]{1,0:T(8,128)S(1)} %copy-done.3, f32[8,512]{1,0:T(8,128)S(1)} %copy-done.4, f32[80,512]{1,0:T(8,128)S(1)} %collective-permute-done.sibling, ...), custom_call_target="tpu_custom_call" | custom-call | flops 2621440 | bytes 1392640 | tf_op jit(solution)/shard_map/pallas_call | solution.py:688
  21.3 0.6 %shard_map.98 = (f32[16,8,512]{2,1,0:T(8,128)S(1)}, f32[16,8,512]{2,1,0:T(8,128)S(1)}, f32[8,512]{1,0:T(8,128)S(1)}) custom-call(f32[16,8,512]{2,1,0:T(8,128)S(1)} %copy-done, f32[16,8,512]{2,1,0:T(8,128)S(1)} %copy-done.1, s32[8,512]{1,0:T(8,128)S(1)} %copy-done.3, f32[8,512]{1,0:T(8,128)S(1)} %copy-done.4, f32[80,512]{1,0:T(8,128)S(1)} %collective-permute-done.sibling, ...), custom_call_target="tpu_custom_call" | custom-call | flops 2621440 | bytes 1409024 | tf_op jit(solution)/shard_map/pallas_call | solution.py:688
  21.9 2.2 %all-to-all-done = f32[16,1,128]{2,1,0:T(1,128)S(1)} async-done(((f32[16,1,128]{2,1,0:T(1,128)}), f32[16,1,128]{2,1,0:T(1,128)S(1)}, u32[]{:S(2)}, u32[]{:S(2)}) %all-to-all-start) | async-done | bytes 8224 | tf_op jit(solution)/shard_map/all_to_all | solution.py:751
  24.1 1.5 %shard_map.99 = (f32[16,8,512]{2,1,0:T(8,128)}, f32[16,8,512]{2,1,0:T(8,128)}, f32[8,512]{1,0:T(8,128)}) custom-call(f32[16,128]{1,0:T(8,128)S(1)} %bitcast.4, f32[144,512]{1,0:T(8,128)S(1)} %get-tuple-element.34.vectors, f32[144,128]{1,0:T(8,128)S(1)} %get-tuple-element.35.vectors_last, f32[16,8,512]{2,1,0:T(8,128)S(1)} %get-tuple-element.36.zonal, ...), custom_call_target="tpu_custom_call" | custom-call | bytes 1458176 | tf_op jit(solution)/shard_map/pallas_call | solution.py:688
Async XLA Ops:
  2.2 6.2 %collective-permute-start = (f32[80,512]{1,0:T(8,128)S(1)}, f32[80,512]{1,0:T(8,128)S(1)}, u32[]{:S(2)}, u32[]{:S(2)}) collective-permute-start(f32[80,512]{1,0:T(8,128)S(1)} %get-tuple-element.23.inner), channel_id=1, source_target_pairs={{0,1},{1,0},{2,3},{3,2},{4,5},{5,4},{6,7},{7,6},{8,9},{9,8},{10,11... | collective-permute-start | bytes 491528 | tf_op jit(solution)/shard_map/ppermute | solution.py:704
  2.8 8.4 %collective-permute-start.1 = (f32[64,512]{1,0:T(8,128)S(1)}, f32[64,512]{1,0:T(8,128)S(1)}, u32[]{:S(2)}, u32[]{:S(2)}) collective-permute-start(f32[64,512]{1,0:T(8,128)S(1)} %get-tuple-element.24.outer), channel_id=1, source_target_pairs={{0,15},{1,2},{2,1},{3,4},{4,3},{5,6},{6,5},{7,8},{8,7},{9,10},{10,... | collective-permute-start | bytes 393224 | tf_op jit(solution)/shard_map/ppermute | solution.py:704
  8.4 11.7 %copy-start.2 = (f32[16,8,512]{2,1,0:T(8,128)S(1)}, f32[16,8,512]{2,1,0:T(8,128)}, u32[]{:S(2)}) copy-start(f32[16,8,512]{2,1,0:T(8,128)} %tracer.1) | copy-start | bytes 786436
  8.6 5.8 %collective-permute-start.2 = (f32[16,128]{1,0:T(8,128)S(1)}, f32[16,128]{1,0:T(8,128)S(1)}, u32[]{:S(2)}, u32[]{:S(2)}) collective-permute-start(f32[16,128]{1,0:T(8,128)S(1)} %get-tuple-element.25), channel_id=1, source_target_pairs={{0,15},{1,8},{2,13},{3,14},{4,11},{5,12},{6,9},{7,10},{8,7},{9,6},... | collective-permute-start | bytes 24584 | tf_op jit(solution)/shard_map/ppermute | solution.py:704
  9.6 10.5 %copy-start = (f32[16,8,512]{2,1,0:T(8,128)S(1)}, f32[16,8,512]{2,1,0:T(8,128)}, u32[]{:S(2)}) copy-start(f32[16,8,512]{2,1,0:T(8,128)} %zonal.3) | copy-start | bytes 786436
  9.7 10.5 %copy-start.1 = (f32[16,8,512]{2,1,0:T(8,128)S(1)}, f32[16,8,512]{2,1,0:T(8,128)}, u32[]{:S(2)}) copy-start(f32[16,8,512]{2,1,0:T(8,128)} %meridional.3) | copy-start | bytes 786436
  9.7 4.7 %collective-permute-start.3 = (f32[16,128]{1,0:T(8,128)S(1)}, f32[16,128]{1,0:T(8,128)S(1)}, u32[]{:S(2)}, u32[]{:S(2)}) collective-permute-start(f32[16,128]{1,0:T(8,128)S(1)} %get-tuple-element.26), channel_id=1, source_target_pairs={{0,13},{1,14},{2,11},{3,12},{4,9},{5,10},{6,7},{7,8},{8,5},{9,0},{... | collective-permute-start | bytes 24584 | tf_op jit(solution)/shard_map/ppermute | solution.py:704
  14.4 5.8 %copy-start.4 = (f32[8,512]{1,0:T(8,128)S(1)}, f32[8,512]{1,0:T(8,128)}, u32[]{:S(2)}) copy-start(f32[8,512]{1,0:T(8,128)} %diffusivity.3) | copy-start | bytes 49156
  16.0 4.1 %copy-start.3 = (s32[8,512]{1,0:T(8,128)S(1)}, s32[8,512]{1,0:T(8,128)}, u32[]{:S(2)}) copy-start(s32[8,512]{1,0:T(8,128)} %count.3) | copy-start | bytes 49156
  16.0 8.1 %all-to-all-start = ((f32[16,1,128]{2,1,0:T(1,128)}), f32[16,1,128]{2,1,0:T(1,128)S(1)}, u32[]{:S(2)}, u32[]{:S(2)}) async-start(f32[16,1,128]{2,1,0:T(1,128)} %bitcast.1), calls=%async_computation | async-start | bytes 16384 | tf_op jit(solution)/shard_map/all_to_all | solution.py:751

commit v11 on v10

--- a/solution.py
+++ b/solution.py
@@ -410,15 +410,23 @@
     return [pair_pack(entries[g:g + COLS]) for g in range(0, len(entries), COLS)]
 
 
+def lane_sums(groups, first, last):
+    size = GROUPS * COLS
+    parts = [pair[0] for pair in groups] + [pair[1] for pair in groups]
+    turned = jnp.concatenate(parts + [jnp.zeros((LANES - 2 * size, LANES), f32)], axis=0).T
+    terms = [turned[i:i + COLS] for i in range(first, last, COLS)]
+    return pair_norm(pair_rows(pair_tree([(t, roll(t, -size, 1)) for t in terms])))
+
+
 def inner_kernel(
-    inner, outer, sibling, beyond, last, last_code, vectors, partial, far_tile,
+    inner, outer, sibling, beyond, tile, last, last_code, vectors, partial, ours,
 ):
     even = is_even()
     forcing = chip_forcing(even, inner, sibling)
     coded = beside(even, inner[COLS:2 * COLS], sibling[COLS:2 * COLS])
     at_east, at_west = jnp.where(even, 0, COLS - 1), jnp.where(even, COLS - 1, 0)
     lc_out, diff_out, _ = far_rows(outer, at_west, jnp.where(even, COLS - 2, 1))
-    lc_far, diff_far, far_tile[...] = far_rows(beyond, at_east, jnp.where(even, 1, COLS - 2))
+    lc_far, diff_far, tile_far = far_rows(beyond, at_east, jnp.where(even, 1, COLS - 2))
     flux_out = interface_flux(outer, beyond, lc_out, lc_far)
     own, far = diff_out * flux_out, -diff_far * flux_out
     row = iota((EXT, NY), 0)
@@ -438,30 +446,34 @@
         cut = [q[COLS:2 * COLS, c:c + LANES] for c in range(0, NY, LANES)]
         cut[-1] = jnp.where(lane < LANES - COLS, cut[-1], 0.0)
         blocks.append(cut)
-    for g, pair in enumerate(gram_rows(blocks)):
-        for at, part in zip((0, GROUPS * COLS), pair):
-            partial[at + g * COLS:at + (g + 1) * COLS] = part
+    high, low = lane_sums(gram_rows(blocks), 0, LANES)
+    partial[:COLS] = high
+    partial[COLS:] = low
+    mine = extend(even, tile_far, tile[...], tile_far)
+    lane = iota((EXT, LANES), 1)
+    level = (lane - LANE_P).astype(f32)
+    weight = jnp.where((lane >= LANE_P) & (lane < LANE_P + K), 0.5 * (0.5 + level / K), 0.0)
+    ours[:EXT] = jnp.where(level < mine[:, LANE_LC:LANE_LC + 1], weight, 0.0)
+    ours[EXT:2 * EXT] = weight * mine
+    ours[2 * EXT:] = jnp.where(lane == LANE_F - 1, mine[:, LANE_DIFF:LANE_DIFF + 1], 0.0)
 
 
 def fold_kernel(
-    last, last_code, far_tile, tile, one, two, near, partial, vectors, gram
+    last, last_code, ours, one, two, near, partial, vectors, gram
 ):
     even = is_even()
     lane = iota((EXT, LANES), 1)
-    mine = extend(even, far_tile[...], tile[...], far_tile[...])
     theirs, between = across_fold(even, *patch_order(one[...], two[...], near[...]))
     level = (lane - LANE_P).astype(f32)
-    weight = jnp.where((lane >= LANE_P) & (lane < LANE_P + K), 0.5 * (0.5 + level / K), 0.0)
-    mask_mine = (level < mine[:, LANE_LC:LANE_LC + 1]).astype(f32)
-    mask_theirs = (level < theirs[:, LANE_LC:LANE_LC + 1]).astype(f32)
-    flux = -jnp.sum(weight * (mask_mine * theirs + mask_theirs * mine), axis=1, keepdims=True)
-    own_change = mine[:, LANE_DIFF:LANE_DIFF + 1] * flux
+    flux = -jnp.sum(
+        ours[:EXT] * theirs
+        + jnp.where(level < theirs[:, LANE_LC:LANE_LC + 1], ours[EXT:2 * EXT], 0.0),
+        axis=1, keepdims=True,
+    )
     far_change = theirs[:, LANE_DIFF:LANE_DIFF + 1] * flux
     beyond_fold = lane >= LANE_F
     start = jnp.where(beyond_fold, theirs, last[...]) + between
-    start = start + jnp.where(
-        lane == LANE_F, far_change, jnp.where(lane == LANE_F - 1, own_change, 0.0)
-    )
+    start = start + jnp.where(lane == LANE_F, far_change, ours[2 * EXT:] * flux)
     code = jnp.where(beyond_fold, roll(theirs, LANE_F - LANE_CODE, 1), last_code[...])
     v = basis(start, code)
     for j in range(ITERS):
@@ -469,16 +481,9 @@
     own_lane = lane[:COLS]
     summed = (own_lane >= LANE_F - COLS) & (own_lane < LANE_F)
     blocks = [[jnp.where(summed, q[COLS:2 * COLS], 0.0)] for q in v]
+    sums = lane_sums(gram_rows(blocks), LANE_F - COLS, LANE_F)
+    high, low = pair_norm(pair_add(sums, (partial[:COLS], partial[COLS:])))
     size = GROUPS * COLS
-    high, low = [], []
-    for g, pair in enumerate(gram_rows(blocks)):
-        at = g * COLS
-        pair = pair_add(pair, (partial[at:at + COLS], partial[size + at:size + at + COLS]))
-        high.append(pair[0])
-        low.append(pair[1])
-    turned = jnp.concatenate(high + low + [jnp.zeros((LANES - 2 * size, LANES), f32)], axis=0).T
-    terms = [turned[i * COLS:(i + 1) * COLS] for i in range(LANES // COLS)]
-    high, low = pair_norm(pair_rows(pair_tree([(t, roll(t, -size, 1)) for t in terms])))
     row = jnp.where(iota((COLS, LANES), 1) < size, high, roll(low, size, 1))
     gram[...] = jnp.broadcast_to(row[:1], gram.shape)
 
@@ -724,17 +729,17 @@
     one = permute(one, sorted(first.items()))
     two = permute(two, sorted(second.items()))
     window = (EXT, LANES)
-    last, last_code, vectors, partial, far_tile = call(
+    last, last_code, vectors, partial, ours = call(
         inner_kernel,
         [
-            window, window, (ITERS * EXT, NY), (2 * GROUPS * COLS, LANES), (COLS, LANES),
+            window, window, (ITERS * EXT, NY), (2 * COLS, LANES), (3 * EXT, LANES),
         ],
-        inner, outer, sibling, beyond, flops=8192 * 100,
+        inner, outer, sibling, beyond, tile, flops=8192 * 100,
     )
     vectors_last, gram = call(
         fold_kernel,
         [(ITERS * EXT, LANES), (size, LANES)],
-        last, last_code, far_tile, tile, one, two, near, partial,
+        last, last_code, ours, one, two, near, partial,
     )
     halos = (sibling, beyond, one, two)
     tracer_next, = call(

time: 26 us -> 25.9 us (level)
  transfers between devices with their start and end apart: 5 -> 5, of which waited for: 3 -> 3; matrix products, arithmetic and copies ran while one was open for 0% -> 0% of each run, Pallas kernels for 10% -> 11%
where the time goes in v11:
time: 25.9 us; the launch traced here: 25.7 us
  starting transfers between devices  11.6 us (45%)
  Pallas kernels  7.58 us (29%)
  waiting for transfers between devices  5.81 us (22%)
  between operations  0.7 us (3%)
    pallas_call x7, Pallas kernels, call(): pl.pallas_call(kernel, out_shape=[jax.ShapeDtypeStruct(s, f32) for s in s...  7.58 us
    ppermute x4, starting transfers between devices, permute(): return lax.ppermute(value, 'lon', pairs)  7.45 us
    all_to_all x1, starting transfers between devices, body(): lax.all_to_all(gram, 'lon', 0, 0, tiled=True, axis_index_groups=[group])  4.1 us
    ppermute x4, waiting for transfers between devices, permute(): return lax.ppermute(value, 'lon', pairs)  3.59 us
    all_to_all x1, waiting for transfers between devices, body(): lax.all_to_all(gram, 'lon', 0, 0, tiled=True, axis_index_groups=[group])  2.22 us
  transfers between devices with their start and end apart: 5, of which 3 were waited for; matrix products, arithmetic and copies ran while one was open for 0% of the time, Pallas kernels for 11%

profile of v11, /device:TPU:0, one launch (start us, length us, event | category | flops | bytes accessed | tf_op | source)
XLA Modules:
  0.0 25.7 jit_solution(2675225082664171397)
XLA Ops:
  0.6 1.6 %shard_map.93 = (f32[80,512]{1,0:T(8,128)S(1)}, f32[64,512]{1,0:T(8,128)S(1)}) custom-call(f32[16,8,512]{2,1,0:T(8,128)} %tracer.1, f32[16,8,512]{2,1,0:T(8,128)} %zonal.3, f32[16,8,512]{2,1,0:T(8,128)} %meridional.3, s32[8,512]{1,0:T(8,128)} %count.3, f32[8,512]{1,0:T(8,128)} %diffusivity.3, f32[8,512]{1,0:T(8,128)} %surface_in.1), custom_call_target="tpu_custom_call" | custom-call | bytes 1130496 | tf_op jit(solution)/shard_map/pallas_call | solution.py:693
  2.2 0.5 %collective-permute-start = (f32[80,512]{1,0:T(8,128)S(1)}, f32[80,512]{1,0:T(8,128)S(1)}, u32[]{:S(2)}, u32[]{:S(2)}) collective-permute-start(f32[80,512]{1,0:T(8,128)S(1)} %get-tuple-element.23.inner), channel_id=1, source_target_pairs={{0,1},{1,0},{2,3},{3,2},{4,5},{5,4},{6,7},{7,6},{8,9},{9,8},{10,11... | collective-permute-start | bytes 491528 | tf_op jit(solution)/shard_map/ppermute | solution.py:709
  2.8 5.7 %collective-permute-start.1 = (f32[64,512]{1,0:T(8,128)S(1)}, f32[64,512]{1,0:T(8,128)S(1)}, u32[]{:S(2)}, u32[]{:S(2)}) collective-permute-start(f32[64,512]{1,0:T(8,128)S(1)} %get-tuple-element.24.outer), channel_id=1, source_target_pairs={{0,15},{1,2},{2,1},{3,4},{4,3},{5,6},{6,5},{7,8},{8,7},{9,10},{10,... | collective-permute-start | bytes 393224 | tf_op jit(solution)/shard_map/ppermute | solution.py:709
  8.4 0.0 collective-permute-done.sibling
  8.4 0.0 copy-start.2
  8.4 0.1 shard_map.94
  8.6 1.1 %collective-permute-start.2 = (f32[16,128]{1,0:T(8,128)S(1)}, f32[16,128]{1,0:T(8,128)S(1)}, u32[]{:S(2)}, u32[]{:S(2)}) collective-permute-start(f32[16,128]{1,0:T(8,128)S(1)} %get-tuple-element.25), channel_id=1, source_target_pairs={{0,15},{1,8},{2,13},{3,14},{4,11},{5,12},{6,9},{7,10},{8,7},{9,6},... | collective-permute-start | bytes 24584 | tf_op jit(solution)/shard_map/ppermute | solution.py:709
  9.6 0.2 collective-permute-start.3
  9.8 1.3 %collective-permute-done.1.beyond = f32[64,512]{1,0:T(8,128)S(1)} collective-permute-done((f32[64,512]{1,0:T(8,128)S(1)}, f32[64,512]{1,0:T(8,128)S(1)}, u32[]{:S(2)}, u32[]{:S(2)}) %collective-permute-start.1) | collective-permute-done | bytes 131104 | tf_op jit(solution)/shard_map/ppermute | solution.py:709
  11.2 0.0 copy-start
  11.2 0.0 copy-start.1
  11.2 1.0 %shard_map.96 = (f32[24,128]{1,0:T(8,128)S(1)}, f32[24,128]{1,0:T(8,128)S(1)}, f32[144,512]{1,0:T(8,128)S(1)}, f32[16,128]{1,0:T(8,128)S(1)}, f32[72,128]{1,0:T(8,128)S(1)}) custom-call(f32[80,512]{1,0:T(8,128)S(1)} %get-tuple-element.23.inner, f32[64,512]{1,0:T(8,128)S(1)} %get-tuple-element.24.outer, f32[80,512]{1,0:T(8,128)S(1)} %collective-permute-done.sibling, ...), custom_call_target="tpu_custom_call" | custom-call | flops 819200 | bytes 962560 | tf_op jit(solution)/shard_map/pallas_call | solution.py:693
  12.1 2.3 %collective-permute-done.2.one = f32[16,128]{1,0:T(8,128)S(1)} collective-permute-done((f32[16,128]{1,0:T(8,128)S(1)}, f32[16,128]{1,0:T(8,128)S(1)}, u32[]{:S(2)}, u32[]{:S(2)}) %collective-permute-start.2) | collective-permute-done | bytes 8224 | tf_op jit(solution)/shard_map/ppermute | solution.py:709
  14.4 0.0 collective-permute-done.3.two
  14.4 0.0 copy-start.4
  14.4 1.6 %shard_map.97 = (f32[144,128]{1,0:T(8,128)S(1)}, f32[16,128]{1,0:T(8,128)}) custom-call(f32[24,128]{1,0:T(8,128)S(1)} %get-tuple-element.28.last, f32[24,128]{1,0:T(8,128)S(1)} %get-tuple-element.29.last_code, f32[72,128]{1,0:T(8,128)S(1)} %get-tuple-element.30.ours, f32[16,128]{1,0:T(8,128)S(1)} %collective-permute-done.2.one, ...), custom_call_target="tpu_custom_call" | custom-call | bytes 176128 | tf_op jit(solution)/shard_map/pallas_call | solution.py:693
  16.0 0.0 copy-start.3
  16.0 4.1 %all-to-all-start = ((f32[16,1,128]{2,1,0:T(1,128)}), f32[16,1,128]{2,1,0:T(1,128)S(1)}, u32[]{:S(2)}, u32[]{:S(2)}) async-start(f32[16,1,128]{2,1,0:T(1,128)} %bitcast.1), calls=%async_computation | async-start | bytes 16384 | tf_op jit(solution)/shard_map/all_to_all | solution.py:756
  20.1 0.0 copy-done.2
  20.1 0.0 copy-done
  20.1 0.0 copy-done.1
  20.1 0.0 copy-done.4
  20.2 0.0 copy-done.3
  20.2 1.2 %shard_map.95 = f32[16,8,512]{2,1,0:T(8,128)} custom-call(f32[16,8,512]{2,1,0:T(8,128)S(1)} %copy-done.2, f32[16,8,512]{2,1,0:T(8,128)S(1)} %copy-done, f32[16,8,512]{2,1,0:T(8,128)S(1)} %copy-done.1, s32[8,512]{1,0:T(8,128)S(1)} %copy-done.3, f32[8,512]{1,0:T(8,128)S(1)} %copy-done.4, f32[80,512]{1,0:T(8,128)S(1)} %collective-permute-done.sibling, ...), custom_call_target="tpu_custom_call" | custom-call | flops 2621440 | bytes 1392640 | tf_op jit(solution)/shard_map/pallas_call | solution.py:693
  21.3 0.6 %shard_map.98 = (f32[16,8,512]{2,1,0:T(8,128)S(1)}, f32[16,8,512]{2,1,0:T(8,128)S(1)}, f32[8,512]{1,0:T(8,128)S(1)}) custom-call(f32[16,8,512]{2,1,0:T(8,128)S(1)} %copy-done, f32[16,8,512]{2,1,0:T(8,128)S(1)} %copy-done.1, s32[8,512]{1,0:T(8,128)S(1)} %copy-done.3, f32[8,512]{1,0:T(8,128)S(1)} %copy-done.4, f32[80,512]{1,0:T(8,128)S(1)} %collective-permute-done.sibling, ...), custom_call_target="tpu_custom_call" | custom-call | flops 2621440 | bytes 1409024 | tf_op jit(solution)/shard_map/pallas_call | solution.py:693
  21.9 2.2 %all-to-all-done = f32[16,1,128]{2,1,0:T(1,128)S(1)} async-done(((f32[16,1,128]{2,1,0:T(1,128)}), f32[16,1,128]{2,1,0:T(1,128)S(1)}, u32[]{:S(2)}, u32[]{:S(2)}) %all-to-all-start) | async-done | bytes 8224 | tf_op jit(solution)/shard_map/all_to_all | solution.py:756
  24.1 1.5 %shard_map.99 = (f32[16,8,512]{2,1,0:T(8,128)}, f32[16,8,512]{2,1,0:T(8,128)}, f32[8,512]{1,0:T(8,128)}) custom-call(f32[16,128]{1,0:T(8,128)S(1)} %bitcast.4, f32[144,512]{1,0:T(8,128)S(1)} %get-tuple-element.34.vectors, f32[144,128]{1,0:T(8,128)S(1)} %get-tuple-element.35.vectors_last, f32[16,8,512]{2,1,0:T(8,128)S(1)} %get-tuple-element.36.zonal, ...), custom_call_target="tpu_custom_call" | custom-call | bytes 1458176 | tf_op jit(solution)/shard_map/pallas_call | solution.py:693
Async XLA Ops:
  2.2 6.2 %collective-permute-start = (f32[80,512]{1,0:T(8,128)S(1)}, f32[80,512]{1,0:T(8,128)S(1)}, u32[]{:S(2)}, u32[]{:S(2)}) collective-permute-start(f32[80,512]{1,0:T(8,128)S(1)} %get-tuple-element.23.inner), channel_id=1, source_target_pairs={{0,1},{1,0},{2,3},{3,2},{4,5},{5,4},{6,7},{7,6},{8,9},{9,8},{10,11... | collective-permute-start | bytes 491528 | tf_op jit(solution)/shard_map/ppermute | solution.py:709
  2.8 8.4 %collective-permute-start.1 = (f32[64,512]{1,0:T(8,128)S(1)}, f32[64,512]{1,0:T(8,128)S(1)}, u32[]{:S(2)}, u32[]{:S(2)}) collective-permute-start(f32[64,512]{1,0:T(8,128)S(1)} %get-tuple-element.24.outer), channel_id=1, source_target_pairs={{0,15},{1,2},{2,1},{3,4},{4,3},{5,6},{6,5},{7,8},{8,7},{9,10},{10,... | collective-permute-start | bytes 393224 | tf_op jit(solution)/shard_map/ppermute | solution.py:709
  8.4 11.7 %copy-start.2 = (f32[16,8,512]{2,1,0:T(8,128)S(1)}, f32[16,8,512]{2,1,0:T(8,128)}, u32[]{:S(2)}) copy-start(f32[16,8,512]{2,1,0:T(8,128)} %tracer.1) | copy-start | bytes 786436
  8.6 5.8 %collective-permute-start.2 = (f32[16,128]{1,0:T(8,128)S(1)}, f32[16,128]{1,0:T(8,128)S(1)}, u32[]{:S(2)}, u32[]{:S(2)}) collective-permute-start(f32[16,128]{1,0:T(8,128)S(1)} %get-tuple-element.25), channel_id=1, source_target_pairs={{0,15},{1,8},{2,13},{3,14},{4,11},{5,12},{6,9},{7,10},{8,7},{9,6},... | collective-permute-start | bytes 24584 | tf_op jit(solution)/shard_map/ppermute | solution.py:709
  9.6 4.8 %collective-permute-start.3 = (f32[16,128]{1,0:T(8,128)S(1)}, f32[16,128]{1,0:T(8,128)S(1)}, u32[]{:S(2)}, u32[]{:S(2)}) collective-permute-start(f32[16,128]{1,0:T(8,128)S(1)} %get-tuple-element.26), channel_id=1, source_target_pairs={{0,13},{1,14},{2,11},{3,12},{4,9},{5,10},{6,7},{7,8},{8,5},{9,0},{... | collective-permute-start | bytes 24584 | tf_op jit(solution)/shard_map/ppermute | solution.py:709
  11.2 9.0 %copy-start = (f32[16,8,512]{2,1,0:T(8,128)S(1)}, f32[16,8,512]{2,1,0:T(8,128)}, u32[]{:S(2)}) copy-start(f32[16,8,512]{2,1,0:T(8,128)} %zonal.3) | copy-start | bytes 786436
  11.2 9.0 %copy-start.1 = (f32[16,8,512]{2,1,0:T(8,128)S(1)}, f32[16,8,512]{2,1,0:T(8,128)}, u32[]{:S(2)}) copy-start(f32[16,8,512]{2,1,0:T(8,128)} %meridional.3) | copy-start | bytes 786436
  14.4 5.7 %copy-start.4 = (f32[8,512]{1,0:T(8,128)S(1)}, f32[8,512]{1,0:T(8,128)}, u32[]{:S(2)}) copy-start(f32[8,512]{1,0:T(8,128)} %diffusivity.3) | copy-start | bytes 49156
  16.0 4.1 %copy-start.3 = (s32[8,512]{1,0:T(8,128)S(1)}, s32[8,512]{1,0:T(8,128)}, u32[]{:S(2)}) copy-start(s32[8,512]{1,0:T(8,128)} %count.3) | copy-start | bytes 49156
  16.0 8.1 %all-to-all-start = ((f32[16,1,128]{2,1,0:T(1,128)}), f32[16,1,128]{2,1,0:T(1,128)S(1)}, u32[]{:S(2)}, u32[]{:S(2)}) async-start(f32[16,1,128]{2,1,0:T(1,128)} %bitcast.1), calls=%async_computation | async-start | bytes 16384 | tf_op jit(solution)/shard_map/all_to_all | solution.py:756

commit v12 on v11

--- a/solution.py
+++ b/solution.py
@@ -568,16 +568,7 @@
     return solution
 
 
-def finish_kernel(
-    gram, vectors, vectors_last, zonal, meridional, levels, zonal_next, meridional_next, height
-):
-    x = coefficients(gram)
-
-    def combine(part):
-        terms = [x[j:j + 1, :1] * part[j * EXT:(j + 1) * EXT] for j in range(ITERS)]
-        return sum(terms[1:], terms[0])
-
-    total, window = combine(vectors), combine(vectors_last)
+def slope_kernel(vectors, vectors_last, parts):
     near = iota((COLS, LANES), 1) >= CUT - (NY - LANES)
 
     def finished(value, from_window):
@@ -586,11 +577,29 @@
         last = jnp.where(near, moved, value[:, NY - LANES:])
         return jnp.concatenate([value[:, :NY - LANES], last], axis=1)
 
-    def step(axis):
-        return gravity * finished(roll(total, -1, axis) - total, roll(window, -1, axis) - window)
-
-    height[...] = finished(total, window)
-    east, north = step(0), step(1)
+    for j in range(ITERS):
+        at = slice(j * EXT, (j + 1) * EXT)
+        total, window = vectors[at], vectors_last[at]
+        row = 3 * j * COLS
+        parts[row:row + COLS] = finished(total, window)
+        for axis in (0, 1):
+            row += COLS
+            parts[row:row + COLS] = gravity * finished(
+                roll(total, -1, axis) - total, roll(window, -1, axis) - window
+            )
+
+
+def finish_kernel(gram, parts, zonal, meridional, levels, zonal_next, meridional_next, height):
+    x = coefficients(gram)
+
+    def combine(which):
+        rows = [(3 * j + which) * COLS for j in range(ITERS)]
+        terms = [x[j:j + 1, :1] * parts[row:row + COLS] for j, row in enumerate(rows)]
+        pairs = [sum(terms[j + 1:j + 2], terms[j]) for j in range(0, ITERS, 2)]
+        return sum(pairs[1:], pairs[0])
+
+    height[...] = combine(0)
+    east, north = combine(1), combine(2)
     lc = levels[...]
     for k in range(K):
         zonal_next[k] = zonal[k] - jnp.where(lc > k, east, 0.0)
@@ -754,9 +763,10 @@
     )
     group = [(5 * i + size // 2 - 1) % size for i in range(size)]
     gram = lax.all_to_all(gram, "lon", 0, 0, tiled=True, axis_index_groups=[group])
+    parts, = call(slope_kernel, [(3 * ITERS * COLS, NY)], vectors, vectors_last, flops=8192 * 20)
     zonal_next, meridional_next, height = call(
         finish_kernel, [block, block, (COLS, NY)],
-        gram, vectors, vectors_last, zonal_step, meridional_step, levels,
+        gram, parts, zonal_step, meridional_step, levels,
     )
     return tracer_next, zonal_next, meridional_next, height
 

time: 25.9 us -> 25.7 us (level)
  waiting for transfers between devices: 5.81 us -> 4.82 us
  local copies, waits for them, and re-layouts: 0.02 us -> 0.85 us
    all_to_all x1, waiting for transfers between devices: 2.22 us -> 1.23 us  [body(): lax.all_to_all(gram, 'lon', 0, 0, tiled=True, axis_index_groups=[group])]
    unnamed x10, local copies, waits for them, and re-layouts: 0.02 us -> 0.85 us
    pallas_call x7 -> x8, Pallas kernels: 7.58 us -> 7.66 us  [call(): pl.pallas_call(kernel, out_shape=[jax.ShapeDtypeStruct(s, f32) for s in s...]
  transfers between devices with their start and end apart: 5 -> 5, of which waited for: 3 -> 3; matrix products, arithmetic and copies ran while one was open for 0% -> 0% of each run, Pallas kernels for 11% -> 12%
where the time goes in v12:
time: 25.7 us; the launch traced here: 25.5 us
  starting transfers between devices  11.4 us (44%)
  Pallas kernels  7.66 us (30%)
  waiting for transfers between devices  4.82 us (19%)
  local copies, waits for them, and re-layouts  0.85 us (3%)
  between operations  0.71 us (3%)
    pallas_call x8, Pallas kernels, call(): pl.pallas_call(kernel, out_shape=[jax.ShapeDtypeStruct(s, f32) for s in s...  7.66 us
    ppermute x4, starting transfers between devices, permute(): return lax.ppermute(value, 'lon', pairs)  7.45 us
    all_to_all x1, starting transfers between devices, body(): lax.all_to_all(gram, 'lon', 0, 0, tiled=True, axis_index_groups=[group])  3.97 us
    ppermute x4, waiting for transfers between devices, permute(): return lax.ppermute(value, 'lon', pairs)  3.6 us
    all_to_all x1, waiting for transfers between devices, body(): lax.all_to_all(gram, 'lon', 0, 0, tiled=True, axis_index_groups=[group])  1.23 us
    unnamed x10, local copies, waits for them, and re-layouts  0.85 us
  transfers between devices with their start and end apart: 5, of which 3 were waited for; matrix products, arithmetic and copies ran while one was open for 0% of the time, Pallas kernels for 12%

profile of v12, /device:TPU:0, one launch (start us, length us, event | category | flops | bytes accessed | tf_op | source)
XLA Modules:
  0.0 25.5 jit_solution(1234309111984044785)
XLA Ops:
  0.6 1.6 %shard_map.93 = (f32[80,512]{1,0:T(8,128)S(1)}, f32[64,512]{1,0:T(8,128)S(1)}) custom-call(f32[16,8,512]{2,1,0:T(8,128)} %tracer.1, f32[16,8,512]{2,1,0:T(8,128)} %zonal.3, f32[16,8,512]{2,1,0:T(8,128)} %meridional.3, s32[8,512]{1,0:T(8,128)} %count.3, f32[8,512]{1,0:T(8,128)} %diffusivity.3, f32[8,512]{1,0:T(8,128)} %surface_in.1), custom_call_target="tpu_custom_call" | custom-call | bytes 1130496 | tf_op jit(solution)/shard_map/pallas_call | solution.py:702
  2.2 0.5 %collective-permute-start = (f32[80,512]{1,0:T(8,128)S(1)}, f32[80,512]{1,0:T(8,128)S(1)}, u32[]{:S(2)}, u32[]{:S(2)}) collective-permute-start(f32[80,512]{1,0:T(8,128)S(1)} %get-tuple-element.23.inner), channel_id=1, source_target_pairs={{0,1},{1,0},{2,3},{3,2},{4,5},{5,4},{6,7},{7,6},{8,9},{9,8},{10,11... | collective-permute-start | bytes 491528 | tf_op jit(solution)/shard_map/ppermute | solution.py:718
  2.8 5.7 %collective-permute-start.1 = (f32[64,512]{1,0:T(8,128)S(1)}, f32[64,512]{1,0:T(8,128)S(1)}, u32[]{:S(2)}, u32[]{:S(2)}) collective-permute-start(f32[64,512]{1,0:T(8,128)S(1)} %get-tuple-element.24.outer), channel_id=1, source_target_pairs={{0,15},{1,2},{2,1},{3,4},{4,3},{5,6},{6,5},{7,8},{8,7},{9,10},{10,... | collective-permute-start | bytes 393224 | tf_op jit(solution)/shard_map/ppermute | solution.py:718
  8.4 0.0 collective-permute-done.sibling
  8.4 0.1 shard_map.94
  8.6 1.1 %collective-permute-start.2 = (f32[16,128]{1,0:T(8,128)S(1)}, f32[16,128]{1,0:T(8,128)S(1)}, u32[]{:S(2)}, u32[]{:S(2)}) collective-permute-start(f32[16,128]{1,0:T(8,128)S(1)} %get-tuple-element.25), channel_id=1, source_target_pairs={{0,15},{1,8},{2,13},{3,14},{4,11},{5,12},{6,9},{7,10},{8,7},{9,6},... | collective-permute-start | bytes 24584 | tf_op jit(solution)/shard_map/ppermute | solution.py:718
  9.6 0.2 collective-permute-start.3
  9.8 1.3 %collective-permute-done.1.beyond = f32[64,512]{1,0:T(8,128)S(1)} collective-permute-done((f32[64,512]{1,0:T(8,128)S(1)}, f32[64,512]{1,0:T(8,128)S(1)}, u32[]{:S(2)}, u32[]{:S(2)}) %collective-permute-start.1) | collective-permute-done | bytes 131104 | tf_op jit(solution)/shard_map/ppermute | solution.py:718
  11.2 0.0 copy-start.2
  11.2 1.0 %shard_map.96 = (f32[24,128]{1,0:T(8,128)S(1)}, f32[24,128]{1,0:T(8,128)S(1)}, f32[144,512]{1,0:T(8,128)S(1)}, f32[16,128]{1,0:T(8,128)S(1)}, f32[72,128]{1,0:T(8,128)S(1)}) custom-call(f32[80,512]{1,0:T(8,128)S(1)} %get-tuple-element.23.inner, f32[64,512]{1,0:T(8,128)S(1)} %get-tuple-element.24.outer, f32[80,512]{1,0:T(8,128)S(1)} %collective-permute-done.sibling, ...), custom_call_target="tpu_custom_call" | custom-call | flops 819200 | bytes 962560 | tf_op jit(solution)/shard_map/pallas_call | solution.py:702
  12.1 2.3 %collective-permute-done.2.one = f32[16,128]{1,0:T(8,128)S(1)} collective-permute-done((f32[16,128]{1,0:T(8,128)S(1)}, f32[16,128]{1,0:T(8,128)S(1)}, u32[]{:S(2)}, u32[]{:S(2)}) %collective-permute-start.2) | collective-permute-done | bytes 8224 | tf_op jit(solution)/shard_map/ppermute | solution.py:718
  14.4 0.0 collective-permute-done.3.two
  14.4 1.6 %shard_map.97 = (f32[144,128]{1,0:T(8,128)S(1)}, f32[16,128]{1,0:T(8,128)}) custom-call(f32[24,128]{1,0:T(8,128)S(1)} %get-tuple-element.28.last, f32[24,128]{1,0:T(8,128)S(1)} %get-tuple-element.29.last_code, f32[72,128]{1,0:T(8,128)S(1)} %get-tuple-element.30.ours, f32[16,128]{1,0:T(8,128)S(1)} %collective-permute-done.2.one, ...), custom_call_target="tpu_custom_call" | custom-call | bytes 176128 | tf_op jit(solution)/shard_map/pallas_call | solution.py:702
  16.0 4.0 %all-to-all-start = ((f32[16,1,128]{2,1,0:T(1,128)}), f32[16,1,128]{2,1,0:T(1,128)S(1)}, u32[]{:S(2)}, u32[]{:S(2)}) async-start(f32[16,1,128]{2,1,0:T(1,128)} %bitcast.1), calls=%async_computation | async-start | bytes 16384 | tf_op jit(solution)/shard_map/all_to_all | solution.py:765
  20.0 0.0 copy-start
  20.0 0.0 copy-start.1
  20.0 0.0 copy-start.3
  20.0 0.0 copy-start.4
  20.0 0.1 shard_map.98.parts
  20.2 0.0 copy-done.2
  20.2 0.7 %copy-done = f32[16,8,512]{2,1,0:T(8,128)S(1)} copy-done((f32[16,8,512]{2,1,0:T(8,128)S(1)}, f32[16,8,512]{2,1,0:T(8,128)}, u32[]{:S(2)}) %copy-start) | copy-done | bytes 262168
  20.9 0.1 copy-done.1
  21.0 0.0 copy-done.3
  21.0 0.0 copy-done.4
  21.0 1.2 %shard_map.95 = f32[16,8,512]{2,1,0:T(8,128)} custom-call(f32[16,8,512]{2,1,0:T(8,128)S(1)} %copy-done.2, f32[16,8,512]{2,1,0:T(8,128)S(1)} %copy-done, f32[16,8,512]{2,1,0:T(8,128)S(1)} %copy-done.1, s32[8,512]{1,0:T(8,128)S(1)} %copy-done.3, f32[8,512]{1,0:T(8,128)S(1)} %copy-done.4, f32[80,512]{1,0:T(8,128)S(1)} %collective-permute-done.sibling, ...), custom_call_target="tpu_custom_call" | custom-call | flops 2621440 | bytes 1392640 | tf_op jit(solution)/shard_map/pallas_call | solution.py:702
  22.2 0.6 %shard_map.99 = (f32[16,8,512]{2,1,0:T(8,128)S(1)}, f32[16,8,512]{2,1,0:T(8,128)S(1)}, f32[8,512]{1,0:T(8,128)S(1)}) custom-call(f32[16,8,512]{2,1,0:T(8,128)S(1)} %copy-done, f32[16,8,512]{2,1,0:T(8,128)S(1)} %copy-done.1, s32[8,512]{1,0:T(8,128)S(1)} %copy-done.3, f32[8,512]{1,0:T(8,128)S(1)} %copy-done.4, f32[80,512]{1,0:T(8,128)S(1)} %collective-permute-done.sibling, ...), custom_call_target="tpu_custom_call" | custom-call | flops 2621440 | bytes 1409024 | tf_op jit(solution)/shard_map/pallas_call | solution.py:702
  22.8 1.2 %all-to-all-done = f32[16,1,128]{2,1,0:T(1,128)S(1)} async-done(((f32[16,1,128]{2,1,0:T(1,128)}), f32[16,1,128]{2,1,0:T(1,128)S(1)}, u32[]{:S(2)}, u32[]{:S(2)}) %all-to-all-start) | async-done | bytes 8224 | tf_op jit(solution)/shard_map/all_to_all | solution.py:765
  24.0 1.5 %shard_map.100 = (f32[16,8,512]{2,1,0:T(8,128)}, f32[16,8,512]{2,1,0:T(8,128)}, f32[8,512]{1,0:T(8,128)}) custom-call(f32[16,128]{1,0:T(8,128)S(1)} %bitcast.4, f32[144,512]{1,0:T(8,128)S(1)} %shard_map.98.parts, f32[16,8,512]{2,1,0:T(8,128)S(1)} %get-tuple-element.36.zonal, f32[16,8,512]{2,1,0:T(8,128)S(1)} %get-tuple-element.37.meridional, ...), custom_call_target="tpu_custom_call" | custom-call | bytes 1384448 | tf_op jit(solution)/shard_map/pallas_call | solution.py:702
Async XLA Ops:
  2.2 6.2 %collective-permute-start = (f32[80,512]{1,0:T(8,128)S(1)}, f32[80,512]{1,0:T(8,128)S(1)}, u32[]{:S(2)}, u32[]{:S(2)}) collective-permute-start(f32[80,512]{1,0:T(8,128)S(1)} %get-tuple-element.23.inner), channel_id=1, source_target_pairs={{0,1},{1,0},{2,3},{3,2},{4,5},{5,4},{6,7},{7,6},{8,9},{9,8},{10,11... | collective-permute-start | bytes 491528 | tf_op jit(solution)/shard_map/ppermute | solution.py:718
  2.8 8.4 %collective-permute-start.1 = (f32[64,512]{1,0:T(8,128)S(1)}, f32[64,512]{1,0:T(8,128)S(1)}, u32[]{:S(2)}, u32[]{:S(2)}) collective-permute-start(f32[64,512]{1,0:T(8,128)S(1)} %get-tuple-element.24.outer), channel_id=1, source_target_pairs={{0,15},{1,2},{2,1},{3,4},{4,3},{5,6},{6,5},{7,8},{8,7},{9,10},{10,... | collective-permute-start | bytes 393224 | tf_op jit(solution)/shard_map/ppermute | solution.py:718
  8.6 5.8 %collective-permute-start.2 = (f32[16,128]{1,0:T(8,128)S(1)}, f32[16,128]{1,0:T(8,128)S(1)}, u32[]{:S(2)}, u32[]{:S(2)}) collective-permute-start(f32[16,128]{1,0:T(8,128)S(1)} %get-tuple-element.25), channel_id=1, source_target_pairs={{0,15},{1,8},{2,13},{3,14},{4,11},{5,12},{6,9},{7,10},{8,7},{9,6},... | collective-permute-start | bytes 24584 | tf_op jit(solution)/shard_map/ppermute | solution.py:718
  9.6 4.8 %collective-permute-start.3 = (f32[16,128]{1,0:T(8,128)S(1)}, f32[16,128]{1,0:T(8,128)S(1)}, u32[]{:S(2)}, u32[]{:S(2)}) collective-permute-start(f32[16,128]{1,0:T(8,128)S(1)} %get-tuple-element.26), channel_id=1, source_target_pairs={{0,13},{1,14},{2,11},{3,12},{4,9},{5,10},{6,7},{7,8},{8,5},{9,0},{... | collective-permute-start | bytes 24584 | tf_op jit(solution)/shard_map/ppermute | solution.py:718
  11.2 9.0 %copy-start.2 = (f32[16,8,512]{2,1,0:T(8,128)S(1)}, f32[16,8,512]{2,1,0:T(8,128)}, u32[]{:S(2)}) copy-start(f32[16,8,512]{2,1,0:T(8,128)} %tracer.1) | copy-start | bytes 786436
  16.0 8.0 %all-to-all-start = ((f32[16,1,128]{2,1,0:T(1,128)}), f32[16,1,128]{2,1,0:T(1,128)S(1)}, u32[]{:S(2)}, u32[]{:S(2)}) async-start(f32[16,1,128]{2,1,0:T(1,128)} %bitcast.1), calls=%async_computation | async-start | bytes 16384 | tf_op jit(solution)/shard_map/all_to_all | solution.py:765
  20.0 0.9 %copy-start = (f32[16,8,512]{2,1,0:T(8,128)S(1)}, f32[16,8,512]{2,1,0:T(8,128)}, u32[]{:S(2)}) copy-start(f32[16,8,512]{2,1,0:T(8,128)} %zonal.3) | copy-start | bytes 786436
  20.0 1.0 %copy-start.1 = (f32[16,8,512]{2,1,0:T(8,128)S(1)}, f32[16,8,512]{2,1,0:T(8,128)}, u32[]{:S(2)}) copy-start(f32[16,8,512]{2,1,0:T(8,128)} %meridional.3) | copy-start | bytes 786436
  20.0 1.0 %copy-start.3 = (s32[8,512]{1,0:T(8,128)S(1)}, s32[8,512]{1,0:T(8,128)}, u32[]{:S(2)}) copy-start(s32[8,512]{1,0:T(8,128)} %count.3) | copy-start | bytes 49156
  20.0 1.0 %copy-start.4 = (f32[8,512]{1,0:T(8,128)S(1)}, f32[8,512]{1,0:T(8,128)}, u32[]{:S(2)}) copy-start(f32[8,512]{1,0:T(8,128)} %diffusivity.3) | copy-start | bytes 49156

commit v13 on v12

--- a/solution.py
+++ b/solution.py
@@ -590,11 +590,17 @@
 
 
 def finish_kernel(gram, parts, zonal, meridional, levels, zonal_next, meridional_next, height):
-    x = coefficients(gram)
+    solution_rows = coefficients(gram)
+    x = [
+        jnp.concatenate(
+            [jnp.broadcast_to(solution_rows[j:j + 1], (COLS, LANES))] * (NY // LANES), axis=1
+        )
+        for j in range(ITERS)
+    ]
 
     def combine(which):
         rows = [(3 * j + which) * COLS for j in range(ITERS)]
-        terms = [x[j:j + 1, :1] * parts[row:row + COLS] for j, row in enumerate(rows)]
+        terms = [x[j] * parts[row:row + COLS] for j, row in enumerate(rows)]
         pairs = [sum(terms[j + 1:j + 2], terms[j]) for j in range(0, ITERS, 2)]
         return sum(pairs[1:], pairs[0])
 

time: 25.7 us -> 25.7 us (level)
  no operation moved by 1% of the time
where the time goes in v13:
time: 25.7 us; the launch traced here: 25.4 us
  starting transfers between devices  11.4 us (44%)
  Pallas kernels  7.63 us (30%)
  waiting for transfers between devices  4.82 us (19%)
  local copies, waits for them, and re-layouts  0.85 us (3%)
  between operations  0.71 us (3%)
    pallas_call x8, Pallas kernels, call(): pl.pallas_call(kernel, out_shape=[jax.ShapeDtypeStruct(s, f32) for s in s...  7.63 us
    ppermute x4, starting transfers between devices, permute(): return lax.ppermute(value, 'lon', pairs)  7.45 us
    all_to_all x1, starting transfers between devices, body(): lax.all_to_all(gram, 'lon', 0, 0, tiled=True, axis_index_groups=[group])  3.97 us
    ppermute x4, waiting for transfers between devices, permute(): return lax.ppermute(value, 'lon', pairs)  3.6 us
    all_to_all x1, waiting for transfers between devices, body(): lax.all_to_all(gram, 'lon', 0, 0, tiled=True, axis_index_groups=[group])  1.23 us
    unnamed x10, local copies, waits for them, and re-layouts  0.85 us
  transfers between devices with their start and end apart: 5, of which 3 were waited for; matrix products, arithmetic and copies ran while one was open for 0% of the time, Pallas kernels for 12%

profile of v13, /device:TPU:0, one launch (start us, length us, event | category | flops | bytes accessed | tf_op | source)
XLA Modules:
  0.0 25.4 jit_solution(7680981132879543441)
XLA Ops:
  0.6 1.6 %shard_map.93 = (f32[80,512]{1,0:T(8,128)S(1)}, f32[64,512]{1,0:T(8,128)S(1)}) custom-call(f32[16,8,512]{2,1,0:T(8,128)} %tracer.1, f32[16,8,512]{2,1,0:T(8,128)} %zonal.3, f32[16,8,512]{2,1,0:T(8,128)} %meridional.3, s32[8,512]{1,0:T(8,128)} %count.3, f32[8,512]{1,0:T(8,128)} %diffusivity.3, f32[8,512]{1,0:T(8,128)} %surface_in.1), custom_call_target="tpu_custom_call" | custom-call | bytes 1130496 | tf_op jit(solution)/shard_map/pallas_call | solution.py:708
  2.2 0.5 %collective-permute-start = (f32[80,512]{1,0:T(8,128)S(1)}, f32[80,512]{1,0:T(8,128)S(1)}, u32[]{:S(2)}, u32[]{:S(2)}) collective-permute-start(f32[80,512]{1,0:T(8,128)S(1)} %get-tuple-element.23.inner), channel_id=1, source_target_pairs={{0,1},{1,0},{2,3},{3,2},{4,5},{5,4},{6,7},{7,6},{8,9},{9,8},{10,11... | collective-permute-start | bytes 491528 | tf_op jit(solution)/shard_map/ppermute | solution.py:724
  2.8 5.7 %collective-permute-start.1 = (f32[64,512]{1,0:T(8,128)S(1)}, f32[64,512]{1,0:T(8,128)S(1)}, u32[]{:S(2)}, u32[]{:S(2)}) collective-permute-start(f32[64,512]{1,0:T(8,128)S(1)} %get-tuple-element.24.outer), channel_id=1, source_target_pairs={{0,15},{1,2},{2,1},{3,4},{4,3},{5,6},{6,5},{7,8},{8,7},{9,10},{10,... | collective-permute-start | bytes 393224 | tf_op jit(solution)/shard_map/ppermute | solution.py:724
  8.4 0.0 collective-permute-done.sibling
  8.4 0.1 shard_map.94
  8.6 1.1 %collective-permute-start.2 = (f32[16,128]{1,0:T(8,128)S(1)}, f32[16,128]{1,0:T(8,128)S(1)}, u32[]{:S(2)}, u32[]{:S(2)}) collective-permute-start(f32[16,128]{1,0:T(8,128)S(1)} %get-tuple-element.25), channel_id=1, source_target_pairs={{0,15},{1,8},{2,13},{3,14},{4,11},{5,12},{6,9},{7,10},{8,7},{9,6},... | collective-permute-start | bytes 24584 | tf_op jit(solution)/shard_map/ppermute | solution.py:724
  9.6 0.2 collective-permute-start.3
  9.8 1.3 %collective-permute-done.1.beyond = f32[64,512]{1,0:T(8,128)S(1)} collective-permute-done((f32[64,512]{1,0:T(8,128)S(1)}, f32[64,512]{1,0:T(8,128)S(1)}, u32[]{:S(2)}, u32[]{:S(2)}) %collective-permute-start.1) | collective-permute-done | bytes 131104 | tf_op jit(solution)/shard_map/ppermute | solution.py:724
  11.2 0.0 copy-start.2
  11.2 1.0 %shard_map.96 = (f32[24,128]{1,0:T(8,128)S(1)}, f32[24,128]{1,0:T(8,128)S(1)}, f32[144,512]{1,0:T(8,128)S(1)}, f32[16,128]{1,0:T(8,128)S(1)}, f32[72,128]{1,0:T(8,128)S(1)}) custom-call(f32[80,512]{1,0:T(8,128)S(1)} %get-tuple-element.23.inner, f32[64,512]{1,0:T(8,128)S(1)} %get-tuple-element.24.outer, f32[80,512]{1,0:T(8,128)S(1)} %collective-permute-done.sibling, ...), custom_call_target="tpu_custom_call" | custom-call | flops 819200 | bytes 962560 | tf_op jit(solution)/shard_map/pallas_call | solution.py:708
  12.1 2.3 %collective-permute-done.2.one = f32[16,128]{1,0:T(8,128)S(1)} collective-permute-done((f32[16,128]{1,0:T(8,128)S(1)}, f32[16,128]{1,0:T(8,128)S(1)}, u32[]{:S(2)}, u32[]{:S(2)}) %collective-permute-start.2) | collective-permute-done | bytes 8224 | tf_op jit(solution)/shard_map/ppermute | solution.py:724
  14.4 0.0 collective-permute-done.3.two
  14.4 1.6 %shard_map.97 = (f32[144,128]{1,0:T(8,128)S(1)}, f32[16,128]{1,0:T(8,128)}) custom-call(f32[24,128]{1,0:T(8,128)S(1)} %get-tuple-element.28.last, f32[24,128]{1,0:T(8,128)S(1)} %get-tuple-element.29.last_code, f32[72,128]{1,0:T(8,128)S(1)} %get-tuple-element.30.ours, f32[16,128]{1,0:T(8,128)S(1)} %collective-permute-done.2.one, ...), custom_call_target="tpu_custom_call" | custom-call | bytes 176128 | tf_op jit(solution)/shard_map/pallas_call | solution.py:708
  16.0 4.0 %all-to-all-start = ((f32[16,1,128]{2,1,0:T(1,128)}), f32[16,1,128]{2,1,0:T(1,128)S(1)}, u32[]{:S(2)}, u32[]{:S(2)}) async-start(f32[16,1,128]{2,1,0:T(1,128)} %bitcast.1), calls=%async_computation | async-start | bytes 16384 | tf_op jit(solution)/shard_map/all_to_all | solution.py:771
  20.0 0.0 copy-start
  20.0 0.0 copy-start.1
  20.0 0.0 copy-start.3
  20.0 0.0 copy-start.4
  20.0 0.1 shard_map.98.parts
  20.2 0.0 copy-done.2
  20.2 0.7 %copy-done = f32[16,8,512]{2,1,0:T(8,128)S(1)} copy-done((f32[16,8,512]{2,1,0:T(8,128)S(1)}, f32[16,8,512]{2,1,0:T(8,128)}, u32[]{:S(2)}) %copy-start) | copy-done | bytes 262168
  20.9 0.1 copy-done.1
  21.0 0.0 copy-done.3
  21.0 0.0 copy-done.4
  21.0 1.2 %shard_map.95 = f32[16,8,512]{2,1,0:T(8,128)} custom-call(f32[16,8,512]{2,1,0:T(8,128)S(1)} %copy-done.2, f32[16,8,512]{2,1,0:T(8,128)S(1)} %copy-done, f32[16,8,512]{2,1,0:T(8,128)S(1)} %copy-done.1, s32[8,512]{1,0:T(8,128)S(1)} %copy-done.3, f32[8,512]{1,0:T(8,128)S(1)} %copy-done.4, f32[80,512]{1,0:T(8,128)S(1)} %collective-permute-done.sibling, ...), custom_call_target="tpu_custom_call" | custom-call | flops 2621440 | bytes 1392640 | tf_op jit(solution)/shard_map/pallas_call | solution.py:708
  22.2 0.6 %shard_map.99 = (f32[16,8,512]{2,1,0:T(8,128)S(1)}, f32[16,8,512]{2,1,0:T(8,128)S(1)}, f32[8,512]{1,0:T(8,128)S(1)}) custom-call(f32[16,8,512]{2,1,0:T(8,128)S(1)} %copy-done, f32[16,8,512]{2,1,0:T(8,128)S(1)} %copy-done.1, s32[8,512]{1,0:T(8,128)S(1)} %copy-done.3, f32[8,512]{1,0:T(8,128)S(1)} %copy-done.4, f32[80,512]{1,0:T(8,128)S(1)} %collective-permute-done.sibling, ...), custom_call_target="tpu_custom_call" | custom-call | flops 2621440 | bytes 1409024 | tf_op jit(solution)/shard_map/pallas_call | solution.py:708
  22.8 1.2 %all-to-all-done = f32[16,1,128]{2,1,0:T(1,128)S(1)} async-done(((f32[16,1,128]{2,1,0:T(1,128)}), f32[16,1,128]{2,1,0:T(1,128)S(1)}, u32[]{:S(2)}, u32[]{:S(2)}) %all-to-all-start) | async-done | bytes 8224 | tf_op jit(solution)/shard_map/all_to_all | solution.py:771
  24.0 1.4 %shard_map.100 = (f32[16,8,512]{2,1,0:T(8,128)}, f32[16,8,512]{2,1,0:T(8,128)}, f32[8,512]{1,0:T(8,128)}) custom-call(f32[16,128]{1,0:T(8,128)S(1)} %bitcast.4, f32[144,512]{1,0:T(8,128)S(1)} %shard_map.98.parts, f32[16,8,512]{2,1,0:T(8,128)S(1)} %get-tuple-element.36.zonal, f32[16,8,512]{2,1,0:T(8,128)S(1)} %get-tuple-element.37.meridional, ...), custom_call_target="tpu_custom_call" | custom-call | bytes 1384448 | tf_op jit(solution)/shard_map/pallas_call | solution.py:708
Async XLA Ops:
  2.2 6.2 %collective-permute-start = (f32[80,512]{1,0:T(8,128)S(1)}, f32[80,512]{1,0:T(8,128)S(1)}, u32[]{:S(2)}, u32[]{:S(2)}) collective-permute-start(f32[80,512]{1,0:T(8,128)S(1)} %get-tuple-element.23.inner), channel_id=1, source_target_pairs={{0,1},{1,0},{2,3},{3,2},{4,5},{5,4},{6,7},{7,6},{8,9},{9,8},{10,11... | collective-permute-start | bytes 491528 | tf_op jit(solution)/shard_map/ppermute | solution.py:724
  2.8 8.4 %collective-permute-start.1 = (f32[64,512]{1,0:T(8,128)S(1)}, f32[64,512]{1,0:T(8,128)S(1)}, u32[]{:S(2)}, u32[]{:S(2)}) collective-permute-start(f32[64,512]{1,0:T(8,128)S(1)} %get-tuple-element.24.outer), channel_id=1, source_target_pairs={{0,15},{1,2},{2,1},{3,4},{4,3},{5,6},{6,5},{7,8},{8,7},{9,10},{10,... | collective-permute-start | bytes 393224 | tf_op jit(solution)/shard_map/ppermute | solution.py:724
  8.6 5.8 %collective-permute-start.2 = (f32[16,128]{1,0:T(8,128)S(1)}, f32[16,128]{1,0:T(8,128)S(1)}, u32[]{:S(2)}, u32[]{:S(2)}) collective-permute-start(f32[16,128]{1,0:T(8,128)S(1)} %get-tuple-element.25), channel_id=1, source_target_pairs={{0,15},{1,8},{2,13},{3,14},{4,11},{5,12},{6,9},{7,10},{8,7},{9,6},... | collective-permute-start | bytes 24584 | tf_op jit(solution)/shard_map/ppermute | solution.py:724
  9.6 4.8 %collective-permute-start.3 = (f32[16,128]{1,0:T(8,128)S(1)}, f32[16,128]{1,0:T(8,128)S(1)}, u32[]{:S(2)}, u32[]{:S(2)}) collective-permute-start(f32[16,128]{1,0:T(8,128)S(1)} %get-tuple-element.26), channel_id=1, source_target_pairs={{0,13},{1,14},{2,11},{3,12},{4,9},{5,10},{6,7},{7,8},{8,5},{9,0},{... | collective-permute-start | bytes 24584 | tf_op jit(solution)/shard_map/ppermute | solution.py:724
  11.2 9.0 %copy-start.2 = (f32[16,8,512]{2,1,0:T(8,128)S(1)}, f32[16,8,512]{2,1,0:T(8,128)}, u32[]{:S(2)}) copy-start(f32[16,8,512]{2,1,0:T(8,128)} %tracer.1) | copy-start | bytes 786436
  16.0 8.0 %all-to-all-start = ((f32[16,1,128]{2,1,0:T(1,128)}), f32[16,1,128]{2,1,0:T(1,128)S(1)}, u32[]{:S(2)}, u32[]{:S(2)}) async-start(f32[16,1,128]{2,1,0:T(1,128)} %bitcast.1), calls=%async_computation | async-start | bytes 16384 | tf_op jit(solution)/shard_map/all_to_all | solution.py:771
  20.0 0.9 %copy-start = (f32[16,8,512]{2,1,0:T(8,128)S(1)}, f32[16,8,512]{2,1,0:T(8,128)}, u32[]{:S(2)}) copy-start(f32[16,8,512]{2,1,0:T(8,128)} %zonal.3) | copy-start | bytes 786436
  20.0 1.0 %copy-start.1 = (f32[16,8,512]{2,1,0:T(8,128)S(1)}, f32[16,8,512]{2,1,0:T(8,128)}, u32[]{:S(2)}) copy-start(f32[16,8,512]{2,1,0:T(8,128)} %meridional.3) | copy-start | bytes 786436
  20.0 1.0 %copy-start.3 = (s32[8,512]{1,0:T(8,128)S(1)}, s32[8,512]{1,0:T(8,128)}, u32[]{:S(2)}) copy-start(s32[8,512]{1,0:T(8,128)} %count.3) | copy-start | bytes 49156
  20.0 1.0 %copy-start.4 = (f32[8,512]{1,0:T(8,128)S(1)}, f32[8,512]{1,0:T(8,128)}, u32[]{:S(2)}) copy-start(f32[8,512]{1,0:T(8,128)} %diffusivity.3) | copy-start | bytes 49156

commit v14 on v13

--- a/solution.py
+++ b/solution.py
@@ -205,6 +205,7 @@
     fold = jnp.where(level.astype(f32) < lc_fold, fold, 0.0)
     momentum = roll(fold, LANE_P - LANE_MU, 1) + roll(fold, LANE_P - LANE_MV, 1)
     fold = jnp.where((tile_lane >= LANE_P) & (tile_lane < LANE_P + K), momentum, fold)
+    fold = jnp.where(tile_lane < K, jnp.where(tile_lane.astype(f32) < lc_fold, 1.0, 0.0), fold)
     fold = jnp.where(tile_lane == LANE_LC, lc_fold, fold)
     fold = jnp.where(tile_lane == LANE_DIFF, diff[:, NY - 1:], fold)
     edge_level = iota((K, NY), 0).astype(f32)
@@ -453,9 +454,10 @@
     lane = iota((EXT, LANES), 1)
     level = (lane - LANE_P).astype(f32)
     weight = jnp.where((lane >= LANE_P) & (lane < LANE_P + K), 0.5 * (0.5 + level / K), 0.0)
-    ours[:EXT] = jnp.where(level < mine[:, LANE_LC:LANE_LC + 1], weight, 0.0)
-    ours[EXT:2 * EXT] = weight * mine
-    ours[2 * EXT:] = jnp.where(lane == LANE_F - 1, mine[:, LANE_DIFF:LANE_DIFF + 1], 0.0)
+    ours[:EXT] = jnp.where(level < mine[:, LANE_LC:LANE_LC + 1], weight, 0.0) + roll(
+        weight * mine, -LANE_P, 1
+    )
+    ours[EXT:] = jnp.where(lane == LANE_F - 1, mine[:, LANE_DIFF:LANE_DIFF + 1], 0.0)
 
 
 def fold_kernel(
@@ -464,16 +466,11 @@
     even = is_even()
     lane = iota((EXT, LANES), 1)
     theirs, between = across_fold(even, *patch_order(one[...], two[...], near[...]))
-    level = (lane - LANE_P).astype(f32)
-    flux = -jnp.sum(
-        ours[:EXT] * theirs
-        + jnp.where(level < theirs[:, LANE_LC:LANE_LC + 1], ours[EXT:2 * EXT], 0.0),
-        axis=1, keepdims=True,
-    )
+    flux = -jnp.sum(ours[:EXT] * theirs, axis=1, keepdims=True)
     far_change = theirs[:, LANE_DIFF:LANE_DIFF + 1] * flux
     beyond_fold = lane >= LANE_F
     start = jnp.where(beyond_fold, theirs, last[...]) + between
-    start = start + jnp.where(lane == LANE_F, far_change, ours[2 * EXT:] * flux)
+    start = start + jnp.where(lane == LANE_F, far_change, ours[EXT:] * flux)
     code = jnp.where(beyond_fold, roll(theirs, LANE_F - LANE_CODE, 1), last_code[...])
     v = basis(start, code)
     for j in range(ITERS):
@@ -747,7 +744,7 @@
     last, last_code, vectors, partial, ours = call(
         inner_kernel,
         [
-            window, window, (ITERS * EXT, NY), (2 * COLS, LANES), (3 * EXT, LANES),
+            window, window, (ITERS * EXT, NY), (2 * COLS, LANES), (2 * EXT, LANES),
         ],
         inner, outer, sibling, beyond, tile, flops=8192 * 100,
     )

time: 25.7 us -> 25.6 us (level)
  no operation moved by 1% of the time
where the time goes in v14:
time: 25.6 us; the launch traced here: 25.4 us
  starting transfers between devices  11.4 us (45%)
  Pallas kernels  7.57 us (30%)
  waiting for transfers between devices  4.82 us (19%)
  local copies, waits for them, and re-layouts  0.85 us (3%)
  between operations  0.71 us (3%)
    pallas_call x8, Pallas kernels, call(): pl.pallas_call(kernel, out_shape=[jax.ShapeDtypeStruct(s, f32) for s in s...  7.57 us
    ppermute x4, starting transfers between devices, permute(): return lax.ppermute(value, 'lon', pairs)  7.45 us
    all_to_all x1, starting transfers between devices, body(): lax.all_to_all(gram, 'lon', 0, 0, tiled=True, axis_index_groups=[group])  3.97 us
    ppermute x4, waiting for transfers between devices, permute(): return lax.ppermute(value, 'lon', pairs)  3.59 us
    all_to_all x1, waiting for transfers between devices, body(): lax.all_to_all(gram, 'lon', 0, 0, tiled=True, axis_index_groups=[group])  1.23 us
    unnamed x10, local copies, waits for them, and re-layouts  0.85 us
  transfers between devices with their start and end apart: 5, of which 3 were waited for; matrix products, arithmetic and copies ran while one was open for 0% of the time, Pallas kernels for 12%

profile of v14, /device:TPU:0, one launch (start us, length us, event | category | flops | bytes accessed | tf_op | source)
XLA Modules:
  0.0 25.4 jit_solution(11856430152057289786)
XLA Ops:
  0.6 1.6 %shard_map.93 = (f32[80,512]{1,0:T(8,128)S(1)}, f32[64,512]{1,0:T(8,128)S(1)}) custom-call(f32[16,8,512]{2,1,0:T(8,128)} %tracer.1, f32[16,8,512]{2,1,0:T(8,128)} %zonal.3, f32[16,8,512]{2,1,0:T(8,128)} %meridional.3, s32[8,512]{1,0:T(8,128)} %count.3, f32[8,512]{1,0:T(8,128)} %diffusivity.3, f32[8,512]{1,0:T(8,128)} %surface_in.1), custom_call_target="tpu_custom_call" | custom-call | bytes 1130496 | tf_op jit(solution)/shard_map/pallas_call | solution.py:705
  2.2 0.5 %collective-permute-start = (f32[80,512]{1,0:T(8,128)S(1)}, f32[80,512]{1,0:T(8,128)S(1)}, u32[]{:S(2)}, u32[]{:S(2)}) collective-permute-start(f32[80,512]{1,0:T(8,128)S(1)} %get-tuple-element.23.inner), channel_id=1, source_target_pairs={{0,1},{1,0},{2,3},{3,2},{4,5},{5,4},{6,7},{7,6},{8,9},{9,8},{10,11... | collective-permute-start | bytes 491528 | tf_op jit(solution)/shard_map/ppermute | solution.py:721
  2.8 5.7 %collective-permute-start.1 = (f32[64,512]{1,0:T(8,128)S(1)}, f32[64,512]{1,0:T(8,128)S(1)}, u32[]{:S(2)}, u32[]{:S(2)}) collective-permute-start(f32[64,512]{1,0:T(8,128)S(1)} %get-tuple-element.24.outer), channel_id=1, source_target_pairs={{0,15},{1,2},{2,1},{3,4},{4,3},{5,6},{6,5},{7,8},{8,7},{9,10},{10,... | collective-permute-start | bytes 393224 | tf_op jit(solution)/shard_map/ppermute | solution.py:721
  8.4 0.0 collective-permute-done.sibling
  8.4 0.1 shard_map.94
  8.6 1.1 %collective-permute-start.2 = (f32[16,128]{1,0:T(8,128)S(1)}, f32[16,128]{1,0:T(8,128)S(1)}, u32[]{:S(2)}, u32[]{:S(2)}) collective-permute-start(f32[16,128]{1,0:T(8,128)S(1)} %get-tuple-element.25), channel_id=1, source_target_pairs={{0,15},{1,8},{2,13},{3,14},{4,11},{5,12},{6,9},{7,10},{8,7},{9,6},... | collective-permute-start | bytes 24584 | tf_op jit(solution)/shard_map/ppermute | solution.py:721
  9.6 0.2 collective-permute-start.3
  9.8 1.3 %collective-permute-done.1.beyond = f32[64,512]{1,0:T(8,128)S(1)} collective-permute-done((f32[64,512]{1,0:T(8,128)S(1)}, f32[64,512]{1,0:T(8,128)S(1)}, u32[]{:S(2)}, u32[]{:S(2)}) %collective-permute-start.1) | collective-permute-done | bytes 131104 | tf_op jit(solution)/shard_map/ppermute | solution.py:721
  11.2 0.0 copy-start.2
  11.2 1.0 %shard_map.96 = (f32[24,128]{1,0:T(8,128)S(1)}, f32[24,128]{1,0:T(8,128)S(1)}, f32[144,512]{1,0:T(8,128)S(1)}, f32[16,128]{1,0:T(8,128)S(1)}, f32[48,128]{1,0:T(8,128)S(1)}) custom-call(f32[80,512]{1,0:T(8,128)S(1)} %get-tuple-element.23.inner, f32[64,512]{1,0:T(8,128)S(1)} %get-tuple-element.24.outer, f32[80,512]{1,0:T(8,128)S(1)} %collective-permute-done.sibling, ...), custom_call_target="tpu_custom_call" | custom-call | flops 819200 | bytes 950272 | tf_op jit(solution)/shard_map/pallas_call | solution.py:705
  12.1 2.3 %collective-permute-done.2.one = f32[16,128]{1,0:T(8,128)S(1)} collective-permute-done((f32[16,128]{1,0:T(8,128)S(1)}, f32[16,128]{1,0:T(8,128)S(1)}, u32[]{:S(2)}, u32[]{:S(2)}) %collective-permute-start.2) | collective-permute-done | bytes 8224 | tf_op jit(solution)/shard_map/ppermute | solution.py:721
  14.4 0.0 collective-permute-done.3.two
  14.4 1.6 %shard_map.97 = (f32[144,128]{1,0:T(8,128)S(1)}, f32[16,128]{1,0:T(8,128)}) custom-call(f32[24,128]{1,0:T(8,128)S(1)} %get-tuple-element.28.last, f32[24,128]{1,0:T(8,128)S(1)} %get-tuple-element.29.last_code, f32[48,128]{1,0:T(8,128)S(1)} %get-tuple-element.30.ours, f32[16,128]{1,0:T(8,128)S(1)} %collective-permute-done.2.one, ...), custom_call_target="tpu_custom_call" | custom-call | bytes 163840 | tf_op jit(solution)/shard_map/pallas_call | solution.py:705
  16.0 4.0 %all-to-all-start = ((f32[16,1,128]{2,1,0:T(1,128)}), f32[16,1,128]{2,1,0:T(1,128)S(1)}, u32[]{:S(2)}, u32[]{:S(2)}) async-start(f32[16,1,128]{2,1,0:T(1,128)} %bitcast.1), calls=%async_computation | async-start | bytes 16384 | tf_op jit(solution)/shard_map/all_to_all | solution.py:768
  19.9 0.0 copy-start
  19.9 0.0 copy-start.1
  19.9 0.0 copy-start.3
  20.0 0.0 copy-start.4
  20.0 0.1 shard_map.98.parts
  20.1 0.0 copy-done.2
  20.1 0.7 %copy-done = f32[16,8,512]{2,1,0:T(8,128)S(1)} copy-done((f32[16,8,512]{2,1,0:T(8,128)S(1)}, f32[16,8,512]{2,1,0:T(8,128)}, u32[]{:S(2)}) %copy-start) | copy-done | bytes 262168
  20.9 0.1 copy-done.1
  21.0 0.0 copy-done.3
  21.0 0.0 copy-done.4
  21.0 1.2 %shard_map.95 = f32[16,8,512]{2,1,0:T(8,128)} custom-call(f32[16,8,512]{2,1,0:T(8,128)S(1)} %copy-done.2, f32[16,8,512]{2,1,0:T(8,128)S(1)} %copy-done, f32[16,8,512]{2,1,0:T(8,128)S(1)} %copy-done.1, s32[8,512]{1,0:T(8,128)S(1)} %copy-done.3, f32[8,512]{1,0:T(8,128)S(1)} %copy-done.4, f32[80,512]{1,0:T(8,128)S(1)} %collective-permute-done.sibling, ...), custom_call_target="tpu_custom_call" | custom-call | flops 2621440 | bytes 1392640 | tf_op jit(solution)/shard_map/pallas_call | solution.py:705
  22.1 0.6 %shard_map.99 = (f32[16,8,512]{2,1,0:T(8,128)S(1)}, f32[16,8,512]{2,1,0:T(8,128)S(1)}, f32[8,512]{1,0:T(8,128)S(1)}) custom-call(f32[16,8,512]{2,1,0:T(8,128)S(1)} %copy-done, f32[16,8,512]{2,1,0:T(8,128)S(1)} %copy-done.1, s32[8,512]{1,0:T(8,128)S(1)} %copy-done.3, f32[8,512]{1,0:T(8,128)S(1)} %copy-done.4, f32[80,512]{1,0:T(8,128)S(1)} %collective-permute-done.sibling, ...), custom_call_target="tpu_custom_call" | custom-call | flops 2621440 | bytes 1409024 | tf_op jit(solution)/shard_map/pallas_call | solution.py:705
  22.7 1.2 %all-to-all-done = f32[16,1,128]{2,1,0:T(1,128)S(1)} async-done(((f32[16,1,128]{2,1,0:T(1,128)}), f32[16,1,128]{2,1,0:T(1,128)S(1)}, u32[]{:S(2)}, u32[]{:S(2)}) %all-to-all-start) | async-done | bytes 8224 | tf_op jit(solution)/shard_map/all_to_all | solution.py:768
  23.9 1.4 %shard_map.100 = (f32[16,8,512]{2,1,0:T(8,128)}, f32[16,8,512]{2,1,0:T(8,128)}, f32[8,512]{1,0:T(8,128)}) custom-call(f32[16,128]{1,0:T(8,128)S(1)} %bitcast.4, f32[144,512]{1,0:T(8,128)S(1)} %shard_map.98.parts, f32[16,8,512]{2,1,0:T(8,128)S(1)} %get-tuple-element.36.zonal, f32[16,8,512]{2,1,0:T(8,128)S(1)} %get-tuple-element.37.meridional, ...), custom_call_target="tpu_custom_call" | custom-call | bytes 1384448 | tf_op jit(solution)/shard_map/pallas_call | solution.py:705
Async XLA Ops:
  2.2 6.2 %collective-permute-start = (f32[80,512]{1,0:T(8,128)S(1)}, f32[80,512]{1,0:T(8,128)S(1)}, u32[]{:S(2)}, u32[]{:S(2)}) collective-permute-start(f32[80,512]{1,0:T(8,128)S(1)} %get-tuple-element.23.inner), channel_id=1, source_target_pairs={{0,1},{1,0},{2,3},{3,2},{4,5},{5,4},{6,7},{7,6},{8,9},{9,8},{10,11... | collective-permute-start | bytes 491528 | tf_op jit(solution)/shard_map/ppermute | solution.py:721
  2.8 8.4 %collective-permute-start.1 = (f32[64,512]{1,0:T(8,128)S(1)}, f32[64,512]{1,0:T(8,128)S(1)}, u32[]{:S(2)}, u32[]{:S(2)}) collective-permute-start(f32[64,512]{1,0:T(8,128)S(1)} %get-tuple-element.24.outer), channel_id=1, source_target_pairs={{0,15},{1,2},{2,1},{3,4},{4,3},{5,6},{6,5},{7,8},{8,7},{9,10},{10,... | collective-permute-start | bytes 393224 | tf_op jit(solution)/shard_map/ppermute | solution.py:721
  8.6 5.8 %collective-permute-start.2 = (f32[16,128]{1,0:T(8,128)S(1)}, f32[16,128]{1,0:T(8,128)S(1)}, u32[]{:S(2)}, u32[]{:S(2)}) collective-permute-start(f32[16,128]{1,0:T(8,128)S(1)} %get-tuple-element.25), channel_id=1, source_target_pairs={{0,15},{1,8},{2,13},{3,14},{4,11},{5,12},{6,9},{7,10},{8,7},{9,6},... | collective-permute-start | bytes 24584 | tf_op jit(solution)/shard_map/ppermute | solution.py:721
  9.6 4.8 %collective-permute-start.3 = (f32[16,128]{1,0:T(8,128)S(1)}, f32[16,128]{1,0:T(8,128)S(1)}, u32[]{:S(2)}, u32[]{:S(2)}) collective-permute-start(f32[16,128]{1,0:T(8,128)S(1)} %get-tuple-element.26), channel_id=1, source_target_pairs={{0,13},{1,14},{2,11},{3,12},{4,9},{5,10},{6,7},{7,8},{8,5},{9,0},{... | collective-permute-start | bytes 24584 | tf_op jit(solution)/shard_map/ppermute | solution.py:721
  11.2 9.0 %copy-start.2 = (f32[16,8,512]{2,1,0:T(8,128)S(1)}, f32[16,8,512]{2,1,0:T(8,128)}, u32[]{:S(2)}) copy-start(f32[16,8,512]{2,1,0:T(8,128)} %tracer.1) | copy-start | bytes 786436
  16.0 8.0 %all-to-all-start = ((f32[16,1,128]{2,1,0:T(1,128)}), f32[16,1,128]{2,1,0:T(1,128)S(1)}, u32[]{:S(2)}, u32[]{:S(2)}) async-start(f32[16,1,128]{2,1,0:T(1,128)} %bitcast.1), calls=%async_computation | async-start | bytes 16384 | tf_op jit(solution)/shard_map/all_to_all | solution.py:768
  19.9 0.9 %copy-start = (f32[16,8,512]{2,1,0:T(8,128)S(1)}, f32[16,8,512]{2,1,0:T(8,128)}, u32[]{:S(2)}) copy-start(f32[16,8,512]{2,1,0:T(8,128)} %zonal.3) | copy-start | bytes 786436
  19.9 1.0 %copy-start.1 = (f32[16,8,512]{2,1,0:T(8,128)S(1)}, f32[16,8,512]{2,1,0:T(8,128)}, u32[]{:S(2)}) copy-start(f32[16,8,512]{2,1,0:T(8,128)} %meridional.3) | copy-start | bytes 786436
  19.9 1.0 %copy-start.3 = (s32[8,512]{1,0:T(8,128)S(1)}, s32[8,512]{1,0:T(8,128)}, u32[]{:S(2)}) copy-start(s32[8,512]{1,0:T(8,128)} %count.3) | copy-start | bytes 49156
  20.0 1.0 %copy-start.4 = (f32[8,512]{1,0:T(8,128)S(1)}, f32[8,512]{1,0:T(8,128)}, u32[]{:S(2)}) copy-start(f32[8,512]{1,0:T(8,128)} %diffusivity.3) | copy-start | bytes 49156

commit v15 on v14

--- a/solution.py
+++ b/solution.py
@@ -491,18 +491,21 @@
     total = pair_norm(pair_rows(pair_tree([(t, roll(t, -GROUPS * COLS, 1)) for t in tiles])))
     wide = lambda column: jnp.broadcast_to(column, shape)
     sub = iota(shape, 0)
-    tile_lane = iota(shape, 1)
+    zero = jnp.zeros(shape, f32)
+
+    spread = {}
+    for i in range(BASIS):
+        for j in range(i, BASIS):
+            at = i * (2 * BASIS - 1 - i) // 2 + j
+            spread[i, j] = spread[j, i] = tuple(wide(part[:, at:at + 1]) for part in total)
 
     def column(j):
-        low, high = jnp.minimum(sub, j), jnp.maximum(sub, j)
-        entry = ((low * (2 * BASIS - 1 - low)) >> 1) + high
-        here = (tile_lane == entry) & (sub < BASIS)
-        return tuple(
-            wide(jnp.sum(jnp.where(here, part, 0.0), axis=1, keepdims=True)) for part in total
-        )
+        result = (zero, zero)
+        for i in range(BASIS):
+            result = tuple(jnp.where(sub == i, a, b) for a, b in zip(spread[i, j], result))
+        return result
 
     matrix = [column(j) for j in range(BASIS)]
-    zero = jnp.zeros(shape, f32)
     half = scale / 2
 
     def times_power(pair, factor):

time: 25.6 us -> 25.7 us (level)
  no operation moved by 1% of the time
where the time goes in v15:
time: 25.7 us; the launch traced here: 25.4 us
  starting transfers between devices  11.4 us (44%)
  Pallas kernels  7.62 us (30%)
  waiting for transfers between devices  4.82 us (19%)
  local copies, waits for them, and re-layouts  0.85 us (3%)
  between operations  0.71 us (3%)
    pallas_call x8, Pallas kernels, call(): pl.pallas_call(kernel, out_shape=[jax.ShapeDtypeStruct(s, f32) for s in s...  7.62 us
    ppermute x4, starting transfers between devices, permute(): return lax.ppermute(value, 'lon', pairs)  7.45 us
    all_to_all x1, starting transfers between devices, body(): lax.all_to_all(gram, 'lon', 0, 0, tiled=True, axis_index_groups=[group])  3.97 us
    ppermute x4, waiting for transfers between devices, permute(): return lax.ppermute(value, 'lon', pairs)  3.59 us
    all_to_all x1, waiting for transfers between devices, body(): lax.all_to_all(gram, 'lon', 0, 0, tiled=True, axis_index_groups=[group])  1.23 us
    unnamed x10, local copies, waits for them, and re-layouts  0.85 us
  transfers between devices with their start and end apart: 5, of which 3 were waited for; matrix products, arithmetic and copies ran while one was open for 0% of the time, Pallas kernels for 12%

profile of v15, /device:TPU:0, one launch (start us, length us, event | category | flops | bytes accessed | tf_op | source)
XLA Modules:
  0.0 25.4 jit_solution(5837702938365232900)
XLA Ops:
  0.6 1.6 %shard_map.93 = (f32[80,512]{1,0:T(8,128)S(1)}, f32[64,512]{1,0:T(8,128)S(1)}) custom-call(f32[16,8,512]{2,1,0:T(8,128)} %tracer.1, f32[16,8,512]{2,1,0:T(8,128)} %zonal.3, f32[16,8,512]{2,1,0:T(8,128)} %meridional.3, s32[8,512]{1,0:T(8,128)} %count.3, f32[8,512]{1,0:T(8,128)} %diffusivity.3, f32[8,512]{1,0:T(8,128)} %surface_in.1), custom_call_target="tpu_custom_call" | custom-call | bytes 1130496 | tf_op jit(solution)/shard_map/pallas_call | solution.py:708
  2.2 0.5 %collective-permute-start = (f32[80,512]{1,0:T(8,128)S(1)}, f32[80,512]{1,0:T(8,128)S(1)}, u32[]{:S(2)}, u32[]{:S(2)}) collective-permute-start(f32[80,512]{1,0:T(8,128)S(1)} %get-tuple-element.23.inner), channel_id=1, source_target_pairs={{0,1},{1,0},{2,3},{3,2},{4,5},{5,4},{6,7},{7,6},{8,9},{9,8},{10,11... | collective-permute-start | bytes 491528 | tf_op jit(solution)/shard_map/ppermute | solution.py:724
  2.8 5.7 %collective-permute-start.1 = (f32[64,512]{1,0:T(8,128)S(1)}, f32[64,512]{1,0:T(8,128)S(1)}, u32[]{:S(2)}, u32[]{:S(2)}) collective-permute-start(f32[64,512]{1,0:T(8,128)S(1)} %get-tuple-element.24.outer), channel_id=1, source_target_pairs={{0,15},{1,2},{2,1},{3,4},{4,3},{5,6},{6,5},{7,8},{8,7},{9,10},{10,... | collective-permute-start | bytes 393224 | tf_op jit(solution)/shard_map/ppermute | solution.py:724
  8.4 0.0 collective-permute-done.sibling
  8.4 0.1 shard_map.94
  8.6 1.1 %collective-permute-start.2 = (f32[16,128]{1,0:T(8,128)S(1)}, f32[16,128]{1,0:T(8,128)S(1)}, u32[]{:S(2)}, u32[]{:S(2)}) collective-permute-start(f32[16,128]{1,0:T(8,128)S(1)} %get-tuple-element.25), channel_id=1, source_target_pairs={{0,15},{1,8},{2,13},{3,14},{4,11},{5,12},{6,9},{7,10},{8,7},{9,6},... | collective-permute-start | bytes 24584 | tf_op jit(solution)/shard_map/ppermute | solution.py:724
  9.6 0.2 collective-permute-start.3
  9.8 1.3 %collective-permute-done.1.beyond = f32[64,512]{1,0:T(8,128)S(1)} collective-permute-done((f32[64,512]{1,0:T(8,128)S(1)}, f32[64,512]{1,0:T(8,128)S(1)}, u32[]{:S(2)}, u32[]{:S(2)}) %collective-permute-start.1) | collective-permute-done | bytes 131104 | tf_op jit(solution)/shard_map/ppermute | solution.py:724
  11.2 0.0 copy-start.2
  11.2 1.0 %shard_map.96 = (f32[24,128]{1,0:T(8,128)S(1)}, f32[24,128]{1,0:T(8,128)S(1)}, f32[144,512]{1,0:T(8,128)S(1)}, f32[16,128]{1,0:T(8,128)S(1)}, f32[48,128]{1,0:T(8,128)S(1)}) custom-call(f32[80,512]{1,0:T(8,128)S(1)} %get-tuple-element.23.inner, f32[64,512]{1,0:T(8,128)S(1)} %get-tuple-element.24.outer, f32[80,512]{1,0:T(8,128)S(1)} %collective-permute-done.sibling, ...), custom_call_target="tpu_custom_call" | custom-call | flops 819200 | bytes 950272 | tf_op jit(solution)/shard_map/pallas_call | solution.py:708
  12.1 2.3 %collective-permute-done.2.one = f32[16,128]{1,0:T(8,128)S(1)} collective-permute-done((f32[16,128]{1,0:T(8,128)S(1)}, f32[16,128]{1,0:T(8,128)S(1)}, u32[]{:S(2)}, u32[]{:S(2)}) %collective-permute-start.2) | collective-permute-done | bytes 8224 | tf_op jit(solution)/shard_map/ppermute | solution.py:724
  14.4 0.0 collective-permute-done.3.two
  14.4 1.6 %shard_map.97 = (f32[144,128]{1,0:T(8,128)S(1)}, f32[16,128]{1,0:T(8,128)}) custom-call(f32[24,128]{1,0:T(8,128)S(1)} %get-tuple-element.28.last, f32[24,128]{1,0:T(8,128)S(1)} %get-tuple-element.29.last_code, f32[48,128]{1,0:T(8,128)S(1)} %get-tuple-element.30.ours, f32[16,128]{1,0:T(8,128)S(1)} %collective-permute-done.2.one, ...), custom_call_target="tpu_custom_call" | custom-call | bytes 163840 | tf_op jit(solution)/shard_map/pallas_call | solution.py:708
  16.0 4.0 %all-to-all-start = ((f32[16,1,128]{2,1,0:T(1,128)}), f32[16,1,128]{2,1,0:T(1,128)S(1)}, u32[]{:S(2)}, u32[]{:S(2)}) async-start(f32[16,1,128]{2,1,0:T(1,128)} %bitcast.1), calls=%async_computation | async-start | bytes 16384 | tf_op jit(solution)/shard_map/all_to_all | solution.py:771
  19.9 0.0 copy-start
  19.9 0.0 copy-start.1
  19.9 0.0 copy-start.3
  20.0 0.0 copy-start.4
  20.0 0.1 shard_map.98.parts
  20.1 0.0 copy-done.2
  20.1 0.7 %copy-done = f32[16,8,512]{2,1,0:T(8,128)S(1)} copy-done((f32[16,8,512]{2,1,0:T(8,128)S(1)}, f32[16,8,512]{2,1,0:T(8,128)}, u32[]{:S(2)}) %copy-start) | copy-done | bytes 262168
  20.9 0.1 copy-done.1
  21.0 0.0 copy-done.3
  21.0 0.0 copy-done.4
  21.0 1.2 %shard_map.95 = f32[16,8,512]{2,1,0:T(8,128)} custom-call(f32[16,8,512]{2,1,0:T(8,128)S(1)} %copy-done.2, f32[16,8,512]{2,1,0:T(8,128)S(1)} %copy-done, f32[16,8,512]{2,1,0:T(8,128)S(1)} %copy-done.1, s32[8,512]{1,0:T(8,128)S(1)} %copy-done.3, f32[8,512]{1,0:T(8,128)S(1)} %copy-done.4, f32[80,512]{1,0:T(8,128)S(1)} %collective-permute-done.sibling, ...), custom_call_target="tpu_custom_call" | custom-call | flops 2621440 | bytes 1392640 | tf_op jit(solution)/shard_map/pallas_call | solution.py:708
  22.1 0.6 %shard_map.99 = (f32[16,8,512]{2,1,0:T(8,128)S(1)}, f32[16,8,512]{2,1,0:T(8,128)S(1)}, f32[8,512]{1,0:T(8,128)S(1)}) custom-call(f32[16,8,512]{2,1,0:T(8,128)S(1)} %copy-done, f32[16,8,512]{2,1,0:T(8,128)S(1)} %copy-done.1, s32[8,512]{1,0:T(8,128)S(1)} %copy-done.3, f32[8,512]{1,0:T(8,128)S(1)} %copy-done.4, f32[80,512]{1,0:T(8,128)S(1)} %collective-permute-done.sibling, ...), custom_call_target="tpu_custom_call" | custom-call | flops 2621440 | bytes 1409024 | tf_op jit(solution)/shard_map/pallas_call | solution.py:708
  22.7 1.2 %all-to-all-done = f32[16,1,128]{2,1,0:T(1,128)S(1)} async-done(((f32[16,1,128]{2,1,0:T(1,128)}), f32[16,1,128]{2,1,0:T(1,128)S(1)}, u32[]{:S(2)}, u32[]{:S(2)}) %all-to-all-start) | async-done | bytes 8224 | tf_op jit(solution)/shard_map/all_to_all | solution.py:771
  23.9 1.5 %shard_map.100 = (f32[16,8,512]{2,1,0:T(8,128)}, f32[16,8,512]{2,1,0:T(8,128)}, f32[8,512]{1,0:T(8,128)}) custom-call(f32[16,128]{1,0:T(8,128)S(1)} %bitcast.4, f32[144,512]{1,0:T(8,128)S(1)} %shard_map.98.parts, f32[16,8,512]{2,1,0:T(8,128)S(1)} %get-tuple-element.36.zonal, f32[16,8,512]{2,1,0:T(8,128)S(1)} %get-tuple-element.37.meridional, ...), custom_call_target="tpu_custom_call" | custom-call | bytes 1384448 | tf_op jit(solution)/shard_map/pallas_call | solution.py:708
Async XLA Ops:
  2.2 6.2 %collective-permute-start = (f32[80,512]{1,0:T(8,128)S(1)}, f32[80,512]{1,0:T(8,128)S(1)}, u32[]{:S(2)}, u32[]{:S(2)}) collective-permute-start(f32[80,512]{1,0:T(8,128)S(1)} %get-tuple-element.23.inner), channel_id=1, source_target_pairs={{0,1},{1,0},{2,3},{3,2},{4,5},{5,4},{6,7},{7,6},{8,9},{9,8},{10,11... | collective-permute-start | bytes 491528 | tf_op jit(solution)/shard_map/ppermute | solution.py:724
  2.8 8.4 %collective-permute-start.1 = (f32[64,512]{1,0:T(8,128)S(1)}, f32[64,512]{1,0:T(8,128)S(1)}, u32[]{:S(2)}, u32[]{:S(2)}) collective-permute-start(f32[64,512]{1,0:T(8,128)S(1)} %get-tuple-element.24.outer), channel_id=1, source_target_pairs={{0,15},{1,2},{2,1},{3,4},{4,3},{5,6},{6,5},{7,8},{8,7},{9,10},{10,... | collective-permute-start | bytes 393224 | tf_op jit(solution)/shard_map/ppermute | solution.py:724
  8.6 5.8 %collective-permute-start.2 = (f32[16,128]{1,0:T(8,128)S(1)}, f32[16,128]{1,0:T(8,128)S(1)}, u32[]{:S(2)}, u32[]{:S(2)}) collective-permute-start(f32[16,128]{1,0:T(8,128)S(1)} %get-tuple-element.25), channel_id=1, source_target_pairs={{0,15},{1,8},{2,13},{3,14},{4,11},{5,12},{6,9},{7,10},{8,7},{9,6},... | collective-permute-start | bytes 24584 | tf_op jit(solution)/shard_map/ppermute | solution.py:724
  9.6 4.8 %collective-permute-start.3 = (f32[16,128]{1,0:T(8,128)S(1)}, f32[16,128]{1,0:T(8,128)S(1)}, u32[]{:S(2)}, u32[]{:S(2)}) collective-permute-start(f32[16,128]{1,0:T(8,128)S(1)} %get-tuple-element.26), channel_id=1, source_target_pairs={{0,13},{1,14},{2,11},{3,12},{4,9},{5,10},{6,7},{7,8},{8,5},{9,0},{... | collective-permute-start | bytes 24584 | tf_op jit(solution)/shard_map/ppermute | solution.py:724
  11.2 9.0 %copy-start.2 = (f32[16,8,512]{2,1,0:T(8,128)S(1)}, f32[16,8,512]{2,1,0:T(8,128)}, u32[]{:S(2)}) copy-start(f32[16,8,512]{2,1,0:T(8,128)} %tracer.1) | copy-start | bytes 786436
  16.0 8.0 %all-to-all-start = ((f32[16,1,128]{2,1,0:T(1,128)}), f32[16,1,128]{2,1,0:T(1,128)S(1)}, u32[]{:S(2)}, u32[]{:S(2)}) async-start(f32[16,1,128]{2,1,0:T(1,128)} %bitcast.1), calls=%async_computation | async-start | bytes 16384 | tf_op jit(solution)/shard_map/all_to_all | solution.py:771
  19.9 0.9 %copy-start = (f32[16,8,512]{2,1,0:T(8,128)S(1)}, f32[16,8,512]{2,1,0:T(8,128)}, u32[]{:S(2)}) copy-start(f32[16,8,512]{2,1,0:T(8,128)} %zonal.3) | copy-start | bytes 786436
  19.9 1.0 %copy-start.1 = (f32[16,8,512]{2,1,0:T(8,128)S(1)}, f32[16,8,512]{2,1,0:T(8,128)}, u32[]{:S(2)}) copy-start(f32[16,8,512]{2,1,0:T(8,128)} %meridional.3) | copy-start | bytes 786436
  19.9 1.0 %copy-start.3 = (s32[8,512]{1,0:T(8,128)S(1)}, s32[8,512]{1,0:T(8,128)}, u32[]{:S(2)}) copy-start(s32[8,512]{1,0:T(8,128)} %count.3) | copy-start | bytes 49156
  20.0 1.0 %copy-start.4 = (f32[8,512]{1,0:T(8,128)S(1)}, f32[8,512]{1,0:T(8,128)}, u32[]{:S(2)}) copy-start(f32[8,512]{1,0:T(8,128)} %diffusivity.3) | copy-start | bytes 49156
